TPU v7x, 32 devices: a whole 2x2x4 slice. The times are simulated.
32 devices in a mesh: src: 4 (over y, x), space: 8 (over z, core).
Axes of the slice: x: 2, y: 2, z: 4, core: 2. Of those that a mesh axis runs over, the one named last changes fastest.
Arguments:
- velocity: float32 [8, 512, 256], P('space'), may hold values from 0.5 to 2
- station_cells: int32 [4, 3], P('src'), may hold values from 0 to 511, as said below
- event_cells: int32 [3, 2048], replicated, may hold values from 0 to 511, as said below
- delays: float32 [4, 2048], P('src'), may hold values from -6 to 6
- active: int32 [2, 4, 8, 16], P(None, 'src', 'space'), may hold values from 0 to 1, as said below
Outputs:
- traveltimes: float32 [4, 8, 512, 256], P('src', 'space')
- kernel: float32 [8, 512, 256], P('space', 'src')
Inputs may be any that keep to these rules, and one draw needn't show every extreme that they name: `station_cells`: stations lie in the top four layers: third coordinate below 4, first below 8, second below 512. `event_cells`: row 0 holds first coordinates below 8, row 1 second ones below 512, row 2 third ones below 256. `active`: 1 marks a tile whose cells are updated in that round for that station.
All inputs are finite; a program needn't handle non-finite values.
Results may differ from a plain program's by a relative error of at most 0.0003.
Values sent between devices are 32-bit elements; how exact they have to be, the bound alone decides.
No kernel may reach another device: no remote copies, remote signals or barrier semaphores. Data moves between devices by JAX's collectives and lax.ppermute only.
A program may use at most 64 MiB of HBM per device.

v0:
```python
import jax
import jax.numpy as jnp
from jax import lax
from jax.sharding import PartitionSpec as P

TY = 32
ROUNDS = 2
SWEEPS = 2
ADJ_SWEEPS = 4


BIG = 1000000.0


def padded(array, sides, width):
    for axis, dim in sides:
        size, length = (lax.axis_size(axis), array.shape[dim])
        up = [(i, (i + 1) % size) for i in range(size - 1)]
        down = [(j, i) for i, j in up]
        last = lax.slice_in_dim(array, length - width, length, axis=dim)
        first = lax.slice_in_dim(array, 0, width, axis=dim)
        before = lax.ppermute(last, axis, up)
        after = lax.ppermute(first, axis, down)
        array = jnp.concatenate([before, array, after], axis=dim)
    return array


def godunov(near_x, near_y, near_z, cost_cell):
    lowest = jnp.minimum(jnp.minimum(near_x, near_y), near_z)
    highest = jnp.maximum(jnp.maximum(near_x, near_y), near_z)
    middle = jnp.maximum(
        jnp.minimum(near_x, near_y), jnp.minimum(jnp.maximum(near_x, near_y), near_z)
    )
    first_gap = middle - lowest
    second_gap = highest - lowest
    single = lowest + cost_cell
    double = lowest + 0.5 * (
        first_gap + jnp.sqrt(jnp.maximum(2.0 * cost_cell * cost_cell - first_gap * first_gap, 0.0))
    )
    gaps = first_gap + second_gap
    triple = (
        lowest
        + (
            gaps
            + jnp.sqrt(
                jnp.maximum(
                    gaps * gaps
                    - 3.0
                    * (first_gap * first_gap + second_gap * second_gap - cost_cell * cost_cell),
                    0.0,
                )
            )
        )
        / 3.0
    )
    return jnp.where(single <= middle, single, jnp.where(double <= highest, double, triple))


def end_slab(field, axis_index, fill):
    return jnp.full_like(lax.slice_in_dim(field, 0, 1, axis=axis_index), fill)


def shifted(field, axis_index, low_rim, high_rim):
    length = field.shape[axis_index]
    before = jnp.concatenate(
        [low_rim, lax.slice_in_dim(field, 0, length - 1, axis=axis_index)], axis=axis_index
    )
    after = jnp.concatenate(
        [lax.slice_in_dim(field, 1, length, axis=axis_index), high_rim], axis=axis_index
    )
    return (before, after)


def six_neighbours(field, low_rim, high_rim, fill):
    x_before, x_after = shifted(field, 1, low_rim, high_rim)
    y_before, y_after = shifted(field, 2, end_slab(field, 2, fill), end_slab(field, 2, fill))
    z_before, z_after = shifted(field, 3, end_slab(field, 3, fill), end_slab(field, 3, fill))
    return [x_before, x_after, y_before, y_after, z_before, z_after]


def outer_rims(extended):
    position = lax.axis_index("space")
    final_index = lax.axis_size("space") - 1
    low_rim = jnp.where(position == 0, BIG, extended[:, :1])
    high_rim = jnp.where(position == final_index, BIG, extended[:, -1:])
    return (low_rim, high_rim)


def sweep_once(times, slowness, tile_mask, station_mask):
    extended = padded(times, (("space", 1),), 1)
    low_rim, high_rim = outer_rims(extended)
    beside_all = six_neighbours(times, low_rim, high_rim, BIG)
    update = godunov(
        jnp.minimum(beside_all[0], beside_all[1]),
        jnp.minimum(beside_all[2], beside_all[3]),
        jnp.minimum(beside_all[4], beside_all[5]),
        slowness[None],
    )
    station_count, rows_x, rows_y, rows_z = times.shape
    tile_count = rows_y // TY
    shape_tiles = (station_count, rows_x, tile_count, TY, rows_z)
    chosen = jnp.where(tile_mask, update.reshape(shape_tiles), times.reshape(shape_tiles)).reshape(
        times.shape
    )
    return jnp.where(station_mask, 0.0, chosen)


def smooth_along(extended, axis_index):
    length = extended.shape[axis_index]
    first = lax.slice_in_dim(extended, 0, length - 2, axis=axis_index)
    centre = lax.slice_in_dim(extended, 1, length - 1, axis=axis_index)
    after = lax.slice_in_dim(extended, 2, length, axis=axis_index)
    return (first + 2.0 * centre + after) * 0.25


def pad_zero(field, axis_index):
    widths = [(0, 0)] * field.ndim
    widths[axis_index] = (1, 1)
    return jnp.pad(field, widths)


def per_device(velocity, station_cells, event_cells, delays, active):
    slowness = 1.0 / velocity
    rows_x, rows_y, rows_z = velocity.shape
    station_count = station_cells.shape[0]
    offset_x = lax.axis_index("space") * rows_x
    grid_x = (lax.broadcasted_iota(jnp.int32, (rows_x, rows_y, rows_z), 0) + offset_x)[None]
    grid_y = lax.broadcasted_iota(jnp.int32, (rows_x, rows_y, rows_z), 1)[None]
    grid_z = lax.broadcasted_iota(jnp.int32, (rows_x, rows_y, rows_z), 2)[None]
    station_x = station_cells[:, 0][:, None, None, None]
    station_y = station_cells[:, 1][:, None, None, None]
    station_z = station_cells[:, 2][:, None, None, None]
    diff_x = (grid_x - station_x).astype(jnp.float32)
    diff_y = (grid_y - station_y).astype(jnp.float32)
    diff_z = (grid_z - station_z).astype(jnp.float32)
    times = jnp.sqrt(diff_x * diff_x + diff_y * diff_y + diff_z * diff_z)
    station_mask = (grid_x == station_x) & (grid_y == station_y) & (grid_z == station_z)
    for round_index in range(ROUNDS):
        tile_mask = (active[round_index][:, 0, :] > 0)[:, None, :, None, None]
        for sweep in range(SWEEPS):
            times = sweep_once(times, slowness, tile_mask, station_mask)
    cell_count = rows_x * rows_y * rows_z
    event_x = event_cells[0]
    event_y = event_cells[1]
    event_z = event_cells[2]
    local_x = event_x - offset_x
    inside = (local_x >= 0) & (local_x < rows_x)
    flat_index = jnp.where(
        inside, local_x * (rows_y * rows_z) + event_y * rows_z + event_z, cell_count
    )
    flat_times = times.reshape(station_count, cell_count)
    picked = jnp.take(flat_times, jnp.minimum(flat_index, cell_count - 1), axis=1)
    event_dx = (event_x[None, :] - station_cells[:, 0:1]).astype(jnp.float32)
    event_dy = (event_y[None, :] - station_cells[:, 1:2]).astype(jnp.float32)
    event_dz = (event_z[None, :] - station_cells[:, 2:3]).astype(jnp.float32)
    direct = jnp.sqrt(event_dx * event_dx + event_dy * event_dy + event_dz * event_dz)
    misfit = jnp.where(inside[None, :], picked - direct - delays, 0.0)
    source = (
        jnp.zeros((station_count, cell_count), jnp.float32)
        .at[:, flat_index]
        .add(misfit, mode="drop")
    )
    source = source.reshape(times.shape)
    final_ext = padded(times, (("space", 1),), 1)
    low_rim, high_rim = outer_rims(final_ext)
    time_around = six_neighbours(times, low_rim, high_rim, BIG)
    weights = [
        jnp.maximum(neighbour - times, 0.0) * velocity[None] / 6.0 for neighbour in time_around
    ]
    adjoint = source
    for sweep in range(ADJ_SWEEPS):
        adjoint_ext = padded(adjoint, (("space", 1),), 1)
        adjoint_around = six_neighbours(adjoint, adjoint_ext[:, :1], adjoint_ext[:, -1:], 0.0)
        summed = source
        for weight, neighbour in zip(weights, adjoint_around):
            summed = summed + weight * neighbour
        adjoint = summed
    density = slowness * jnp.sum(adjoint, axis=0)
    summed_density = lax.psum(density, "src")
    extended = padded(summed_density, (("space", 0),), 1)
    along_x = smooth_along(extended, 0)
    along_y = smooth_along(pad_zero(along_x, 1), 1)
    filtered = smooth_along(pad_zero(along_y, 2), 2)
    row_count = rows_y // lax.axis_size("src")
    kernel = lax.dynamic_slice_in_dim(filtered, lax.axis_index("src") * row_count, row_count, 1)
    return (times, kernel)


def solution(mesh):
    return jax.shard_map(
        per_device,
        mesh=mesh,
        in_specs=(
            P("space", None, None),
            P("src", None),
            P(),
            P("src", None),
            P(None, "src", "space", None),
        ),
        out_specs=(P("src", "space", None, None), P("space", "src", None)),
        check_vma=False,
    )
```

profile of v0, /device:TPU:1, one launch (start us, length us, event | category | flops | bytes accessed | tf_op | source)
XLA Modules:
  0.0 224.5 jit_solution(1707893802803897388)
XLA Ops:
  9.1 1.4 add_sqrt_fusion
  10.6 2.0 collective-permute-start.1
  12.5 4.6 %collective-permute-start = (f32[1,1,512,256]{3,2,1,0:T(8,128)S(1)}, f32[1,1,512,256]{3,2,1,0:T(8,128)}, u32[]{:S(2)}, u32[]{:S(2)}) collective-permute-start(f32[1,1,512,256]{3,2,1,0:T(8,128)S(1)} %add_sqrt_fusion), channel_id=1, source_target_pairs={{0,1},{1,2},{2,3},{3,4},{4,5},{5,6},{6,7},{8,9},{9,10},{10,11},{11... | collective-permute-start | bytes 1572872 | tf_op jit(solution)/shard_map/ppermute | solution.py:22
  19.8 2.3 %collective-permute-done.1 = f32[1,1,512,256]{3,2,1,0:T(8,128)} collective-permute-done((f32[1,1,512,256]{3,2,1,0:T(8,128)S(1)}, f32[1,1,512,256]{3,2,1,0:T(8,128)}, u32[]{:S(2)}, u32[]{:S(2)}) %collective-permute-start.1) | collective-permute-done | bytes 524320 | tf_op jit(solution)/shard_map/ppermute | solution.py:23
  23.2 3.8 %fusion.1 = f32[1,1,512,256]{3,2,1,0:T(8,128)S(1)} fusion(f32[1,1,512,255]{3,2,1,0:T(8,128)S(1)} %get-tuple-element.50, f32[1,1,512,255]{3,2,1,0:T(8,128)S(1)} %get-tuple-element.49, f32[1,1,511,256]{3,2,1,0:T(8,128)S(1)} %get-tuple-element.48, f32[1,1,511,256]{3,2,1,0:T(8,128)S(1)} %get-tuple-element.47, f32[1,1,512,256]{3,2,1,0:T(8,128)} %collective-permute-done.1, ...), kind=kLoop, calls=%fused_computation.14 | loop fusion | flops 6422528 | bytes 4190731 | tf_op jit(solution)/shard_map/jit(_where)/select_n | solution.py:105
  27.0 1.9 collective-permute-start.3
  28.9 4.5 %collective-permute-start.2 = (f32[1,1,512,256]{3,2,1,0:T(8,128)S(1)}, f32[1,1,512,256]{3,2,1,0:T(8,128)S(1)}, u32[]{:S(2)}, u32[]{:S(2)}) collective-permute-start(f32[1,1,512,256]{3,2,1,0:T(8,128)S(1)} %fusion.1), channel_id=1, source_target_pairs={{0,1},{1,2},{2,3},{3,4},{4,5},{5,6},{6,7},{8,9},{9,10},{10,11},{11... | collective-permute-start | bytes 1572872 | tf_op jit(solution)/shard_map/ppermute | solution.py:22
  33.7 4.6 %collective-permute-done.3 = f32[1,1,512,256]{3,2,1,0:T(8,128)S(1)} collective-permute-done((f32[1,1,512,256]{3,2,1,0:T(8,128)S(1)}, f32[1,1,512,256]{3,2,1,0:T(8,128)S(1)}, u32[]{:S(2)}, u32[]{:S(2)}) %collective-permute-start.3) | collective-permute-done | bytes 524320 | tf_op jit(solution)/shard_map/ppermute | solution.py:23
  38.3 1.2 collective-permute-done.2
  39.5 2.4 %fusion.3 = f32[1,1,512,256]{3,2,1,0:T(8,128)S(1)} fusion(f32[1,1,512,256]{3,2,1,0:T(8,128)S(1)} %fusion.1, f32[1,1,512,255]{3,2,1,0:T(8,128)S(1)} %get-tuple-element.46, f32[1,1,512,255]{3,2,1,0:T(8,128)S(1)} %get-tuple-element.45, f32[1,1,511,256]{3,2,1,0:T(8,128)S(1)} %get-tuple-element.44, f32[1,1,511,256]{3,2,1,0:T(8,128)S(1)} %get-tuple-element.43, ...), kind=kLoop, calls=%fused_computation.16 | loop fusion | flops 5898240 | bytes 4712971 | tf_op jit(solution)/shard_map/jit(_where)/select_n | solution.py:105
  41.9 1.9 collective-permute-start.5
  43.9 4.4 %collective-permute-start.4 = (f32[1,1,512,256]{3,2,1,0:T(8,128)S(1)}, f32[1,1,512,256]{3,2,1,0:T(8,128)S(1)}, u32[]{:S(2)}, u32[]{:S(2)}) collective-permute-start(f32[1,1,512,256]{3,2,1,0:T(8,128)S(1)} %fusion.3), channel_id=1, source_target_pairs={{0,1},{1,2},{2,3},{3,4},{4,5},{5,6},{6,7},{8,9},{9,10},{10,11},{11... | collective-permute-start | bytes 1572872 | tf_op jit(solution)/shard_map/ppermute | solution.py:22
  48.5 4.6 %collective-permute-done.5 = f32[1,1,512,256]{3,2,1,0:T(8,128)S(1)} collective-permute-done((f32[1,1,512,256]{3,2,1,0:T(8,128)S(1)}, f32[1,1,512,256]{3,2,1,0:T(8,128)S(1)}, u32[]{:S(2)}, u32[]{:S(2)}) %collective-permute-start.5) | collective-permute-done | bytes 524320 | tf_op jit(solution)/shard_map/ppermute | solution.py:23
  53.2 1.2 collective-permute-done.4
  54.4 2.4 %fusion.5 = f32[1,1,512,256]{3,2,1,0:T(8,128)S(1)} fusion(f32[1,1,512,256]{3,2,1,0:T(8,128)S(1)} %fusion.3, f32[1,1,512,255]{3,2,1,0:T(8,128)S(1)} %get-tuple-element.42, f32[1,1,512,255]{3,2,1,0:T(8,128)S(1)} %get-tuple-element.41, f32[1,1,511,256]{3,2,1,0:T(8,128)S(1)} %get-tuple-element.40, f32[1,1,511,256]{3,2,1,0:T(8,128)S(1)} %get-tuple-element.39, ...), kind=kLoop, calls=%fused_computation.18 | loop fusion | flops 5898240 | bytes 4712971 | tf_op jit(solution)/shard_map/jit(_where)/select_n | solution.py:105
  56.8 1.9 collective-permute-start.7
  58.7 4.4 %collective-permute-start.6 = (f32[1,1,512,256]{3,2,1,0:T(8,128)S(1)}, f32[1,1,512,256]{3,2,1,0:T(8,128)S(1)}, u32[]{:S(2)}, u32[]{:S(2)}) collective-permute-start(f32[1,1,512,256]{3,2,1,0:T(8,128)S(1)} %fusion.5), channel_id=1, source_target_pairs={{0,1},{1,2},{2,3},{3,4},{4,5},{5,6},{6,7},{8,9},{9,10},{10,11},{11... | collective-permute-start | bytes 1572872 | tf_op jit(solution)/shard_map/ppermute | solution.py:22
  63.4 4.6 %collective-permute-done.7 = f32[1,1,512,256]{3,2,1,0:T(8,128)S(1)} collective-permute-done((f32[1,1,512,256]{3,2,1,0:T(8,128)S(1)}, f32[1,1,512,256]{3,2,1,0:T(8,128)S(1)}, u32[]{:S(2)}, u32[]{:S(2)}) %collective-permute-start.7) | collective-permute-done | bytes 524320 | tf_op jit(solution)/shard_map/ppermute | solution.py:23
  68.0 1.2 collective-permute-done.6
  69.2 2.4 %fusion.7 = f32[1,1,512,256]{3,2,1,0:T(8,128)S(1)} fusion(f32[1,1,512,256]{3,2,1,0:T(8,128)S(1)} %fusion.5, f32[1,1,512,255]{3,2,1,0:T(8,128)S(1)} %get-tuple-element.38, f32[1,1,512,255]{3,2,1,0:T(8,128)S(1)} %get-tuple-element.37, f32[1,1,511,256]{3,2,1,0:T(8,128)S(1)} %get-tuple-element.36, f32[1,1,511,256]{3,2,1,0:T(8,128)S(1)} %get-tuple-element.35, ...), kind=kLoop, calls=%fused_computation.20 | loop fusion | flops 5898240 | bytes 4712971 | tf_op jit(solution)/shard_map/jit(_where)/select_n | solution.py:105
  72.0 11.8 %gather_fusion = f32[2048]{0:T(1024)S(1)} fusion(f32[131072]{0:T(1024)S(1)} %bitcast.79, s32[2048]{0:T(1024)S(1)} %broadcast_clamp_fusion), kind=kCustom, calls=%fused_computation | custom fusion | bytes 24576 | tf_op jit(solution)/shard_map/jit(_take)/gather | solution.py:152
  83.8 1.9 subtract_select_fusion
  85.7 11.4 %scatter_custom_fusion = f32[131072]{0:T(1024)S(1)} fusion(s32[2048]{0:T(1024)S(1)} %bitcast.83, f32[2048]{0:T(1024)S(1)} %bitcast.84, f32[]{:T(128)} %constant.24.clone.1), kind=kCustom, calls=%fused_computation.66 | custom fusion | flops 2048 | bytes 524292 | tf_op jit(solution)/shard_map/scatter-add | solution.py:161
  97.2 1.9 collective-permute-start.11
  99.2 4.4 %collective-permute-start.9 = (f32[1,1,512,256]{3,2,1,0:T(8,128)S(1)}, f32[1,1,512,256]{3,2,1,0:T(8,128)S(1)}, u32[]{:S(2)}, u32[]{:S(2)}) collective-permute-start(f32[1,1,512,256]{3,2,1,0:T(8,128)S(1)} %reshape.397), channel_id=1, source_target_pairs={{0,1},{1,2},{2,3},{3,4},{4,5},{5,6},{6,7},{8,9},{9,10},{10,11},{11... | collective-permute-start | bytes 1572872 | tf_op jit(solution)/shard_map/ppermute | solution.py:22
  103.6 1.9 collective-permute-start.10
  105.5 3.6 %collective-permute-start.8 = (f32[1,1,512,256]{3,2,1,0:T(8,128)S(1)}, f32[1,1,512,256]{3,2,1,0:T(8,128)S(1)}, u32[]{:S(2)}, u32[]{:S(2)}) collective-permute-start(f32[1,1,512,256]{3,2,1,0:T(8,128)S(1)} %fusion.7), channel_id=1, source_target_pairs={{0,1},{1,2},{2,3},{3,4},{4,5},{5,6},{6,7},{8,9},{9,10},{10,11},{11... | collective-permute-start | bytes 1572872 | tf_op jit(solution)/shard_map/ppermute | solution.py:22
  109.7 4.4 %collective-permute-done.10 = f32[1,1,512,256]{3,2,1,0:T(8,128)S(1)} collective-permute-done((f32[1,1,512,256]{3,2,1,0:T(8,128)S(1)}, f32[1,1,512,256]{3,2,1,0:T(8,128)S(1)}, u32[]{:S(2)}, u32[]{:S(2)}) %collective-permute-start.10) | collective-permute-done | bytes 524320 | tf_op jit(solution)/shard_map/ppermute | solution.py:23
  114.1 1.2 collective-permute-done.8
  116.2 1.9 collective-permute-start.13
  118.1 4.6 %collective-permute-start.12 = (f32[1,1,512,256]{3,2,1,0:T(8,128)S(1)}, f32[1,1,512,256]{3,2,1,0:T(8,128)S(1)}, u32[]{:S(2)}, u32[]{:S(2)}) collective-permute-start(f32[1,1,512,256]{3,2,1,0:T(8,128)S(1)} %get-tuple-element.4), channel_id=1, source_target_pairs={{0,1},{1,2},{2,3},{3,4},{4,5},{5,6},{6,7},{8,9},{9,10},{10,11},{11... | collective-permute-start | bytes 1572872 | tf_op jit(solution)/shard_map/ppermute | solution.py:22
  123.0 4.5 %collective-permute-done.13 = f32[1,1,512,256]{3,2,1,0:T(8,128)S(1)} collective-permute-done((f32[1,1,512,256]{3,2,1,0:T(8,128)S(1)}, f32[1,1,512,256]{3,2,1,0:T(8,128)S(1)}, u32[]{:S(2)}, u32[]{:S(2)}) %collective-permute-start.13) | collective-permute-done | bytes 524320 | tf_op jit(solution)/shard_map/ppermute | solution.py:23
  127.4 1.2 collective-permute-done.12
  129.1 1.9 collective-permute-start.15
  131.0 4.4 %collective-permute-start.14 = (f32[1,1,512,256]{3,2,1,0:T(8,128)S(1)}, f32[1,1,512,256]{3,2,1,0:T(8,128)S(1)}, u32[]{:S(2)}, u32[]{:S(2)}) collective-permute-start(f32[1,1,512,256]{3,2,1,0:T(8,128)S(1)} %multiply_add_fusion.1), channel_id=1, source_target_pairs={{0,1},{1,2},{2,3},{3,4},{4,5},{5,6},{6,7},{8,9},{9,10},{10,11},{11... | collective-permute-start | bytes 1572872 | tf_op jit(solution)/shard_map/ppermute | solution.py:22
  135.7 4.6 %collective-permute-done.15 = f32[1,1,512,256]{3,2,1,0:T(8,128)S(1)} collective-permute-done((f32[1,1,512,256]{3,2,1,0:T(8,128)S(1)}, f32[1,1,512,256]{3,2,1,0:T(8,128)S(1)}, u32[]{:S(2)}, u32[]{:S(2)}) %collective-permute-start.15) | collective-permute-done | bytes 524320 | tf_op jit(solution)/shard_map/ppermute | solution.py:23
  140.3 1.2 collective-permute-done.14
  142.0 1.9 collective-permute-start.17
  143.9 4.4 %collective-permute-start.16 = (f32[1,1,512,256]{3,2,1,0:T(8,128)S(1)}, f32[1,1,512,256]{3,2,1,0:T(8,128)S(1)}, u32[]{:S(2)}, u32[]{:S(2)}) collective-permute-start(f32[1,1,512,256]{3,2,1,0:T(8,128)S(1)} %multiply_add_fusion), channel_id=1, source_target_pairs={{0,1},{1,2},{2,3},{3,4},{4,5},{5,6},{6,7},{8,9},{9,10},{10,11},{11... | collective-permute-start | bytes 1572872 | tf_op jit(solution)/shard_map/ppermute | solution.py:22
  148.6 4.6 %collective-permute-done.17 = f32[1,1,512,256]{3,2,1,0:T(8,128)S(1)} collective-permute-done((f32[1,1,512,256]{3,2,1,0:T(8,128)S(1)}, f32[1,1,512,256]{3,2,1,0:T(8,128)S(1)}, u32[]{:S(2)}, u32[]{:S(2)}) %collective-permute-start.17) | collective-permute-done | bytes 524320 | tf_op jit(solution)/shard_map/ppermute | solution.py:23
  153.3 1.2 collective-permute-done.16
  154.4 1.4 bitcast_multiply_fusion
  155.9 47.2 %all-reduce.40.cloned.1.call-done = f32[1,512,256]{2,1,0:T(8,128)} async-done(((f32[1,512,256]{2,1,0:T(8,128)}), f32[1,512,256]{2,1,0:T(8,128)}) %all-reduce.40.cloned.1.call-update) | async-done | bytes 524304 | tf_op jit(solution)/shard_map/psum | solution.py:179
  203.1 2.8 %collective-permute-start.19 = (f32[1,512,256]{2,1,0:T(8,128)}, f32[1,512,256]{2,1,0:T(8,128)S(1)}, u32[]{:S(2)}, u32[]{:S(2)}) collective-permute-start(f32[1,512,256]{2,1,0:T(8,128)} %all-reduce.40.cloned.1.call-done), channel_id=1, source_target_pairs={{1,0},{2,1},{3,2},{4,3},{5,4},{6,5},{7,6},{9,8},{10,9},{11,10},{12... | collective-permute-start | bytes 1572872 | tf_op jit(solution)/shard_map/ppermute | solution.py:23
  205.8 3.0 %collective-permute-start.18 = (f32[1,512,256]{2,1,0:T(8,128)}, f32[1,512,256]{2,1,0:T(8,128)S(1)}, u32[]{:S(2)}, u32[]{:S(2)}) collective-permute-start(f32[1,512,256]{2,1,0:T(8,128)} %all-reduce.40.cloned.1.call-done), channel_id=1, source_target_pairs={{0,1},{1,2},{2,3},{3,4},{4,5},{5,6},{6,7},{8,9},{9,10},{10,11},{11... | collective-permute-start | bytes 1572872 | tf_op jit(solution)/shard_map/ppermute | solution.py:22
  208.9 5.1 %collective-permute-done.19 = f32[1,512,256]{2,1,0:T(8,128)S(1)} collective-permute-done((f32[1,512,256]{2,1,0:T(8,128)}, f32[1,512,256]{2,1,0:T(8,128)S(1)}, u32[]{:S(2)}, u32[]{:S(2)}) %collective-permute-start.19) | collective-permute-done | bytes 524320 | tf_op jit(solution)/shard_map/ppermute | solution.py:23
  214.0 1.3 collective-permute-done.18
  215.3 1.1 broadcast_multiply_fusion.1
  (54 shorter events, 10.2 us)
Async XLA Ops:
  7.2 195.9 %all-reduce.40.cloned.1.call-start = ((), (), s32[]{:S(2)}) async-start(), calls=%async_computation | async-start | bytes 1048576 | tf_op jit(solution)/shard_map/psum | solution.py:179
  7.2 0.7 copy-start.5
  10.6 11.6 %collective-permute-start.1 = (f32[1,1,512,256]{3,2,1,0:T(8,128)S(1)}, f32[1,1,512,256]{3,2,1,0:T(8,128)}, u32[]{:S(2)}, u32[]{:S(2)}) collective-permute-start(f32[1,1,512,256]{3,2,1,0:T(8,128)S(1)} %add_sqrt_fusion), channel_id=1, source_target_pairs={{1,0},{2,1},{3,2},{4,3},{5,4},{6,5},{7,6},{9,8},{10,9},{11,10},{12... | collective-permute-start | bytes 1572872 | tf_op jit(solution)/shard_map/ppermute | solution.py:23
  12.5 10.7 %collective-permute-start = (f32[1,1,512,256]{3,2,1,0:T(8,128)S(1)}, f32[1,1,512,256]{3,2,1,0:T(8,128)}, u32[]{:S(2)}, u32[]{:S(2)}) collective-permute-start(f32[1,1,512,256]{3,2,1,0:T(8,128)S(1)} %add_sqrt_fusion), channel_id=1, source_target_pairs={{0,1},{1,2},{2,3},{3,4},{4,5},{5,6},{6,7},{8,9},{9,10},{10,11},{11... | collective-permute-start | bytes 1572872 | tf_op jit(solution)/shard_map/ppermute | solution.py:22
  17.9 1.2 copy-start.3
  17.9 5.3 %copy-start.1 = (f32[1,512,256]{2,1,0:T(8,128)S(1)}, f32[1,512,256]{2,1,0:T(8,128)}, u32[]{:S(2)}) copy-start(f32[1,512,256]{2,1,0:T(8,128)} %param.5) | copy-start | bytes 1572868
  18.0 0.7 copy-start.6
  27.0 11.4 %collective-permute-start.3 = (f32[1,1,512,256]{3,2,1,0:T(8,128)S(1)}, f32[1,1,512,256]{3,2,1,0:T(8,128)S(1)}, u32[]{:S(2)}, u32[]{:S(2)}) collective-permute-start(f32[1,1,512,256]{3,2,1,0:T(8,128)S(1)} %fusion.1), channel_id=1, source_target_pairs={{1,0},{2,1},{3,2},{4,3},{5,4},{6,5},{7,6},{9,8},{10,9},{11,10},{12... | collective-permute-start | bytes 1572872 | tf_op jit(solution)/shard_map/ppermute | solution.py:23
  28.9 10.6 %collective-permute-start.2 = (f32[1,1,512,256]{3,2,1,0:T(8,128)S(1)}, f32[1,1,512,256]{3,2,1,0:T(8,128)S(1)}, u32[]{:S(2)}, u32[]{:S(2)}) collective-permute-start(f32[1,1,512,256]{3,2,1,0:T(8,128)S(1)} %fusion.1), channel_id=1, source_target_pairs={{0,1},{1,2},{2,3},{3,4},{4,5},{5,6},{6,7},{8,9},{9,10},{10,11},{11... | collective-permute-start | bytes 1572872 | tf_op jit(solution)/shard_map/ppermute | solution.py:22
  41.9 11.2 %collective-permute-start.5 = (f32[1,1,512,256]{3,2,1,0:T(8,128)S(1)}, f32[1,1,512,256]{3,2,1,0:T(8,128)S(1)}, u32[]{:S(2)}, u32[]{:S(2)}) collective-permute-start(f32[1,1,512,256]{3,2,1,0:T(8,128)S(1)} %fusion.3), channel_id=1, source_target_pairs={{1,0},{2,1},{3,2},{4,3},{5,4},{6,5},{7,6},{9,8},{10,9},{11,10},{12... | collective-permute-start | bytes 1572872 | tf_op jit(solution)/shard_map/ppermute | solution.py:23
  43.9 10.5 %collective-permute-start.4 = (f32[1,1,512,256]{3,2,1,0:T(8,128)S(1)}, f32[1,1,512,256]{3,2,1,0:T(8,128)S(1)}, u32[]{:S(2)}, u32[]{:S(2)}) collective-permute-start(f32[1,1,512,256]{3,2,1,0:T(8,128)S(1)} %fusion.3), channel_id=1, source_target_pairs={{0,1},{1,2},{2,3},{3,4},{4,5},{5,6},{6,7},{8,9},{9,10},{10,11},{11... | collective-permute-start | bytes 1572872 | tf_op jit(solution)/shard_map/ppermute | solution.py:22
  56.8 11.2 %collective-permute-start.7 = (f32[1,1,512,256]{3,2,1,0:T(8,128)S(1)}, f32[1,1,512,256]{3,2,1,0:T(8,128)S(1)}, u32[]{:S(2)}, u32[]{:S(2)}) collective-permute-start(f32[1,1,512,256]{3,2,1,0:T(8,128)S(1)} %fusion.5), channel_id=1, source_target_pairs={{1,0},{2,1},{3,2},{4,3},{5,4},{6,5},{7,6},{9,8},{10,9},{11,10},{12... | collective-permute-start | bytes 1572872 | tf_op jit(solution)/shard_map/ppermute | solution.py:23
  58.7 10.5 %collective-permute-start.6 = (f32[1,1,512,256]{3,2,1,0:T(8,128)S(1)}, f32[1,1,512,256]{3,2,1,0:T(8,128)S(1)}, u32[]{:S(2)}, u32[]{:S(2)}) collective-permute-start(f32[1,1,512,256]{3,2,1,0:T(8,128)S(1)} %fusion.5), channel_id=1, source_target_pairs={{0,1},{1,2},{2,3},{3,4},{4,5},{5,6},{6,7},{8,9},{9,10},{10,11},{11... | collective-permute-start | bytes 1572872 | tf_op jit(solution)/shard_map/ppermute | solution.py:22
  71.7 43.6 %copy-start = (f32[1,1,512,256]{3,2,1,0:T(8,128)}, f32[1,1,512,256]{3,2,1,0:T(8,128)S(1)}, u32[]{:S(2)}) copy-start(f32[1,1,512,256]{3,2,1,0:T(8,128)S(1)} %fusion.7) | copy-start | bytes 1572868
  72.0 11.8 %copy-start.4 = (f32[1,2048]{1,0:T(1,128)S(1)}, f32[1,2048]{1,0:T(1,128)}, u32[]{:S(2)}) copy-start(f32[1,2048]{1,0:T(1,128)} %param.8) | copy-start | bytes 24580
  97.2 12.4 %collective-permute-start.11 = (f32[1,1,512,256]{3,2,1,0:T(8,128)S(1)}, f32[1,1,512,256]{3,2,1,0:T(8,128)S(1)}, u32[]{:S(2)}, u32[]{:S(2)}) collective-permute-start(f32[1,1,512,256]{3,2,1,0:T(8,128)S(1)} %reshape.397), channel_id=1, source_target_pairs={{1,0},{2,1},{3,2},{4,3},{5,4},{6,5},{7,6},{9,8},{10,9},{11,10},{12... | collective-permute-start | bytes 1572872 | tf_op jit(solution)/shard_map/ppermute | solution.py:23
  99.2 10.5 %collective-permute-start.9 = (f32[1,1,512,256]{3,2,1,0:T(8,128)S(1)}, f32[1,1,512,256]{3,2,1,0:T(8,128)S(1)}, u32[]{:S(2)}, u32[]{:S(2)}) collective-permute-start(f32[1,1,512,256]{3,2,1,0:T(8,128)S(1)} %reshape.397), channel_id=1, source_target_pairs={{0,1},{1,2},{2,3},{3,4},{4,5},{5,6},{6,7},{8,9},{9,10},{10,11},{11... | collective-permute-start | bytes 1572872 | tf_op jit(solution)/shard_map/ppermute | solution.py:22
  103.6 10.5 %collective-permute-start.10 = (f32[1,1,512,256]{3,2,1,0:T(8,128)S(1)}, f32[1,1,512,256]{3,2,1,0:T(8,128)S(1)}, u32[]{:S(2)}, u32[]{:S(2)}) collective-permute-start(f32[1,1,512,256]{3,2,1,0:T(8,128)S(1)} %fusion.7), channel_id=1, source_target_pairs={{1,0},{2,1},{3,2},{4,3},{5,4},{6,5},{7,6},{9,8},{10,9},{11,10},{12... | collective-permute-start | bytes 1572872 | tf_op jit(solution)/shard_map/ppermute | solution.py:23
  105.5 9.8 %collective-permute-start.8 = (f32[1,1,512,256]{3,2,1,0:T(8,128)S(1)}, f32[1,1,512,256]{3,2,1,0:T(8,128)S(1)}, u32[]{:S(2)}, u32[]{:S(2)}) collective-permute-start(f32[1,1,512,256]{3,2,1,0:T(8,128)S(1)} %fusion.7), channel_id=1, source_target_pairs={{0,1},{1,2},{2,3},{3,4},{4,5},{5,6},{6,7},{8,9},{9,10},{10,11},{11... | collective-permute-start | bytes 1572872 | tf_op jit(solution)/shard_map/ppermute | solution.py:22
  116.2 11.2 %collective-permute-start.13 = (f32[1,1,512,256]{3,2,1,0:T(8,128)S(1)}, f32[1,1,512,256]{3,2,1,0:T(8,128)S(1)}, u32[]{:S(2)}, u32[]{:S(2)}) collective-permute-start(f32[1,1,512,256]{3,2,1,0:T(8,128)S(1)} %get-tuple-element.4), channel_id=1, source_target_pairs={{1,0},{2,1},{3,2},{4,3},{5,4},{6,5},{7,6},{9,8},{10,9},{11,10},{12... | collective-permute-start | bytes 1572872 | tf_op jit(solution)/shard_map/ppermute | solution.py:23
  118.1 10.5 %collective-permute-start.12 = (f32[1,1,512,256]{3,2,1,0:T(8,128)S(1)}, f32[1,1,512,256]{3,2,1,0:T(8,128)S(1)}, u32[]{:S(2)}, u32[]{:S(2)}) collective-permute-start(f32[1,1,512,256]{3,2,1,0:T(8,128)S(1)} %get-tuple-element.4), channel_id=1, source_target_pairs={{0,1},{1,2},{2,3},{3,4},{4,5},{5,6},{6,7},{8,9},{9,10},{10,11},{11... | collective-permute-start | bytes 1572872 | tf_op jit(solution)/shard_map/ppermute | solution.py:22
  129.1 11.2 %collective-permute-start.15 = (f32[1,1,512,256]{3,2,1,0:T(8,128)S(1)}, f32[1,1,512,256]{3,2,1,0:T(8,128)S(1)}, u32[]{:S(2)}, u32[]{:S(2)}) collective-permute-start(f32[1,1,512,256]{3,2,1,0:T(8,128)S(1)} %multiply_add_fusion.1), channel_id=1, source_target_pairs={{1,0},{2,1},{3,2},{4,3},{5,4},{6,5},{7,6},{9,8},{10,9},{11,10},{12... | collective-permute-start | bytes 1572872 | tf_op jit(solution)/shard_map/ppermute | solution.py:23
  131.0 10.5 %collective-permute-start.14 = (f32[1,1,512,256]{3,2,1,0:T(8,128)S(1)}, f32[1,1,512,256]{3,2,1,0:T(8,128)S(1)}, u32[]{:S(2)}, u32[]{:S(2)}) collective-permute-start(f32[1,1,512,256]{3,2,1,0:T(8,128)S(1)} %multiply_add_fusion.1), channel_id=1, source_target_pairs={{0,1},{1,2},{2,3},{3,4},{4,5},{5,6},{6,7},{8,9},{9,10},{10,11},{11... | collective-permute-start | bytes 1572872 | tf_op jit(solution)/shard_map/ppermute | solution.py:22
  142.0 11.2 %collective-permute-start.17 = (f32[1,1,512,256]{3,2,1,0:T(8,128)S(1)}, f32[1,1,512,256]{3,2,1,0:T(8,128)S(1)}, u32[]{:S(2)}, u32[]{:S(2)}) collective-permute-start(f32[1,1,512,256]{3,2,1,0:T(8,128)S(1)} %multiply_add_fusion), channel_id=1, source_target_pairs={{1,0},{2,1},{3,2},{4,3},{5,4},{6,5},{7,6},{9,8},{10,9},{11,10},{12... | collective-permute-start | bytes 1572872 | tf_op jit(solution)/shard_map/ppermute | solution.py:23
  143.9 10.5 %collective-permute-start.16 = (f32[1,1,512,256]{3,2,1,0:T(8,128)S(1)}, f32[1,1,512,256]{3,2,1,0:T(8,128)S(1)}, u32[]{:S(2)}, u32[]{:S(2)}) collective-permute-start(f32[1,1,512,256]{3,2,1,0:T(8,128)S(1)} %multiply_add_fusion), channel_id=1, source_target_pairs={{0,1},{1,2},{2,3},{3,4},{4,5},{5,6},{6,7},{8,9},{9,10},{10,11},{11... | collective-permute-start | bytes 1572872 | tf_op jit(solution)/shard_map/ppermute | solution.py:22
  203.1 10.9 %collective-permute-start.19 = (f32[1,512,256]{2,1,0:T(8,128)}, f32[1,512,256]{2,1,0:T(8,128)S(1)}, u32[]{:S(2)}, u32[]{:S(2)}) collective-permute-start(f32[1,512,256]{2,1,0:T(8,128)} %all-reduce.40.cloned.1.call-done), channel_id=1, source_target_pairs={{1,0},{2,1},{3,2},{4,3},{5,4},{6,5},{7,6},{9,8},{10,9},{11,10},{12... | collective-permute-start | bytes 1572872 | tf_op jit(solution)/shard_map/ppermute | solution.py:23
  205.8 9.4 %collective-permute-start.18 = (f32[1,512,256]{2,1,0:T(8,128)}, f32[1,512,256]{2,1,0:T(8,128)S(1)}, u32[]{:S(2)}, u32[]{:S(2)}) collective-permute-start(f32[1,512,256]{2,1,0:T(8,128)} %all-reduce.40.cloned.1.call-done), channel_id=1, source_target_pairs={{0,1},{1,2},{2,3},{3,4},{4,5},{5,6},{6,7},{8,9},{9,10},{10,11},{11... | collective-permute-start | bytes 1572872 | tf_op jit(solution)/shard_map/ppermute | solution.py:22
  208.9 7.6 %copy-start.2 = (f32[1,512,256]{2,1,0:T(8,128)S(1)}, f32[1,512,256]{2,1,0:T(8,128)}, u32[]{:S(2)}) copy-start(f32[1,512,256]{2,1,0:T(8,128)} %all-reduce.40.cloned.1.call-done) | copy-start | bytes 1572868
Sparse Core Ops, SparseCore 0:
  156.0 47.0 all-reduce.39
where the time goes:
time: 225 us
  waiting for transfers between devices  97.3 us (43%)
  starting transfers between devices  62.3 us (28%)
  other arithmetic  31.7 us (14%)
  local copies, waits for them, and re-layouts  17.5 us (8%)
  between operations  15.6 us (7%)
    psum x1, waiting for transfers between devices, per_device(): summed_density = lax.psum(density, 'src')  47.2 us
    ppermute x10, starting transfers between devices, padded(): before = lax.ppermute(last, axis, up)  42.2 us
    ppermute x10, waiting for transfers between devices, padded(): after = lax.ppermute(first, axis, down)  39.5 us
    ppermute x10, starting transfers between devices, padded(): after = lax.ppermute(first, axis, down)  20.1 us
    gather x1, local copies, waits for them, and re-layouts, per_device(): jnp.take(flat_times, jnp.minimum(flat_index, cell_count - 1), axis=1)  11.8 us
    scatter-add x1, other arithmetic, per_device(): source = jnp.zeros((station_count, cell_count), jnp.float32).at[:, flat_i...  11.4 us
    select_n x4, other arithmetic, sweep_once(): return jnp.where(station_mask, 0.0, chosen)  11 us
    ppermute x10, waiting for transfers between devices, padded(): before = lax.ppermute(last, axis, up)  10.6 us
  transfers between devices with their start and end apart: 21, of which 19 were waited for; matrix products, arithmetic and copies ran while one was open for 2% of the time, Pallas kernels for 0%

commit v1 on v0

v1 whole, which is shorter than its diff:
```python
import functools
import math

import jax
import jax.numpy as jnp
from jax import lax
from jax.experimental import pallas as pl
from jax.experimental.pallas import tpu as pltpu
from jax.sharding import PartitionSpec as P

TY = 32
ROUNDS = 2
SWEEPS = 2
ADJ_SWEEPS = 4
BIG = 1000000.0

HALO = ROUNDS * SWEEPS + ADJ_SWEEPS
ADJ_HALO = ADJ_SWEEPS + 1

VMEM = pltpu.VMEM
SMEM = pltpu.SMEM


def params(mib):
    return pltpu.CompilerParams(vmem_limit_bytes=mib * 1024 * 1024)


def spec(space):
    return pl.BlockSpec(memory_space=space)


def pack_kernel(rows, own_rows, scal, own, other, *outs):
    line_row, chip, core = scal[0], scal[1], scal[2]
    total = own.shape[0]
    chunk = math.gcd(own_rows, 8)
    for j, out in enumerate(outs):
        first = line_row + ((chip ^ j) * 2 + core) * own_rows - HALO
        for piece in range(rows // chunk):
            start = jnp.clip(first + piece * chunk, 0, total - chunk)
            start = pl.multiple_of(start, chunk)
            mine = own[pl.ds(start, chunk), :]
            theirs = other[pl.ds(start, chunk), :]
            out[0, piece * chunk : (piece + 1) * chunk, :] = jnp.where(core == 0, mine, theirs)
            out[1, piece * chunk : (piece + 1) * chunk, :] = jnp.where(core == 0, theirs, mine)


def scatter_kernel(layers, events, scal, cells, *refs):
    slots = len(refs) - 2
    pays, count, delay_sum = refs[:slots], refs[slots], refs[slots + 1]
    first_row = scal[3] + HALO - ADJ_HALO
    height, width = count.shape
    chunk = min(events, 512)
    cells_iota = lax.broadcasted_iota(jnp.int32, (height, chunk), 0)
    depth_iota = lax.broadcasted_iota(jnp.int32, (width, chunk), 0)
    contract = (((1,), (1,)), ((), ()))

    def step(index, carry):
        start = pl.multiple_of(index * chunk, chunk)
        where_x = cells[0:1, pl.ds(start, chunk)]
        where_y = cells[1:2, pl.ds(start, chunk)] - first_row
        where_z = cells[2:3, pl.ds(start, chunk)]
        at = jnp.where(where_y >= 0, where_y * layers + where_x, -1)
        hit = (cells_iota == at).astype(jnp.bfloat16)
        depth = (depth_iota == where_z).astype(jnp.bfloat16)

        def add(ref_index, value):
            if ref_index is None:
                count[...] += value
            else:
                delay_sum[ref_index] += value

        def dot(left):
            return lax.dot_general(left, depth, contract, preferred_element_type=jnp.float32)

        add(None, dot(hit))
        for slot in range(slots):
            delay = pays[slot][:, pl.ds(start, chunk)]
            high = delay.astype(jnp.bfloat16)
            low = (delay - high.astype(jnp.float32)).astype(jnp.bfloat16)
            add(slot, dot(hit * high) + dot(hit * low))
        return carry

    count[...] = jnp.zeros_like(count)
    delay_sum[...] = jnp.zeros_like(delay_sum)
    lax.fori_loop(0, events // chunk, step, 0)


def local_solve(near_x, near_y, near_z, cost, twice, one_half):
    small = jnp.minimum(near_x, near_y)
    large = jnp.maximum(near_x, near_y)
    lowest = jnp.minimum(small, near_z)
    highest = jnp.maximum(large, near_z)
    middle = jnp.maximum(small, jnp.minimum(large, near_z))
    first_gap = middle - lowest
    second_gap = highest - lowest
    single = lowest + cost
    double = lowest + 0.5 * (
        first_gap + jnp.sqrt(jnp.maximum(twice - first_gap * first_gap, 0.0))
    )
    rest = first_gap * first_gap + second_gap * (second_gap - first_gap)
    root = jnp.sqrt(jnp.maximum(one_half - rest, 0.0))
    triple = lowest + ((first_gap + second_gap) * (1.0 / 3.0) + root * (math.sqrt(2.0) / 3.0))
    return jnp.where(single <= middle, single, jnp.where(double <= highest, double, triple))


def solve_kernel(layers, own_rows, slots, chips, scal, *refs):
    rows = own_rows + 2 * HALO
    depth = refs[0].shape[-1]
    vel_in, refs = refs[:chips], refs[chips:]
    act_in, refs = refs[:chips], refs[chips:]
    count, delay_sum, refs = refs[0], refs[1], refs[2:]
    times_out, kernel_out, refs = refs[0], refs[1], refs[2:]
    speed, cost, twice, one_half, start, ping, pong, acts, mask, weight, src, adj_a, adj_b, total, flat = refs
    line, chip, y_first = scal[4], scal[1], scal[3]
    grid_rows = scal[5]
    block = math.gcd(own_rows, 2)

    shape3 = (block, layers, depth)
    layer_iota = lax.broadcasted_iota(jnp.int32, shape3, 1)
    depth_iota = lax.broadcasted_iota(jnp.int32, shape3, 2)
    layer_low, layer_high = layer_iota == 0, layer_iota == layers - 1
    depth_low, depth_high = depth_iota == 0, depth_iota == depth - 1

    def before(value, axis):
        return pltpu.roll(value, 1, axis)

    def after(value, axis):
        return pltpu.roll(value, value.shape[axis] - 1, axis)

    def loop(low, high, body, unroll=2):
        steps = (high - low) // block
        lax.fori_loop(
            0, steps, lambda i, carry: (body(low + i * block), carry)[1], 0, unroll=min(unroll, steps)
        )

    parts = depth // 128

    def scatter_layer(place, count_rows, value):
        for part in range(parts):
            flat.at[part][pl.ds(place, count_rows, stride=layers), :] = value[
                :, part * 128 : (part + 1) * 128
            ]

    def gather_layer(place, count_rows):
        return jnp.concatenate(
            [flat.at[part][pl.ds(place, count_rows, stride=layers), :] for part in range(parts)],
            axis=1,
        )

    def flat_span(row):
        return pl.ds(pl.multiple_of(row * layers, layers), block * layers)

    def take_rows(row):
        pieces = [flat[part, flat_span(row), :] for part in range(parts)]
        return jnp.concatenate(pieces, axis=1).reshape(shape3)

    def put_rows(row, value):
        value = value.reshape(block * layers, depth)
        for part in range(parts):
            flat[part, flat_span(row), :] = value[:, part * 128 : (part + 1) * 128]

    for place in range(layers):
        value = vel_in[0][place % 2]
        for j in range(1, chips):
            value = jnp.where((place // 2) ^ chip == j, vel_in[j][place % 2], value)
        scatter_layer(place, rows, value)
        row = act_in[0][place % 2 : place % 2 + 1, :]
        for j in range(1, chips):
            row = jnp.where(
                (place // 2) ^ chip == j, act_in[j][place % 2 : place % 2 + 1, :], row
            )
        acts[place : place + 1, :] = row

    def prepare(row):
        value = take_rows(row)
        slow = 1.0 / value
        square = slow * slow
        here = pl.ds(row, block)
        speed[here] = value * (1.0 / 6.0)
        cost[here] = slow
        twice[here] = 2.0 * square
        one_half[here] = 1.5 * square

    loop(0, rows, prepare)

    lanes = acts.shape[1]
    tiles = lanes // (slots * ROUNDS)
    lane_iota = lax.broadcasted_iota(jnp.int32, (layers, lanes), 1)
    tile_first = (y_first + TY) // TY - 1
    tile_span = (rows + TY - 2) // TY + 1

    for slot in range(slots):
        at_x, at_y, at_z = scal[6 + 3 * slot], scal[7 + 3 * slot], scal[8 + 3 * slot]
        flat_x = (layer_iota - at_x)[0:1].astype(jnp.float32)
        flat_z = (depth_iota - at_z)[0:1].astype(jnp.float32)
        across = flat_x * flat_x + flat_z * flat_z
        at_station = ((layer_iota == at_x) & (depth_iota == at_z))[0:1]

        def fill(i, carry):
            y = y_first - 1 + i
            gap = (y - at_y).astype(jnp.float32)
            far = jnp.where((y >= 0) & (y < grid_rows), gap * gap, BIG * BIG)
            start[pl.ds(i, 1)] = jnp.where(
                far < BIG * BIG, jnp.sqrt(across + far), BIG
            )
            return carry

        lax.fori_loop(0, rows + 2, fill, 0, unroll=2)

        for part in range(ROUNDS):
            columns = []
            for t in range(tile_span):
                tile = tile_first + t
                column = (slot * ROUNDS + part) * tiles + tile
                column = jnp.where((tile >= 0) & (tile < tiles), column, -1)
                picked = jnp.sum(jnp.where(lane_iota == column, acts[...], 0.0), axis=1, keepdims=True)
                columns.append(jnp.broadcast_to(picked, (layers, 128)))
            for i in range(rows):
                value = columns[0]
                for t in range(1, tile_span):
                    value = jnp.where(y_first + i >= (tile_first + t) * TY, columns[t], value)
                mask[part, i] = value

        def sweep(source, target, low, high, part):
            def body(row):
                field = source[pl.ds(row, block + 2)]
                here = field[1 : block + 1]
                near_y = jnp.minimum(field[:block], field[2:])
                near_x = jnp.minimum(
                    jnp.where(layer_low, BIG, before(here, 1)), jnp.where(layer_high, BIG, after(here, 1))
                )
                near_z = jnp.minimum(
                    jnp.where(depth_low, BIG, before(here, 2)), jnp.where(depth_high, BIG, after(here, 2))
                )
                span = pl.ds(row, block)
                update = local_solve(near_x, near_y, near_z, cost[span], twice[span], one_half[span])
                on = mask[part, span]
                on = jnp.concatenate([on] * (depth // 128), axis=2)
                target[pl.ds(row + 1, block)] = jnp.where(on > 0.0, update, here)

            loop(low, high, body)
            local = at_y - y_first

            @pl.when((local >= low) & (local < high))
            def _():
                line_here = pl.ds(local + 1, 1)
                target[line_here] = jnp.where(at_station, 0.0, target[line_here])

        fields = [start, ping, pong, ping, pong]
        for index in range(ROUNDS * SWEEPS):
            sweep(fields[index], fields[index + 1], index, rows - index, index // SWEEPS)
        final = fields[ROUNDS * SWEEPS]

        to_line = line ^ slot

        def flatten(row):
            put_rows(row, final[pl.ds(row + HALO + 1, block)])

        loop(0, own_rows, flatten)
        for place in range(layers):
            times_out[to_line, place] = gather_layer(place, own_rows)

        shift = HALO - ADJ_HALO
        adj_rows = own_rows + 2 * ADJ_HALO

        def make_source(row):
            span = pl.ds(pl.multiple_of(row * layers, layers), block * layers)
            moved = final[pl.ds(row + shift + 1, block)] - start[pl.ds(row + shift + 1, block)]
            src[pl.ds(row, block)] = count[span, :].reshape(shape3) * moved - delay_sum[
                slot, span, :
            ].reshape(shape3)

        loop(0, adj_rows, make_source)

        def make_weight(row):
            field = final[pl.ds(row + shift, block + 2)]
            here = field[1 : block + 1]
            scale = speed[pl.ds(row + shift, block)]
            span = pl.ds(row, block)

            def rise(value):
                return jnp.maximum(value - here, 0.0) * scale

            weight[0, span] = jnp.where(layer_low, 0.0, rise(before(here, 1)))
            weight[1, span] = jnp.where(layer_high, 0.0, rise(after(here, 1)))
            weight[2, span] = rise(field[:block])
            weight[3, span] = rise(field[2:])
            weight[4, span] = jnp.where(depth_low, 0.0, rise(before(here, 2)))
            weight[5, span] = jnp.where(depth_high, 0.0, rise(after(here, 2)))

        loop(1, adj_rows - 1, make_weight)

        def adjoint_sweep(source, target, low, high, last):
            def body(row):
                field = source[pl.ds(row - 1, block + 2)]
                here = field[1 : block + 1]
                span = pl.ds(row, block)
                value = src[span]
                value = value + weight[0, span] * before(here, 1)
                value = value + weight[1, span] * after(here, 1)
                value = value + weight[2, span] * field[:block]
                value = value + weight[3, span] * field[2:]
                value = value + weight[4, span] * before(here, 2)
                value = value + weight[5, span] * after(here, 2)
                if last and slot > 0:
                    value = value + target[span]
                target[span] = value

            loop(low, high, body)

        fields = [src, adj_a, adj_b, adj_a, total]
        for index in range(ADJ_SWEEPS):
            adjoint_sweep(
                fields[index],
                fields[index + 1],
                index + 1,
                adj_rows - 1 - index,
                index == ADJ_SWEEPS - 1,
            )

    def smooth(low, here, high):
        return (low + 2.0 * here + high) * 0.25

    def density(row):
        span = pl.ds(row, block)
        value = total[span] * cost[pl.ds(row + HALO - ADJ_HALO, block)]
        low = jnp.where(layer_low, 0.0, before(value, 1))
        high = jnp.where(layer_high, 0.0, after(value, 1))
        adj_a[span] = smooth(low, value, high)

    loop(ADJ_SWEEPS, ADJ_SWEEPS + own_rows + 2, density)

    def finish(row):
        field = adj_a[pl.ds(row + ADJ_SWEEPS, block + 2)]
        value = smooth(field[:block], field[1 : block + 1], field[2:])
        low = jnp.where(depth_low, 0.0, before(value, 2))
        high = jnp.where(depth_high, 0.0, after(value, 2))
        value = smooth(low, value, high)
        put_rows(row, value)

    loop(0, own_rows, finish)
    for place in range(layers):
        kernel_out[place] = gather_layer(place, own_rows)


def per_device(velocity, station_cells, event_cells, delays, active):
    _, grid_rows, depth = velocity.shape
    slots, layers = lax.axis_size("src"), lax.axis_size("space")
    chips = layers // 2
    events = event_cells.shape[1]
    tiles = active.shape[-1]
    line_rows = grid_rows // slots
    own_rows = line_rows // layers
    rows = own_rows + 2 * HALO
    adj_rows = own_rows + 2 * ADJ_HALO
    line, place = lax.axis_index("src"), lax.axis_index("space")
    chip, core = place // 2, place % 2

    def to_line(array, j):
        return lax.ppermute(array, "src", [(i, i ^ j) for i in range(slots)])

    def to_chip(array, j):
        return lax.ppermute(array, "space", [(i, i ^ (2 * j)) for i in range(layers)])

    def to_core(array):
        return lax.ppermute(array, "space", [(i, i ^ 1) for i in range(layers)])

    f32 = jnp.float32
    pad = -(-(3 + ROUNDS * tiles) // 128) * 128
    tail = jnp.concatenate(
        [station_cells.reshape(1, 3), active.reshape(1, ROUNDS * tiles)], axis=1
    ).astype(f32)
    tail = jnp.pad(tail, ((0, 0), (0, pad - tail.shape[1])))
    payload = jnp.concatenate([delays, tail], axis=1)
    pays = [payload] + [to_line(payload, j) for j in range(1, slots)]

    other = to_core(velocity[0])
    y_first = line * line_rows + place * own_rows - HALO
    here = jnp.stack([line * line_rows, chip, core, y_first, line, jnp.int32(grid_rows)]).astype(jnp.int32)
    block = jax.ShapeDtypeStruct((2, rows, depth), f32)
    packed = pl.pallas_call(
        functools.partial(pack_kernel, rows, own_rows),
        out_shape=[block] * chips,
        in_specs=[spec(SMEM), spec(VMEM), spec(VMEM)],
        out_specs=[spec(VMEM)] * chips,
        compiler_params=params(32),
        name="pack",
    )(here, velocity[0], other)
    vel = [packed[0]] + [to_chip(packed[j], j) for j in range(1, chips)]

    tails = [p[:, events:] for p in pays]
    act = jnp.concatenate([t[:, 3 : 3 + ROUNDS * tiles] for t in tails], axis=1)
    act_other = to_core(act)
    act_pair = jnp.where(
        core == 0, jnp.concatenate([act, act_other]), jnp.concatenate([act_other, act])
    )
    acts = [act_pair] + [to_chip(act_pair, j) for j in range(1, chips)]

    stations = jnp.concatenate([t[0, :3] for t in tails]).astype(jnp.int32)
    scal = jnp.concatenate([here, stations])

    count, delay_sum = pl.pallas_call(
        functools.partial(scatter_kernel, layers, events),
        out_shape=[
            jax.ShapeDtypeStruct((adj_rows * layers, depth), f32),
            jax.ShapeDtypeStruct((slots, adj_rows * layers, depth), f32),
        ],
        in_specs=[spec(SMEM), spec(VMEM)] + [spec(VMEM)] * slots,
        out_specs=[spec(VMEM)] * 2,
        compiler_params=params(32),
        cost_estimate=pl.CostEstimate(flops=2 * 10**9, bytes_accessed=2 * 10**6, transcendentals=0),
        name="events",
    )(here, event_cells, *pays)

    def field(*lead):
        return pltpu.VMEM((*lead, layers, depth), f32)

    times, kernel = pl.pallas_call(
        functools.partial(solve_kernel, layers, own_rows, slots, chips),
        out_shape=[
            jax.ShapeDtypeStruct((slots, layers, own_rows, depth), f32),
            jax.ShapeDtypeStruct((layers, own_rows, depth), f32),
        ],
        in_specs=[spec(SMEM)] + [spec(VMEM)] * (2 * chips + 2),
        out_specs=[spec(VMEM)] * 2,
        scratch_shapes=[
            field(rows),
            field(rows),
            field(rows),
            field(rows),
            field(rows + 2),
            field(rows + 2),
            field(rows + 2),
            pltpu.VMEM((layers, act.shape[1]), f32),
            pltpu.VMEM((ROUNDS, rows, layers, 128), f32),
            field(6, adj_rows),
            field(adj_rows),
            field(adj_rows),
            field(adj_rows),
            field(adj_rows),
            pltpu.VMEM((depth // 128, rows * layers, 128), f32),
        ],
        compiler_params=params(60),
        name="solve",
    )(scal, *vel, *acts, count, delay_sum)

    out = lax.all_to_all(
        times.reshape(slots * layers, own_rows, depth), ("src", "space"), 0, 0, tiled=True
    )
    kernel = lax.all_to_all(kernel, "space", 0, 0, tiled=True)
    return (out.reshape(1, 1, grid_rows, depth), kernel.reshape(1, line_rows, depth))


def solution(mesh):
    return jax.shard_map(
        per_device,
        mesh=mesh,
        in_specs=(
            P("space", None, None),
            P("src", None),
            P(),
            P("src", None),
            P(None, "src", "space", None),
        ),
        out_specs=(P("src", "space", None, None), P("space", "src", None)),
        check_vma=False,
    )
```

time: 225 us -> 96.2 us (0.43)
  waiting for transfers between devices: 97.3 us -> 21.6 us
  starting transfers between devices: 62.3 us -> 17.7 us
  Pallas kernels: 0 us -> 35.5 us
  other arithmetic: 31.7 us -> 2.32 us
  between operations: 15.6 us -> 0.76 us
  local copies, waits for them, and re-layouts: 17.5 us -> 5.61 us
  blocking collectives: 0 us -> 11.8 us
    ppermute x20 -> x11, starting transfers between devices: 62.3 us -> 14.3 us  [the longest x6 7.25 us: to_chip(): return lax.ppermute(array, 'space', [(i, i ^ 2 * j) for i in range(layers)])]
    psum x1 -> x0, waiting for transfers between devices: 47.2 us -> none  [per_device(): summed_density = lax.psum(density, 'src')]
    ppermute x20 -> x11, waiting for transfers between devices: 50.1 us -> 5.48 us  [the longest x6 3.83 us: to_chip(): return lax.ppermute(array, 'space', [(i, i ^ 2 * j) for i in range(layers)])]
    pallas_call x0 -> x3, Pallas kernels: none -> 35.5 us  [the longest x1 30.5 us: per_device(): pl.pallas_call(functools.partial(solve_kernel, layers, own_rows, slots, c...]
    all_to_all x0 -> x1, waiting for transfers between devices: none -> 16.1 us  [per_device(): lax.all_to_all(times.reshape(slots * layers, own_rows, depth), ('src', 's...]
    select_n x7 -> x1, other arithmetic: 13 us -> 0.08 us  [per_device(): jnp.where(core == 0, jnp.concatenate([act, act_other]), jnp.concatenate([...]
    all_to_all x0 -> x1, blocking collectives: none -> 11.8 us  [per_device(): kernel = lax.all_to_all(kernel, 'space', 0, 0, tiled=True)]
    gather x1 -> x0, local copies, waits for them, and re-layouts: 11.8 us -> none  [per_device(): jnp.take(flat_times, jnp.minimum(flat_index, cell_count - 1), axis=1)]
  transfers between devices with their start and end apart: 21 -> 12, of which waited for: 19 -> 6; matrix products, arithmetic and copies ran while one was open for 2% -> 1% of each run, Pallas kernels for 0% -> 5%
where the time goes in v1:
time: 96.2 us; the launch traced here: 95.3 us
  Pallas kernels  35.5 us (37%)
  waiting for transfers between devices  21.6 us (22%)
  starting transfers between devices  17.7 us (18%)
  blocking collectives  11.8 us (12%)
  local copies, waits for them, and re-layouts  5.61 us (6%)
  other arithmetic  2.32 us (2%)
    pallas_call x1, Pallas kernels, per_device(): pl.pallas_call(functools.partial(solve_kernel, layers, own_rows, slots, c...  30.5 us
    all_to_all x1, waiting for transfers between devices, per_device(): lax.all_to_all(times.reshape(slots * layers, own_rows, depth), ('src', 's...  16.1 us
    all_to_all x1, blocking collectives, per_device(): kernel = lax.all_to_all(kernel, 'space', 0, 0, tiled=True)  11.8 us
    ppermute x6, starting transfers between devices, to_chip(): return lax.ppermute(array, 'space', [(i, i ^ 2 * j) for i in range(layers)])  7.25 us
    unnamed x29, local copies, waits for them, and re-layouts  4.55 us
    pallas_call x1, Pallas kernels, per_device(): pl.pallas_call(functools.partial(scatter_kernel, layers, events), out_sha...  4.41 us
    ppermute x6, waiting for transfers between devices, to_chip(): return lax.ppermute(array, 'space', [(i, i ^ 2 * j) for i in range(layers)])  3.83 us
    ppermute x2, starting transfers between devices, to_core(): return lax.ppermute(array, 'space', [(i, i ^ 1) for i in range(layers)])  3.62 us
  transfers between devices with their start and end apart: 12, of which 6 were waited for; matrix products, arithmetic and copies ran while one was open for 1% of the time, Pallas kernels for 5%

profile of v1, /device:TPU:1, one launch (start us, length us, event | category | flops | bytes accessed | tf_op | source)
XLA Modules:
  0.0 95.3 jit_solution(8279713286308886994)
XLA Ops:
  0.6 0.5 broadcast.11
  1.2 1.3 %reduce.3 = s32[2,16]{1,0:T(2,128)S(1)} reduce(s32[2,1,1,16]{3,2,1,0:T(1,128)} %param.9, s32[]{:T(128)} %broadcast.11), dimensions={1,2}, to_apply=%param.9.reduce_sub_computation.3 | reduce | bytes 260 | tf_op args[4]
  2.5 0.1 concatenate.32
  2.6 0.7 add_convert_fusion
  3.3 3.1 %collective-permute-start.2 = (f32[1,2176]{1,0:T(1,128)S(1)}, f32[1,2176]{1,0:T(1,128)S(1)}, u32[]{:S(2)}, u32[]{:S(2)}) collective-permute-start(f32[1,2176]{1,0:T(1,128)S(1)} %fusion.refs_0_), channel_id=1, source_target_pairs={{0,24},{8,16},{16,8},{24,0},{1,25},{9,17},{17,9},{25,1},{2,26},{10... | collective-permute-start | bytes 26120 | tf_op jit(solution)/shard_map/ppermute | solution.py:360
  6.4 0.2 collective-permute-start.1
  6.6 0.1 collective-permute-start
  6.8 1.2 %collective-permute-start.3 = (f32[512,256]{1,0:T(8,128)}, f32[512,256]{1,0:T(8,128)S(1)}, u32[]{:S(2)}, u32[]{:S(2)}) collective-permute-start(f32[512,256]{1,0:T(8,128)} %bitcast.17), channel_id=1, source_target_pairs={{0,1},{1,0},{2,3},{3,2},{4,5},{5,4},{6,7},{7,6},{8,9},{9,8},{10,11... | collective-permute-start | bytes 1572872 | tf_op jit(solution)/shard_map/ppermute | solution.py:366
  8.0 0.1 slice.39
  8.1 0.1 stack.23.scal
  8.1 0.0 collective-permute-done.2.refs_3_
  8.1 0.1 slice.48
  8.2 0.7 collective-permute-done.1.refs_2_
  8.9 0.1 slice.47
  9.0 0.2 collective-permute-done.refs_1_
  9.1 0.1 slice.46
  9.2 0.1 pad_maximum_fusion
  9.3 2.4 %collective-permute-start.7 = (f32[1,128]{1,0:T(1,128)S(1)}, f32[1,128]{1,0:T(1,128)S(1)}, u32[]{:S(2)}, u32[]{:S(2)}) collective-permute-start(f32[1,128]{1,0:T(1,128)S(1)} %pad_maximum_fusion), channel_id=1, source_target_pairs={{0,1},{1,0},{2,3},{3,2},{4,5},{5,4},{6,7},{7,6},{8,9},{9,8},{10,11... | collective-permute-start | bytes 1544 | tf_op jit(solution)/shard_map/ppermute | solution.py:366
  11.7 0.8 collective-permute-done.7
  12.5 0.1 maximum_select_fusion.refs_4_
  12.6 3.4 %collective-permute-start.10 = (f32[2,128]{1,0:T(2,128)S(1)}, f32[2,128]{1,0:T(2,128)S(1)}, u32[]{:S(2)}, u32[]{:S(2)}) collective-permute-start(f32[2,128]{1,0:T(2,128)S(1)} %maximum_select_fusion.refs_4_), channel_id=1, source_target_pairs={{0,6},{1,7},{2,4},{3,5},{4,2},{5,3},{6,0},{7,1},{8,14},{9,15},{10,... | collective-permute-start | bytes 3080 | tf_op jit(solution)/shard_map/ppermute | solution.py:363
  16.0 4.4 %events.1 = (f32[208,256]{1,0:T(8,128)S(1)}, f32[4,208,256]{2,1,0:T(8,128)S(1)}) custom-call(s32[6]{0:T(128)S(1)} %stack.23.scal, s32[3,2048]{1,0:T(4,128)S(1)} %copy-done.4, f32[1,2176]{1,0:T(1,128)S(1)} %fusion.refs_0_, f32[1,2176]{1,0:T(1,128)S(1)} %collective-permute-done.refs_1_, f32[1,2176]{1,0:T(1,128)S(1)} %collective-permute-done.1.refs_2_, ...), custom_call_target="tpu_custom_call" | custom-call | flops 2000000000 | bytes 2000000 | tf_op jit(solution)/shard_map/events/pallas_call | solution.py:402
  20.4 0.9 copy-done
  21.3 0.0 collective-permute-start.9
  21.3 0.3 collective-permute-start.8
  21.6 0.0 collective-permute-done.3.other
  21.6 0.6 pack.1
  22.2 0.6 copy-done.3
  22.9 1.2 %collective-permute-start.4 = (f32[2,32,256]{2,1,0:T(8,128)S(1)}, f32[2,32,256]{2,1,0:T(8,128)S(1)}, u32[]{:S(2)}, u32[]{:S(2)}) collective-permute-start(f32[2,32,256]{2,1,0:T(8,128)S(1)} %get-tuple-element.11), channel_id=1, source_target_pairs={{0,2},{1,3},{2,0},{3,1},{4,6},{5,7},{6,4},{7,5},{8,10},{9,11},{10,... | collective-permute-start | bytes 196616 | tf_op jit(solution)/shard_map/ppermute | solution.py:363
  24.1 2.3 %collective-permute-start.5 = (f32[2,32,256]{2,1,0:T(8,128)S(1)}, f32[2,32,256]{2,1,0:T(8,128)S(1)}, u32[]{:S(2)}, u32[]{:S(2)}) collective-permute-start(f32[2,32,256]{2,1,0:T(8,128)S(1)} %get-tuple-element.12), channel_id=1, source_target_pairs={{0,4},{1,5},{2,6},{3,7},{4,0},{5,1},{6,2},{7,3},{8,12},{9,13},{10,... | collective-permute-start | bytes 196616 | tf_op jit(solution)/shard_map/ppermute | solution.py:363
  26.4 0.0 collective-permute-done.10.refs_7_
  26.4 0.0 collective-permute-start.6
  26.4 0.1 maximum_convert_fusion
  26.5 0.4 copy-done.10
  26.9 0.6 concatenate.36.scal
  27.5 0.0 collective-permute-done.9.refs_6_
  27.5 0.0 collective-permute-done.8.refs_5_
  27.5 0.0 copy-start.12
  27.5 0.0 collective-permute-done.4.refs_1_
  27.6 1.2 %collective-permute-done.5.refs_2_ = f32[2,32,256]{2,1,0:T(8,128)S(1)} collective-permute-done((f32[2,32,256]{2,1,0:T(8,128)S(1)}, f32[2,32,256]{2,1,0:T(8,128)S(1)}, u32[]{:S(2)}, u32[]{:S(2)}) %collective-permute-start.5) | collective-permute-done | bytes 65568 | tf_op jit(solution)/shard_map/ppermute | solution.py:363
  28.8 2.6 %collective-permute-done.6.refs_3_ = f32[2,32,256]{2,1,0:T(8,128)S(1)} collective-permute-done((f32[2,32,256]{2,1,0:T(8,128)S(1)}, f32[2,32,256]{2,1,0:T(8,128)S(1)}, u32[]{:S(2)}, u32[]{:S(2)}) %collective-permute-start.6) | collective-permute-done | bytes 65568 | tf_op jit(solution)/shard_map/ppermute | solution.py:363
  31.4 0.6 copy-done.7
  32.0 30.5 %solve.1 = (f32[4,8,16,256]{3,2,1,0:T(8,128)}, f32[8,16,256]{2,1,0:T(8,128)}) custom-call(s32[18]{0:T(128)} %concatenate.36.scal, f32[2,32,256]{2,1,0:T(8,128)} %copy-done.3, f32[2,32,256]{2,1,0:T(8,128)} %copy-done.5, f32[2,32,256]{2,1,0:T(8,128)} %copy-done.6, f32[2,32,256]{2,1,0:T(8,128)} %copy-done.7, f32[2,128]{1,0:T(2,128)} %copy-done.9, ...), custom_call_target="tpu_custom_call" | custom-call | tf_op jit(solution)/shard_map/solve/pallas_call | solution.py:418
  62.5 11.8 %all_to_all.10 = f32[8,16,256]{2,1,0:T(8,128)S(1)} all-to-all(f32[8,16,256]{2,1,0:T(8,128)} %get-tuple-element.17), channel_id=1, replica_groups=mesh['src'=4,'space'=8] {'space'}, dimensions={0} | all-to-all | bytes 262144 | tf_op jit(solution)/shard_map/all_to_all | solution.py:450
  74.3 3.4 %all-to-all-start = ((f32[32,16,256]{2,1,0:T(8,128)}), f32[32,16,256]{2,1,0:T(8,128)S(1)}, u32[]{:S(2)}, u32[]{:S(2)}) async-start(f32[32,16,256]{2,1,0:T(8,128)} %bitcast.20), calls=%async_computation | async-start | bytes 1048576 | tf_op jit(solution)/shard_map/all_to_all | solution.py:447
  77.8 16.1 %all-to-all-done = f32[32,16,256]{2,1,0:T(8,128)S(1)} async-done(((f32[32,16,256]{2,1,0:T(8,128)}), f32[32,16,256]{2,1,0:T(8,128)S(1)}, u32[]{:S(2)}, u32[]{:S(2)}) %all-to-all-start) | async-done | bytes 524320 | tf_op jit(solution)/shard_map/all_to_all | solution.py:447
  93.9 0.8 copy.9
  94.7 0.7 copy.10
  (26 shorter events, 0.1 us)
Async XLA Ops:
  0.6 2.7 %copy-start.8 = (f32[1,2048]{1,0:T(1,128)S(1)}, f32[1,2048]{1,0:T(1,128)}, u32[]{:S(2)}) copy-start(f32[1,2048]{1,0:T(1,128)} %param.8) | copy-start | bytes 24580
  3.3 4.8 %collective-permute-start.2 = (f32[1,2176]{1,0:T(1,128)S(1)}, f32[1,2176]{1,0:T(1,128)S(1)}, u32[]{:S(2)}, u32[]{:S(2)}) collective-permute-start(f32[1,2176]{1,0:T(1,128)S(1)} %fusion.refs_0_), channel_id=1, source_target_pairs={{0,24},{8,16},{16,8},{24,0},{1,25},{9,17},{17,9},{25,1},{2,26},{10... | collective-permute-start | bytes 26120 | tf_op jit(solution)/shard_map/ppermute | solution.py:360
  6.4 2.5 %collective-permute-start.1 = (f32[1,2176]{1,0:T(1,128)S(1)}, f32[1,2176]{1,0:T(1,128)S(1)}, u32[]{:S(2)}, u32[]{:S(2)}) collective-permute-start(f32[1,2176]{1,0:T(1,128)S(1)} %fusion.refs_0_), channel_id=1, source_target_pairs={{0,16},{8,24},{16,0},{24,8},{1,17},{9,25},{17,1},{25,9},{2,18},{10... | collective-permute-start | bytes 26120 | tf_op jit(solution)/shard_map/ppermute | solution.py:360
  6.6 2.5 %collective-permute-start = (f32[1,2176]{1,0:T(1,128)S(1)}, f32[1,2176]{1,0:T(1,128)S(1)}, u32[]{:S(2)}, u32[]{:S(2)}) collective-permute-start(f32[1,2176]{1,0:T(1,128)S(1)} %fusion.refs_0_), channel_id=1, source_target_pairs={{0,8},{8,0},{16,24},{24,16},{1,9},{9,1},{17,25},{25,17},{2,10},{10... | collective-permute-start | bytes 26120 | tf_op jit(solution)/shard_map/ppermute | solution.py:360
  6.8 14.9 %collective-permute-start.3 = (f32[512,256]{1,0:T(8,128)}, f32[512,256]{1,0:T(8,128)S(1)}, u32[]{:S(2)}, u32[]{:S(2)}) collective-permute-start(f32[512,256]{1,0:T(8,128)} %bitcast.17), channel_id=1, source_target_pairs={{0,1},{1,0},{2,3},{3,2},{4,5},{5,4},{6,7},{7,6},{8,9},{9,8},{10,11... | collective-permute-start | bytes 1572872 | tf_op jit(solution)/shard_map/ppermute | solution.py:366
  8.1 7.9 %copy-start.4 = (s32[3,2048]{1,0:T(4,128)S(1)}, s32[3,2048]{1,0:T(4,128)}, u32[]{:S(2)}) copy-start(s32[3,2048]{1,0:T(4,128)} %cells.1) | copy-start | bytes 73732
  9.3 3.2 %collective-permute-start.7 = (f32[1,128]{1,0:T(1,128)S(1)}, f32[1,128]{1,0:T(1,128)S(1)}, u32[]{:S(2)}, u32[]{:S(2)}) collective-permute-start(f32[1,128]{1,0:T(1,128)S(1)} %pad_maximum_fusion), channel_id=1, source_target_pairs={{0,1},{1,0},{2,3},{3,2},{4,5},{5,4},{6,7},{7,6},{8,9},{9,8},{10,11... | collective-permute-start | bytes 1544 | tf_op jit(solution)/shard_map/ppermute | solution.py:366
  12.6 8.7 %copy-start.9 = (f32[2,128]{1,0:T(2,128)}, f32[2,128]{1,0:T(2,128)S(1)}, u32[]{:S(2)}) copy-start(f32[2,128]{1,0:T(2,128)S(1)} %maximum_select_fusion.refs_4_) | copy-start | bytes 3076
  12.6 9.1 %copy-start.1 = (f32[1,512,256]{2,1,0:T(8,128)S(1)}, f32[1,512,256]{2,1,0:T(8,128)}, u32[]{:S(2)}) copy-start(f32[1,512,256]{2,1,0:T(8,128)} %param.5) | copy-start | bytes 1572868
  12.6 13.8 %collective-permute-start.10 = (f32[2,128]{1,0:T(2,128)S(1)}, f32[2,128]{1,0:T(2,128)S(1)}, u32[]{:S(2)}, u32[]{:S(2)}) collective-permute-start(f32[2,128]{1,0:T(2,128)S(1)} %maximum_select_fusion.refs_4_), channel_id=1, source_target_pairs={{0,6},{1,7},{2,4},{3,5},{4,2},{5,3},{6,0},{7,1},{8,14},{9,15},{10,... | collective-permute-start | bytes 3080 | tf_op jit(solution)/shard_map/ppermute | solution.py:363
  20.4 0.9 copy-start
  21.3 0.9 copy-start.2
  21.3 6.2 %collective-permute-start.9 = (f32[2,128]{1,0:T(2,128)S(1)}, f32[2,128]{1,0:T(2,128)S(1)}, u32[]{:S(2)}, u32[]{:S(2)}) collective-permute-start(f32[2,128]{1,0:T(2,128)S(1)} %maximum_select_fusion.refs_4_), channel_id=1, source_target_pairs={{0,4},{1,5},{2,6},{3,7},{4,0},{5,1},{6,2},{7,3},{8,12},{9,13},{10,... | collective-permute-start | bytes 3080 | tf_op jit(solution)/shard_map/ppermute | solution.py:363
  21.3 6.2 %collective-permute-start.8 = (f32[2,128]{1,0:T(2,128)S(1)}, f32[2,128]{1,0:T(2,128)S(1)}, u32[]{:S(2)}, u32[]{:S(2)}) collective-permute-start(f32[2,128]{1,0:T(2,128)S(1)} %maximum_select_fusion.refs_4_), channel_id=1, source_target_pairs={{0,2},{1,3},{2,0},{3,1},{4,6},{5,7},{6,4},{7,5},{8,10},{9,11},{10,... | collective-permute-start | bytes 3080 | tf_op jit(solution)/shard_map/ppermute | solution.py:363
  22.2 0.6 copy-start.3
  22.9 4.7 %collective-permute-start.4 = (f32[2,32,256]{2,1,0:T(8,128)S(1)}, f32[2,32,256]{2,1,0:T(8,128)S(1)}, u32[]{:S(2)}, u32[]{:S(2)}) collective-permute-start(f32[2,32,256]{2,1,0:T(8,128)S(1)} %get-tuple-element.11), channel_id=1, source_target_pairs={{0,2},{1,3},{2,0},{3,1},{4,6},{5,7},{6,4},{7,5},{8,10},{9,11},{10,... | collective-permute-start | bytes 196616 | tf_op jit(solution)/shard_map/ppermute | solution.py:363
  24.1 4.7 %collective-permute-start.5 = (f32[2,32,256]{2,1,0:T(8,128)S(1)}, f32[2,32,256]{2,1,0:T(8,128)S(1)}, u32[]{:S(2)}, u32[]{:S(2)}) collective-permute-start(f32[2,32,256]{2,1,0:T(8,128)S(1)} %get-tuple-element.12), channel_id=1, source_target_pairs={{0,4},{1,5},{2,6},{3,7},{4,0},{5,1},{6,2},{7,3},{8,12},{9,13},{10,... | collective-permute-start | bytes 196616 | tf_op jit(solution)/shard_map/ppermute | solution.py:363
  26.4 0.5 copy-start.10
  26.4 5.0 %collective-permute-start.6 = (f32[2,32,256]{2,1,0:T(8,128)S(1)}, f32[2,32,256]{2,1,0:T(8,128)S(1)}, u32[]{:S(2)}, u32[]{:S(2)}) collective-permute-start(f32[2,32,256]{2,1,0:T(8,128)S(1)} %get-tuple-element.13), channel_id=1, source_target_pairs={{0,6},{1,7},{2,4},{3,5},{4,2},{5,3},{6,0},{7,1},{8,14},{9,15},{10,... | collective-permute-start | bytes 196616 | tf_op jit(solution)/shard_map/ppermute | solution.py:363
  27.5 3.9 %copy-start.11 = (f32[2,128]{1,0:T(2,128)}, f32[2,128]{1,0:T(2,128)S(1)}, u32[]{:S(2)}) copy-start(f32[2,128]{1,0:T(2,128)S(1)} %collective-permute-done.9.refs_6_) | copy-start | bytes 3076
  27.5 3.9 %copy-start.12 = (f32[2,128]{1,0:T(2,128)}, f32[2,128]{1,0:T(2,128)S(1)}, u32[]{:S(2)}) copy-start(f32[2,128]{1,0:T(2,128)S(1)} %collective-permute-done.8.refs_5_) | copy-start | bytes 3076
  27.6 3.8 %copy-start.5 = (f32[2,32,256]{2,1,0:T(8,128)}, f32[2,32,256]{2,1,0:T(8,128)S(1)}, u32[]{:S(2)}) copy-start(f32[2,32,256]{2,1,0:T(8,128)S(1)} %collective-permute-done.4.refs_1_) | copy-start | bytes 196612
  28.8 2.6 %copy-start.6 = (f32[2,32,256]{2,1,0:T(8,128)}, f32[2,32,256]{2,1,0:T(8,128)S(1)}, u32[]{:S(2)}) copy-start(f32[2,32,256]{2,1,0:T(8,128)S(1)} %collective-permute-done.5.refs_2_) | copy-start | bytes 196612
  31.4 0.6 copy-start.7
  74.3 19.6 %all-to-all-start = ((f32[32,16,256]{2,1,0:T(8,128)}), f32[32,16,256]{2,1,0:T(8,128)S(1)}, u32[]{:S(2)}, u32[]{:S(2)}) async-start(f32[32,16,256]{2,1,0:T(8,128)} %bitcast.20), calls=%async_computation | async-start | bytes 1048576 | tf_op jit(solution)/shard_map/all_to_all | solution.py:447

commit v2 on v0

v2 whole, which is shorter than its diff:
```python
import functools
import math

import jax
import jax.numpy as jnp
from jax import lax
from jax.experimental import pallas as pl
from jax.experimental.pallas import tpu as pltpu
from jax.sharding import PartitionSpec as P

TY = 32
ROUNDS = 2
SWEEPS = 2
ADJ_SWEEPS = 4
BIG = 1000000.0

HALO = ROUNDS * SWEEPS + ADJ_SWEEPS
ADJ_HALO = ADJ_SWEEPS + 1

VMEM = pltpu.VMEM
SMEM = pltpu.SMEM


def spec(space):
    return pl.BlockSpec(memory_space=space)


def call(body, name, outs, operands, scratch=(), microseconds=1.0):
    held = [*operands, *outs, *scratch]
    limit = 4 * 2**20 + sum(4 * math.prod((*a.shape[:-2], -(-math.prod(a.shape[-2:-1]) // 8) * 8, max(a.shape[-1], 128))) for a in held)
    return pl.pallas_call(
        body,
        out_shape=list(outs),
        in_specs=[spec(SMEM if a.ndim == 1 else VMEM) for a in operands],
        out_specs=[spec(VMEM)] * len(outs),
        scratch_shapes=list(scratch),
        compiler_params=pltpu.CompilerParams(vmem_limit_bytes=limit),
        cost_estimate=pl.CostEstimate(
            flops=0, bytes_accessed=int(microseconds * 3.5e6), transcendentals=0
        ),
        name=name,
    )(*operands)


def head_kernel(delays, station, active, active_other, out):
    events = delays.shape[1]
    out[:, :events] = delays[...]
    out[:, events:] = jnp.zeros((1, out.shape[1] - events), jnp.float32)
    at = events
    out[:, at : at + 3] = station[...].astype(jnp.float32)
    for source in (active, active_other):
        for part in range(ROUNDS):
            at += 128
            out[:, at : at + source.shape[-1]] = source[part].astype(jnp.float32)


def pack_kernel(rows, own_rows, scal, own, other, *outs):
    line_row, chip, core = scal[0], scal[1], scal[2]
    total = own.shape[0]
    chunk = math.gcd(own_rows, 8)
    for j, out in enumerate(outs):
        first = line_row + ((chip ^ j) * 2 + core) * own_rows - HALO
        for piece in range(rows // chunk):
            start = jnp.clip(first + piece * chunk, 0, total - chunk)
            start = pl.multiple_of(start, chunk)
            out[0, piece * chunk : (piece + 1) * chunk, :] = own[pl.ds(start, chunk), :]
            out[1, piece * chunk : (piece + 1) * chunk, :] = other[pl.ds(start, chunk), :]


def scatter_kernel(layers, events, scal, cells, *refs):
    slots = len(refs) - 2
    pays, count, delay_sum = refs[:slots], refs[slots], refs[slots + 1]
    first_row = scal[3] + HALO - ADJ_HALO
    height, width = count.shape
    chunk = min(events, 512)
    cells_iota = lax.broadcasted_iota(jnp.int32, (height, chunk), 0)
    depth_iota = lax.broadcasted_iota(jnp.int32, (width, chunk), 0)
    contract = (((1,), (1,)), ((), ()))

    def step(index, carry):
        start = pl.multiple_of(index * chunk, chunk)
        where_x = cells[0:1, pl.ds(start, chunk)]
        where_y = cells[1:2, pl.ds(start, chunk)] - first_row
        where_z = cells[2:3, pl.ds(start, chunk)]
        at = jnp.where(where_y >= 0, where_y * layers + where_x, -1)
        hit = (cells_iota == at).astype(jnp.bfloat16)
        depth = (depth_iota == where_z).astype(jnp.bfloat16)

        def add(ref_index, value):
            if ref_index is None:
                count[...] += value
            else:
                delay_sum[ref_index] += value

        def dot(left):
            return lax.dot_general(left, depth, contract, preferred_element_type=jnp.float32)

        add(None, dot(hit))
        for slot in range(slots):
            delay = pays[slot][:, pl.ds(start, chunk)]
            high = delay.astype(jnp.bfloat16)
            low = (delay - high.astype(jnp.float32)).astype(jnp.bfloat16)
            add(slot, dot(hit * high) + dot(hit * low))
        return carry

    count[...] = jnp.zeros_like(count)
    delay_sum[...] = jnp.zeros_like(delay_sum)
    lax.fori_loop(0, events // chunk, step, 0)


LANES = 128


def get(ref, row, size, *lead):
    index = (*lead, pl.ds(row, size))
    return [
        ref[(*index, slice(None), slice(p, p + LANES))] for p in range(0, ref.shape[-1], LANES)
    ]


def put(ref, row, size, value, *lead):
    index = (*lead, pl.ds(row, size))
    for p, piece in enumerate(value):
        ref[(*index, slice(None), slice(p * LANES, (p + 1) * LANES))] = piece


def each(function, *values):
    return [function(*pieces) for pieces in zip(*values)]


def loop(low, high, size, body, unroll=1):
    steps = (high - low) // size
    if steps:
        lax.fori_loop(
            0,
            steps,
            lambda i, carry: (body(low + i * size, size), carry)[1],
            0,
            unroll=min(unroll, steps),
        )
    if low + steps * size < high:
        loop(low + steps * size, high, max(size // 2, 1), body)


class Grid:
    def __init__(self, size, layers, depth):
        shape = (size, layers, LANES)
        layer = lax.broadcasted_iota(jnp.int32, shape, 1)
        lane = lax.broadcasted_iota(jnp.int32, shape, 2)
        self.layers = layers
        self.layer_low, self.layer_high = layer == 0, layer == layers - 1
        self.lane_low, self.lane_high = lane == 0, lane == LANES - 1

    def layer_before(self, value):
        return [pltpu.roll(piece, 1, 1) for piece in value]

    def layer_after(self, value):
        return [pltpu.roll(piece, self.layers - 1, 1) for piece in value]

    def depth_before(self, value, fill=None):
        moved = [pltpu.roll(piece, 1, 2) for piece in value]
        first = moved[0] if fill is None else jnp.where(self.lane_low, fill, moved[0])
        rest = [
            jnp.where(self.lane_low, low, here) for low, here in zip(moved[:-1], moved[1:])
        ]
        return [first] + rest

    def depth_after(self, value, fill=None):
        moved = [pltpu.roll(piece, LANES - 1, 2) for piece in value]
        last = moved[-1] if fill is None else jnp.where(self.lane_high, fill, moved[-1])
        rest = [
            jnp.where(self.lane_high, high, here) for here, high in zip(moved[:-1], moved[1:])
        ]
        return rest + [last]

    def no_low(self, value, fill):
        return [jnp.where(self.layer_low, fill, piece) for piece in value]

    def no_high(self, value, fill):
        return [jnp.where(self.layer_high, fill, piece) for piece in value]


class Flat:
    def __init__(self, ref, layers):
        self.ref, self.layers, self.parts = ref, layers, ref.shape[0]

    def put_layer(self, place, rows, value):
        for p in range(self.parts):
            self.ref.at[p][pl.ds(place, rows, stride=self.layers), :] = value[
                :, p * LANES : (p + 1) * LANES
            ]

    def get_layer(self, place, rows):
        pieces = [
            self.ref.at[p][pl.ds(place, rows, stride=self.layers), :] for p in range(self.parts)
        ]
        return jnp.concatenate(pieces, axis=1)

    def span(self, row, size):
        return pl.ds(pl.multiple_of(row * self.layers, self.layers), size * self.layers)

    def get(self, row, size):
        return [
            self.ref[p, self.span(row, size), :].reshape(size, self.layers, LANES)
            for p in range(self.parts)
        ]

    def put(self, row, size, value):
        for p in range(self.parts):
            self.ref[p, self.span(row, size), :] = value[p].reshape(size * self.layers, LANES)


def root_of(value):
    value = jnp.maximum(value, 1e-30)
    return value * lax.rsqrt(value)


def distance(layers, at, y, grid_rows, size, row, piece):
    shape = (size, layers, LANES)
    dx = (lax.broadcasted_iota(jnp.int32, shape, 1) - at[0]).astype(jnp.float32)
    dz = (lax.broadcasted_iota(jnp.int32, shape, 2) + (piece * LANES - at[2])).astype(jnp.float32)
    here = lax.broadcasted_iota(jnp.int32, shape, 0) + (y + row)
    dy = (here - at[1]).astype(jnp.float32)
    far = jnp.sqrt(dx * dx + dy * dy + dz * dz)
    return jnp.where((here >= 0) & (here < grid_rows), far, BIG)


def local_solve(near_x, near_y, near_z, cost, twice, one_half):
    small = jnp.minimum(near_x, near_y)
    large = jnp.maximum(near_x, near_y)
    lowest = jnp.minimum(small, near_z)
    highest = jnp.maximum(large, near_z)
    middle = jnp.maximum(small, jnp.minimum(large, near_z))
    first_gap = middle - lowest
    second_gap = highest - lowest
    square = first_gap * first_gap
    single = lowest + cost
    double = lowest + 0.5 * (first_gap + root_of(twice - square))
    rest = square + second_gap * (second_gap - first_gap)
    root = root_of(one_half - rest)
    triple = lowest + ((first_gap + second_gap) * (1.0 / 3.0) + root * (math.sqrt(2.0) / 3.0))
    return jnp.where(single <= middle, single, jnp.where(double <= highest, double, triple))


SWEEP_ROWS = 4
SWEEP_UNROLL = 2


def sweep_kernel(layers, own_rows, slots, chips, scal, *refs):
    rows = own_rows + 2 * HALO
    depth = refs[0].shape[-1]
    parts = depth // LANES
    vel_in, refs = refs[:chips], refs[chips:]
    act_in, refs = refs[:chips], refs[chips:]
    times_out, final, speed, refs = refs[0], refs[1], refs[2], refs[3:]
    cost, twice, one_half, ping, pong, acts, mask, flat = refs
    flat = Flat(flat, layers)
    line, chip, core, y_first, grid_rows = scal[4], scal[1], scal[2], scal[3], scal[5]
    stations = [[scal[6 + 3 * slot + i] for i in range(3)] for slot in range(slots)]

    for j in range(chips):
        for c in range(2):
            place = (chip ^ j) * 2 + (core ^ c)
            flat.put_layer(place, rows, vel_in[j][c])
            for slot in range(slots):
                for part in range(ROUNDS):
                    acts[slot * ROUNDS + part, pl.ds(place, 1), :] = act_in[j][
                        pl.ds((slot * 2 + c) * ROUNDS + part, 1), :
                    ]

    def prepare(row, size):
        value = flat.get(row, size)
        slow = each(lambda v: 1.0 / v, value)
        put(speed, row, size, value)
        put(cost, row, size, slow)
        put(twice, row, size, each(lambda f: 2.0 * (f * f), slow))
        put(one_half, row, size, each(lambda f: 1.5 * (f * f), slow))

    loop(0, rows, 4, prepare)

    def fill(row, size):
        for slot in range(slots):
            value = [
                distance(layers, stations[slot], y_first - 1, grid_rows, size, row, piece)
                for piece in range(parts)
            ]
            put(ping, row, size, value, slot)

    loop(0, rows + 2, 2, fill)

    lane_iota = lax.broadcasted_iota(jnp.int32, (layers, LANES), 1)
    tile_first = (y_first + TY) // TY - 1
    tile_span = (rows + TY - 2) // TY + 1
    for slot in range(slots):
        for part in range(ROUNDS):
            act = acts[slot * ROUNDS + part]
            columns = []
            for t in range(tile_span):
                here = lane_iota == tile_first + t
                picked = jnp.sum(jnp.where(here, act, 0.0), axis=1, keepdims=True)
                columns.append(jnp.broadcast_to(picked, (layers, LANES)))
            for i in range(rows):
                value = columns[0]
                for t in range(1, tile_span):
                    value = jnp.where(y_first + i >= (tile_first + t) * TY, columns[t], value)
                mask[slot, part, i] = value

    def sweep(source, target, low, high, part, shift):
        def body(row, size):
            grid = Grid(size, layers, depth)
            costs = get(cost, row, size), get(twice, row, size), get(one_half, row, size)
            for slot in range(slots):
                field = get(source, row, size + 2, slot)
                here = each(lambda f: f[1 : size + 1], field)
                near_y = each(lambda f: jnp.minimum(f[:size], f[2:]), field)
                near_x = each(
                    jnp.minimum,
                    grid.no_low(grid.layer_before(here), BIG),
                    grid.no_high(grid.layer_after(here), BIG),
                )
                near_z = each(
                    jnp.minimum, grid.depth_before(here, BIG), grid.depth_after(here, BIG)
                )
                update = each(local_solve, near_x, near_y, near_z, *costs)
                on = mask[slot, part, pl.ds(row, size)] > 0.0
                put(
                    target,
                    row + shift,
                    size,
                    each(lambda u, h: jnp.where(on, u, h), update, here),
                    slot,
                )

        loop(low, high, SWEEP_ROWS, body, SWEEP_UNROLL)
        for slot in range(slots):
            at_x, at_y, at_z = stations[slot]
            local = at_y - y_first

            @pl.when((local >= low) & (local < high))
            def _():
                shape = (1, layers, depth)
                there = (lax.broadcasted_iota(jnp.int32, shape, 1) == at_x) & (
                    lax.broadcasted_iota(jnp.int32, shape, 2) == at_z
                )
                here = slot, pl.ds(local + shift, 1)
                target[here] = jnp.where(there, 0.0, target[here])

    fields = [ping, pong]
    last = ROUNDS * SWEEPS - 1
    for index in range(last):
        sweep(fields[index % 2], fields[(index + 1) % 2], index, rows - index, index // SWEEPS, 1)
    sweep(fields[last % 2], final, last, rows - last, last // SWEEPS, -last)

    for slot in range(slots):
        loop(0, own_rows, 4, lambda row, size: flat.put(row, size, get(final, row + ADJ_HALO, size, slot)))
        for place in range(layers):
            times_out[line ^ slot, place] = flat.get_layer(place, own_rows)


ADJ_ROWS = 4
ADJ_UNROLL = 2


def adjoint_kernel(layers, own_rows, slots, scal, final, speed, count, delay_sum, *refs):
    depth = final.shape[-1]
    parts = depth // LANES
    kernel_out, refs = refs[:layers], refs[layers:]
    weight, src, adj_a, adj_b, density, flat = refs
    together = weight.shape[0]
    flat = Flat(flat, layers)
    y_first, grid_rows = scal[3], scal[5]
    stations = [[scal[6 + 3 * slot + i] for i in range(3)] for slot in range(slots)]
    shift = HALO - ADJ_HALO
    rows = own_rows + 2 * ADJ_HALO

    def sums(ref, row, size, *lead):
        span = pl.ds(pl.multiple_of(row * layers, layers), size * layers)
        return [
            ref[(*lead, span, slice(p * LANES, (p + 1) * LANES))].reshape(size, layers, LANES)
            for p in range(parts)
        ]

    def make_source(group, row, size):
        number = sums(count, row, size)
        for slot in group:
            straight = [
                distance(layers, stations[slot], y_first + shift, grid_rows, size, row, piece)
                for piece in range(parts)
            ]
            value = each(
                lambda n, t, d, s: n * (t - d) - s,
                number,
                get(final, row, size, slot),
                straight,
                sums(delay_sum, row, size, slot),
            )
            put(src, row, size, value, slot - group[0])

    def make_weight(group, row, size):
        grid = Grid(size, layers, depth)
        scale = each(lambda v: v * (1.0 / 6.0), get(speed, row + shift, size))
        for slot in group:
            field = get(final, row - 1, size + 2, slot)
            here = each(lambda f: f[1 : size + 1], field)

            def rise(value):
                return each(lambda v, h, s: jnp.maximum(v - h, 0.0) * s, value, here, scale)

            def keep(value, piece, edge):
                return [jnp.where(edge, 0.0, v) if p == piece else v for p, v in enumerate(value)]

            six = [
                grid.no_low(rise(grid.layer_before(here)), 0.0),
                grid.no_high(rise(grid.layer_after(here)), 0.0),
                rise(each(lambda f: f[:size], field)),
                rise(each(lambda f: f[2:], field)),
                keep(rise(grid.depth_before(here)), 0, grid.lane_low),
                keep(rise(grid.depth_after(here)), parts - 1, grid.lane_high),
            ]
            for n, value in enumerate(six):
                put(weight, row, size, value, slot - group[0], n)

    def multiply_add(value, factor, neighbour):
        return value + factor * neighbour

    def smooth(low, here, high):
        return (low + 2.0 * here + high) * 0.25

    def sweep(group, source, target, low, high):
        def body(row, size):
            grid = Grid(size, layers, depth)
            total = None if group[0] == 0 else get(density, row, size)
            for slot in range(len(group)):
                field = get(source, row - 1, size + 2, slot)
                here = each(lambda f: f[1 : size + 1], field)
                around = [
                    grid.layer_before(here),
                    grid.layer_after(here),
                    each(lambda f: f[:size], field),
                    each(lambda f: f[2:], field),
                    grid.depth_before(here),
                    grid.depth_after(here),
                ]
                value = get(src, row, size, slot)
                for n, neighbour in enumerate(around):
                    value = each(multiply_add, value, get(weight, row, size, slot, n), neighbour)
                if target is not None:
                    put(target, row, size, value, slot)
                else:
                    total = value if total is None else each(jnp.add, total, value)
            if target is None:
                if group[-1] == slots - 1:
                    value = each(lambda t, v: t / v, total, get(speed, row + shift, size))
                    low = grid.no_low(grid.layer_before(value), 0.0)
                    high = grid.no_high(grid.layer_after(value), 0.0)
                    total = each(smooth, low, value, high)
                put(density, row, size, total)

        loop(low, high, ADJ_ROWS, body, ADJ_UNROLL)

    for first in range(0, slots, together):
        group = range(first, min(first + together, slots))
        loop(0, rows, 2, functools.partial(make_source, group))
        loop(1, rows - 1, 2, functools.partial(make_weight, group))
        fields = [src] + [(adj_a, adj_b)[i % 2] for i in range(ADJ_SWEEPS - 1)] + [None]
        for index in range(ADJ_SWEEPS):
            sweep(group, fields[index], fields[index + 1], index + 1, rows - 1 - index)

    def finish(row, size):
        grid = Grid(size, layers, depth)
        field = get(density, row + ADJ_SWEEPS, size + 2)
        value = each(lambda f: smooth(f[:size], f[1 : size + 1], f[2:]), field)
        low, high = grid.depth_before(value, 0.0), grid.depth_after(value, 0.0)
        flat.put(row, size, each(smooth, low, value, high))

    loop(0, own_rows, 4, finish)
    for m, out in enumerate(kernel_out):
        out[...] = flat.get_layer(scal[1] * 2 + scal[2] ^ m, own_rows)


def join_kernel(scal, *refs):
    blocks, out = refs[:-1], refs[-1]
    rows = blocks[0].shape[0]
    for m, block in enumerate(blocks):
        out[0, pl.ds(pl.multiple_of(((scal[1] * 2 + scal[2]) ^ m) * rows, rows), rows), :] = block[...]


def per_device(velocity, station_cells, event_cells, delays, active):
    _, grid_rows, depth = velocity.shape
    slots, layers = lax.axis_size("src"), lax.axis_size("space")
    chips = layers // 2
    events = event_cells.shape[1]
    line_rows = grid_rows // slots
    own_rows = line_rows // layers
    rows = own_rows + 2 * HALO
    adj_rows = own_rows + 2 * ADJ_HALO
    line, place = lax.axis_index("src"), lax.axis_index("space")
    chip, core = place // 2, place % 2

    def to_line(array, j):
        return lax.ppermute(array, "src", [(i, i ^ j) for i in range(slots)])

    def to_chip(array, j):
        return lax.ppermute(array, "space", [(i, i ^ (2 * j)) for i in range(layers)])

    def to_core(array):
        return lax.ppermute(array, "space", [(i, i ^ 1) for i in range(layers)])

    f32 = jnp.float32
    def out(*shape):
        return jax.ShapeDtypeStruct(shape, f32)

    def scratch(*shape):
        return pltpu.VMEM(shape, f32)

    def field(*lead):
        return (*lead, layers, depth)

    y_first = line * line_rows + place * own_rows - HALO
    here = jnp.stack([line * line_rows, chip, core, y_first, line, jnp.int32(grid_rows)])
    here = here.astype(jnp.int32)

    other = to_core(velocity[0])
    active_other = to_core(active[:, 0])
    (payload,) = call(
        head_kernel,
        "head",
        [out(1, events + LANES * (1 + 2 * ROUNDS))],
        [delays, station_cells, active[:, 0], active_other],
    )
    pays = [payload] + [to_line(payload, j) for j in range(1, slots)]

    packed = call(
        functools.partial(pack_kernel, rows, own_rows),
        "pack",
        [out(2, rows, depth)] * chips,
        [here, velocity[0], other],
    )
    vel = [to_chip(packed[j], j) for j in range(1, chips)]

    pays, cells, own_block = lax.optimization_barrier((pays, event_cells, packed[0]))
    act = jnp.concatenate(
        [
            p[:, at : at + LANES]
            for p in pays
            for at in range(events + LANES, payload.shape[1], LANES)
        ]
    )
    acts = [act] + [to_chip(act, j) for j in range(1, chips)]
    stations = jnp.concatenate([p[0, events : events + 3] for p in pays]).astype(jnp.int32)
    scal = jnp.concatenate([here, stations])

    count, delay_sum = call(
        functools.partial(scatter_kernel, layers, events),
        "events",
        [out(adj_rows * layers, depth), out(slots, adj_rows * layers, depth)],
        [here, cells, *pays],
        microseconds=4.0,
    )

    together = min(slots, 4)
    flat = scratch(depth // LANES, rows * layers, LANES)
    times, final, speed = call(
        functools.partial(sweep_kernel, layers, own_rows, slots, chips),
        "sweeps",
        [
            out(slots, layers, own_rows, depth),
            out(*field(slots, adj_rows)),
            out(*field(rows)),
        ],
        [scal, own_block, *vel, *acts],
        [
            scratch(*field(rows)),
            scratch(*field(rows)),
            scratch(*field(rows)),
            scratch(*field(slots, rows + 2)),
            scratch(*field(slots, rows + 2)),
            scratch(slots * ROUNDS, layers, LANES),
            scratch(slots, ROUNDS, rows, layers, LANES),
            flat,
        ],
        microseconds=10.0,
    )
    kernel = call(
        functools.partial(adjoint_kernel, layers, own_rows, slots),
        "adjoint",
        [out(own_rows, depth)] * layers,
        [scal, final, speed, count, delay_sum],
        [
            scratch(*field(together, 6, adj_rows)),
            scratch(*field(together, adj_rows)),
            scratch(*field(together, adj_rows)),
            scratch(*field(together, adj_rows)),
            scratch(*field(adj_rows)),
            flat,
        ],
        microseconds=7.0,
    )

    times = lax.all_to_all(
        times.reshape(slots * layers, own_rows, depth), ("src", "space"), 0, 0, tiled=True
    )
    blocks = [kernel[0]] + [
        lax.ppermute(kernel[m], "space", [(i, i ^ m) for i in range(layers)])
        for m in range(1, layers)
    ]
    (kernel,) = call(join_kernel, "join", [out(1, line_rows, depth)], [here, *blocks])
    return (times.reshape(1, 1, grid_rows, depth), kernel)


def solution(mesh):
    return jax.shard_map(
        per_device,
        mesh=mesh,
        in_specs=(
            P("space", None, None),
            P("src", None),
            P(),
            P("src", None),
            P(None, "src", "space", None),
        ),
        out_specs=(P("src", "space", None, None), P("space", "src", None)),
        check_vma=False,
    )
```

time: 225 us -> 64.1 us (0.28)
  waiting for transfers between devices: 97.3 us -> 13.1 us
  starting transfers between devices: 62.3 us -> 25.7 us
  other arithmetic: 31.7 us -> 0.08 us
  Pallas kernels: 0 us -> 20.5 us
  between operations: 15.6 us -> 0.73 us
  local copies, waits for them, and re-layouts: 17.5 us -> 3.32 us
    psum x1 -> x0, waiting for transfers between devices: 47.2 us -> none  [per_device(): summed_density = lax.psum(density, 'src')]
    ppermute x20 -> x18, starting transfers between devices: 62.3 us -> 19.5 us  [the longest x7 8.5 us: per_device(): lax.ppermute(kernel[m], 'space', [(i, i ^ m) for i in range(layers)])]
    ppermute x20 -> x18, waiting for transfers between devices: 50.1 us -> 13.1 us  [the longest x6 5.47 us: to_chip(): return lax.ppermute(array, 'space', [(i, i ^ 2 * j) for i in range(layers)])]
    pallas_call x0 -> x6, Pallas kernels: none -> 20.5 us  [call(): pl.pallas_call(body, out_shape=list(outs), in_specs=[spec(SMEM if a.ndim...]
    select_n x7 -> x0, other arithmetic: 13 us -> none  [the longest x4 11 us: sweep_once(): return jnp.where(station_mask, 0.0, chosen)]
    gather x1 -> x0, local copies, waits for them, and re-layouts: 11.8 us -> none  [per_device(): jnp.take(flat_times, jnp.minimum(flat_index, cell_count - 1), axis=1)]
    scatter-add x1 -> x0, other arithmetic: 11.4 us -> none  [per_device(): source = jnp.zeros((station_count, cell_count), jnp.float32).at[:, flat_i...]
    all_to_all x0 -> x1, starting transfers between devices: none -> 6.23 us  [per_device(): lax.all_to_all(times.reshape(slots * layers, own_rows, depth), ('src', 's...]
  transfers between devices with their start and end apart: 21 -> 19, of which waited for: 19 -> 8; matrix products, arithmetic and copies ran while one was open for 2% -> 0% of each run, Pallas kernels for 0% -> 18%
where the time goes in v2:
time: 64.1 us; the launch traced here: 63.4 us
  starting transfers between devices  25.7 us (40%)
  Pallas kernels  20.5 us (32%)
  waiting for transfers between devices  13.1 us (20%)
  local copies, waits for them, and re-layouts  3.32 us (5%)
  between operations  0.73 us (1%)
    pallas_call x6, Pallas kernels, call(): pl.pallas_call(body, out_shape=list(outs), in_specs=[spec(SMEM if a.ndim...  20.5 us
    ppermute x7, starting transfers between devices, per_device(): lax.ppermute(kernel[m], 'space', [(i, i ^ m) for i in range(layers)])  8.5 us
    ppermute x6, starting transfers between devices, to_chip(): return lax.ppermute(array, 'space', [(i, i ^ 2 * j) for i in range(layers)])  7.22 us
    all_to_all x1, starting transfers between devices, per_device(): lax.all_to_all(times.reshape(slots * layers, own_rows, depth), ('src', 's...  6.23 us
    ppermute x6, waiting for transfers between devices, to_chip(): return lax.ppermute(array, 'space', [(i, i ^ 2 * j) for i in range(layers)])  5.47 us
    ppermute x7, waiting for transfers between devices, per_device(): lax.ppermute(kernel[m], 'space', [(i, i ^ m) for i in range(layers)])  4.7 us
    ppermute x3, starting transfers between devices, to_line(): return lax.ppermute(array, 'src', [(i, i ^ j) for i in range(slots)])  3.62 us
    unnamed x11, local copies, waits for them, and re-layouts  3.08 us
  transfers between devices with their start and end apart: 19, of which 8 were waited for; matrix products, arithmetic and copies ran while one was open for 0% of the time, Pallas kernels for 18%

profile of v2, /device:TPU:1, one launch (start us, length us, event | category | flops | bytes accessed | tf_op | source)
XLA Modules:
  0.0 63.4 jit_solution(15490911889321306444)
XLA Ops:
  0.7 0.1 collective-permute-start.4
  0.8 0.5 copy-done.3
  1.3 0.1 collective-permute-start
  1.4 1.2 %collective-permute-done.active_other = s32[2,1,16]{2,1,0:T(1,128)S(1)} collective-permute-done((s32[2,1,16]{2,1,0:T(1,128)S(1)}, s32[2,1,16]{2,1,0:T(1,128)S(1)}, u32[]{:S(2)}, u32[]{:S(2)}) %collective-permute-start) | collective-permute-done | bytes 160 | tf_op jit(solution)/shard_map/ppermute | solution.py:507
  2.6 0.7 %copy-done.2 = f32[1,2048]{1,0:T(1,128)S(1)} copy-done((f32[1,2048]{1,0:T(1,128)S(1)}, f32[1,2048]{1,0:T(1,128)}, u32[]{:S(2)}) %copy-start.2) | copy-done | bytes 8216
  3.3 2.4 %collective-permute-start.1 = (f32[1,2688]{1,0:T(1,128)S(1)}, f32[1,2688]{1,0:T(1,128)S(1)}, u32[]{:S(2)}, u32[]{:S(2)}) collective-permute-start(f32[1,2688]{1,0:T(1,128)S(1)} %head.1.refs_0_), channel_id=1, source_target_pairs={{0,8},{8,0},{16,24},{24,16},{1,9},{9,1},{17,25},{25,17},{2,10},{10... | collective-permute-start | bytes 32264 | tf_op jit(solution)/shard_map/ppermute | solution.py:501
  5.7 1.2 %collective-permute-start.2 = (f32[1,2688]{1,0:T(1,128)S(1)}, f32[1,2688]{1,0:T(1,128)S(1)}, u32[]{:S(2)}, u32[]{:S(2)}) collective-permute-start(f32[1,2688]{1,0:T(1,128)S(1)} %head.1.refs_0_), channel_id=1, source_target_pairs={{0,16},{8,24},{16,0},{24,8},{1,17},{9,25},{17,1},{25,9},{2,18},{10... | collective-permute-start | bytes 32264 | tf_op jit(solution)/shard_map/ppermute | solution.py:501
  6.9 0.0 collective-permute-start.3
  6.9 0.1 stack.23.scal
  7.0 0.0 collective-permute-done.4.other
  7.0 1.0 %copy-done = f32[1,512,256]{2,1,0:T(8,128)S(1)} copy-done((f32[1,512,256]{2,1,0:T(8,128)S(1)}, f32[1,512,256]{2,1,0:T(8,128)}, u32[]{:S(2)}) %copy-start) | copy-done | bytes 524312
  8.1 0.6 pack.1
  8.7 0.0 collective-permute-done.1.refs_1_
  8.7 0.0 collective-permute-done.2.refs_2_
  8.7 1.7 %collective-permute-done.3.refs_3_ = f32[1,2688]{1,0:T(1,128)S(1)} collective-permute-done((f32[1,2688]{1,0:T(1,128)S(1)}, f32[1,2688]{1,0:T(1,128)S(1)}, u32[]{:S(2)}, u32[]{:S(2)}) %collective-permute-start.3) | collective-permute-done | bytes 10784 | tf_op jit(solution)/shard_map/ppermute | solution.py:501
  10.4 0.1 concatenate.12.refs_4_
  10.4 1.4 %collective-permute-start.8 = (f32[16,128]{1,0:T(8,128)S(1)}, f32[16,128]{1,0:T(8,128)S(1)}, u32[]{:S(2)}, u32[]{:S(2)}) collective-permute-start(f32[16,128]{1,0:T(8,128)S(1)} %concatenate.12.refs_4_), channel_id=1, source_target_pairs={{0,2},{1,3},{2,0},{3,1},{4,6},{5,7},{6,4},{7,5},{8,10},{9,11},{10,... | collective-permute-start | bytes 24584 | tf_op jit(solution)/shard_map/ppermute | solution.py:504
  11.8 2.3 %collective-permute-start.9 = (f32[16,128]{1,0:T(8,128)S(1)}, f32[16,128]{1,0:T(8,128)S(1)}, u32[]{:S(2)}, u32[]{:S(2)}) collective-permute-start(f32[16,128]{1,0:T(8,128)S(1)} %concatenate.12.refs_4_), channel_id=1, source_target_pairs={{0,4},{1,5},{2,6},{3,7},{4,0},{5,1},{6,2},{7,3},{8,12},{9,13},{10,... | collective-permute-start | bytes 24584 | tf_op jit(solution)/shard_map/ppermute | solution.py:504
  14.1 0.0 collective-permute-start.10
  14.1 0.3 collective-permute-start.5
  14.4 3.2 %collective-permute-start.6 = (f32[2,32,256]{2,1,0:T(8,128)S(1)}, f32[2,32,256]{2,1,0:T(8,128)S(1)}, u32[]{:S(2)}, u32[]{:S(2)}) collective-permute-start(f32[2,32,256]{2,1,0:T(8,128)S(1)} %get-tuple-element.32), channel_id=1, source_target_pairs={{0,4},{1,5},{2,6},{3,7},{4,0},{5,1},{6,2},{7,3},{8,12},{9,13},{10,... | collective-permute-start | bytes 196616 | tf_op jit(solution)/shard_map/ppermute | solution.py:504
  17.6 0.0 collective-permute-done.8.refs_5_
  17.6 0.0 collective-permute-start.7
  17.6 0.1 maximum_convert_fusion
  17.7 0.1 concatenate.11.scal
  17.8 0.6 collective-permute-done.10.refs_7_
  18.4 0.0 collective-permute-done.5.refs_1_
  18.4 1.8 %collective-permute-done.6.refs_2_ = f32[2,32,256]{2,1,0:T(8,128)S(1)} collective-permute-done((f32[2,32,256]{2,1,0:T(8,128)S(1)}, f32[2,32,256]{2,1,0:T(8,128)S(1)}, u32[]{:S(2)}, u32[]{:S(2)}) %collective-permute-start.6) | collective-permute-done | bytes 65568 | tf_op jit(solution)/shard_map/ppermute | solution.py:504
  20.2 3.1 %collective-permute-done.7.refs_3_ = f32[2,32,256]{2,1,0:T(8,128)S(1)} collective-permute-done((f32[2,32,256]{2,1,0:T(8,128)S(1)}, f32[2,32,256]{2,1,0:T(8,128)S(1)}, u32[]{:S(2)}, u32[]{:S(2)}) %collective-permute-start.7) | collective-permute-done | bytes 65568 | tf_op jit(solution)/shard_map/ppermute | solution.py:504
  23.3 9.2 %sweeps.1 = (f32[4,8,16,256]{3,2,1,0:T(8,128)}, f32[4,26,8,256]{3,2,1,0:T(8,128)S(1)}, f32[32,8,256]{2,1,0:T(8,128)S(1)}) custom-call(s32[18]{0:T(128)S(1)} %concatenate.11.scal, f32[2,32,256]{2,1,0:T(8,128)S(1)} %get-tuple-element.30.refs_0_, f32[2,32,256]{2,1,0:T(8,128)S(1)} %collective-permute-done.5.refs_1_, ...), custom_call_target="tpu_custom_call" | custom-call | bytes 35000000 | tf_op jit(solution)/shard_map/sweeps/pallas_call | solution.py:31
  32.4 6.2 %all-to-all-start = ((f32[32,16,256]{2,1,0:T(8,128)}), f32[32,16,256]{2,1,0:T(8,128)S(1)}, u32[]{:S(2)}, u32[]{:S(2)}) async-start(f32[32,16,256]{2,1,0:T(8,128)} %bitcast.13), calls=%async_computation | async-start | bytes 1048576 | tf_op jit(solution)/shard_map/all_to_all | solution.py:600
  38.7 4.4 %events.1 = (f32[208,256]{1,0:T(8,128)S(1)}, f32[4,208,256]{2,1,0:T(8,128)S(1)}) custom-call(s32[6]{0:T(128)S(1)} %stack.23.scal, s32[3,2048]{1,0:T(4,128)S(1)} %copy-done.1, f32[1,2688]{1,0:T(1,128)S(1)} %head.1.refs_0_, f32[1,2688]{1,0:T(1,128)S(1)} %collective-permute-done.1.refs_1_, f32[1,2688]{1,0:T(1,128)S(1)} %collective-permute-done.2.refs_2_, ...), custom_call_target="tpu_custom_call" | custom-call | bytes 14000000 | tf_op jit(solution)/shard_map/events/pallas_call | solution.py:31
  43.1 5.1 %adjoint.1 = (f32[16,256]{1,0:T(8,128)S(1)}, f32[16,256]{1,0:T(8,128)S(1)}, f32[16,256]{1,0:T(8,128)S(1)}, f32[16,256]{1,0:T(8,128)S(1)}, f32[16,256]{1,0:T(8,12...) custom-call(s32[18]{0:T(128)S(1)} %concatenate.11.scal, ...), custom_call_target="tpu_custom_call" | custom-call | bytes 24500000 | tf_op jit(solution)/shard_map/adjoint/pallas_call | solution.py:31
  48.2 0.5 collective-permute-start.11
  48.7 1.4 %collective-permute-start.12 = (f32[16,256]{1,0:T(8,128)S(1)}, f32[16,256]{1,0:T(8,128)S(1)}, u32[]{:S(2)}, u32[]{:S(2)}) collective-permute-start(f32[16,256]{1,0:T(8,128)S(1)} %get-tuple-element.42), channel_id=1, source_target_pairs={{0,2},{1,3},{2,0},{3,1},{4,6},{5,7},{6,4},{7,5},{8,10},{9,11},{10,... | collective-permute-start | bytes 49160 | tf_op jit(solution)/shard_map/ppermute | solution.py:604
  50.1 0.3 collective-permute-start.13
  50.4 2.4 %collective-permute-start.14 = (f32[16,256]{1,0:T(8,128)S(1)}, f32[16,256]{1,0:T(8,128)S(1)}, u32[]{:S(2)}, u32[]{:S(2)}) collective-permute-start(f32[16,256]{1,0:T(8,128)S(1)} %get-tuple-element.44), channel_id=1, source_target_pairs={{0,4},{1,5},{2,6},{3,7},{4,0},{5,1},{6,2},{7,3},{8,12},{9,13},{10,... | collective-permute-start | bytes 49160 | tf_op jit(solution)/shard_map/ppermute | solution.py:604
  52.9 0.3 collective-permute-start.15
  53.1 0.0 collective-permute-done.11.refs_1_
  53.1 3.3 %collective-permute-start.16 = (f32[16,256]{1,0:T(8,128)S(1)}, f32[16,256]{1,0:T(8,128)S(1)}, u32[]{:S(2)}, u32[]{:S(2)}) collective-permute-start(f32[16,256]{1,0:T(8,128)S(1)} %get-tuple-element.46), channel_id=1, source_target_pairs={{0,6},{1,7},{2,4},{3,5},{4,2},{5,3},{6,0},{7,1},{8,14},{9,15},{10,... | collective-permute-start | bytes 49160 | tf_op jit(solution)/shard_map/ppermute | solution.py:604
  56.4 0.0 collective-permute-done.12.refs_2_
  56.4 0.3 collective-permute-start.17
  56.7 0.0 collective-permute-done.13.refs_3_
  56.7 0.2 collective-permute-done.15.refs_5_
  57.0 0.8 %collective-permute-done.16.refs_6_ = f32[16,256]{1,0:T(8,128)S(1)} collective-permute-done((f32[16,256]{1,0:T(8,128)S(1)}, f32[16,256]{1,0:T(8,128)S(1)}, u32[]{:S(2)}, u32[]{:S(2)}) %collective-permute-start.16) | collective-permute-done | bytes 16416 | tf_op jit(solution)/shard_map/ppermute | solution.py:604
  57.8 3.7 %collective-permute-done.17.refs_7_ = f32[16,256]{1,0:T(8,128)S(1)} collective-permute-done((f32[16,256]{1,0:T(8,128)S(1)}, f32[16,256]{1,0:T(8,128)S(1)}, u32[]{:S(2)}, u32[]{:S(2)}) %collective-permute-start.17) | collective-permute-done | bytes 16416 | tf_op jit(solution)/shard_map/ppermute | solution.py:604
  61.4 1.2 %join.1 = f32[1,128,256]{2,1,0:T(8,128)} custom-call(s32[6]{0:T(128)S(1)} %stack.23.scal, f32[16,256]{1,0:T(8,128)S(1)} %get-tuple-element.40.refs_0_, f32[16,256]{1,0:T(8,128)S(1)} %collective-permute-done.11.refs_1_, f32[16,256]{1,0:T(8,128)S(1)} %collective-permute-done.12.refs_2_, f32[16,256]{1,0:T(8,128)S(1)} %collective-permute-done.13.refs_3_, ...), custom_call_target="tpu_custom_call" | custom-call | bytes 3500000 | tf_op jit(solution)/shard_map/join/pallas_call | solution.py:31
  62.6 0.8 %copy.10 = f32[1,1,512,256]{3,2,1,0:T(8,128)} copy(f32[1,1,512,256]{3,2,1,0:T(8,128)S(1)} %bitcast.23) | data formatting | bytes 1048576
  (15 shorter events, 0.0 us)
Async XLA Ops:
  0.6 0.7 %copy-start.3 = (s32[2,1,1,16]{3,2,1,0:T(1,128)S(1)}, s32[2,1,1,16]{3,2,1,0:T(1,128)}, u32[]{:S(2)}) copy-start(s32[2,1,1,16]{3,2,1,0:T(1,128)} %param.9) | copy-start | bytes 388
  0.6 2.0 %copy-start.4 = (s32[1,3]{1,0:T(1,128)S(1)}, s32[1,3]{1,0:T(1,128)}, u32[]{:S(2)}) copy-start(s32[1,3]{1,0:T(1,128)} %station.1) | copy-start | bytes 40
  0.7 6.4 %collective-permute-start.4 = (f32[512,256]{1,0:T(8,128)}, f32[512,256]{1,0:T(8,128)S(1)}, u32[]{:S(2)}, u32[]{:S(2)}) collective-permute-start(f32[512,256]{1,0:T(8,128)} %bitcast.19), channel_id=1, source_target_pairs={{0,1},{1,0},{2,3},{3,2},{4,5},{5,4},{6,7},{7,6},{8,9},{9,8},{10,11... | collective-permute-start | bytes 1572872 | tf_op jit(solution)/shard_map/ppermute | solution.py:507
  1.3 1.3 %collective-permute-start = (s32[2,1,16]{2,1,0:T(1,128)S(1)}, s32[2,1,16]{2,1,0:T(1,128)S(1)}, u32[]{:S(2)}, u32[]{:S(2)}) collective-permute-start(s32[2,1,16]{2,1,0:T(1,128)S(1)} %bitcast.21), channel_id=1, source_target_pairs={{0,1},{1,0},{2,3},{3,2},{4,5},{5,4},{6,7},{7,6},{8,9},{9,8},{10,11... | collective-permute-start | bytes 392 | tf_op jit(solution)/shard_map/ppermute | solution.py:507
  2.6 0.7 %copy-start.2 = (f32[1,2048]{1,0:T(1,128)S(1)}, f32[1,2048]{1,0:T(1,128)}, u32[]{:S(2)}) copy-start(f32[1,2048]{1,0:T(1,128)} %delays.1) | copy-start | bytes 24580
  3.3 5.4 %collective-permute-start.1 = (f32[1,2688]{1,0:T(1,128)S(1)}, f32[1,2688]{1,0:T(1,128)S(1)}, u32[]{:S(2)}, u32[]{:S(2)}) collective-permute-start(f32[1,2688]{1,0:T(1,128)S(1)} %head.1.refs_0_), channel_id=1, source_target_pairs={{0,8},{8,0},{16,24},{24,16},{1,9},{9,1},{17,25},{25,17},{2,10},{10... | collective-permute-start | bytes 32264 | tf_op jit(solution)/shard_map/ppermute | solution.py:501
  5.7 3.0 %collective-permute-start.2 = (f32[1,2688]{1,0:T(1,128)S(1)}, f32[1,2688]{1,0:T(1,128)S(1)}, u32[]{:S(2)}, u32[]{:S(2)}) collective-permute-start(f32[1,2688]{1,0:T(1,128)S(1)} %head.1.refs_0_), channel_id=1, source_target_pairs={{0,16},{8,24},{16,0},{24,8},{1,17},{9,25},{17,1},{25,9},{2,18},{10... | collective-permute-start | bytes 32264 | tf_op jit(solution)/shard_map/ppermute | solution.py:501
  6.9 3.4 %collective-permute-start.3 = (f32[1,2688]{1,0:T(1,128)S(1)}, f32[1,2688]{1,0:T(1,128)S(1)}, u32[]{:S(2)}, u32[]{:S(2)}) collective-permute-start(f32[1,2688]{1,0:T(1,128)S(1)} %head.1.refs_0_), channel_id=1, source_target_pairs={{0,24},{8,16},{16,8},{24,0},{1,25},{9,17},{17,9},{25,1},{2,26},{10... | collective-permute-start | bytes 32264 | tf_op jit(solution)/shard_map/ppermute | solution.py:501
  7.0 1.0 %copy-start = (f32[1,512,256]{2,1,0:T(8,128)S(1)}, f32[1,512,256]{2,1,0:T(8,128)}, u32[]{:S(2)}) copy-start(f32[1,512,256]{2,1,0:T(8,128)} %param.5) | copy-start | bytes 1572868
  10.4 7.2 %collective-permute-start.8 = (f32[16,128]{1,0:T(8,128)S(1)}, f32[16,128]{1,0:T(8,128)S(1)}, u32[]{:S(2)}, u32[]{:S(2)}) collective-permute-start(f32[16,128]{1,0:T(8,128)S(1)} %concatenate.12.refs_4_), channel_id=1, source_target_pairs={{0,2},{1,3},{2,0},{3,1},{4,6},{5,7},{6,4},{7,5},{8,10},{9,11},{10,... | collective-permute-start | bytes 24584 | tf_op jit(solution)/shard_map/ppermute | solution.py:504
  11.8 6.0 %collective-permute-start.9 = (f32[16,128]{1,0:T(8,128)S(1)}, f32[16,128]{1,0:T(8,128)S(1)}, u32[]{:S(2)}, u32[]{:S(2)}) collective-permute-start(f32[16,128]{1,0:T(8,128)S(1)} %concatenate.12.refs_4_), channel_id=1, source_target_pairs={{0,4},{1,5},{2,6},{3,7},{4,0},{5,1},{6,2},{7,3},{8,12},{9,13},{10,... | collective-permute-start | bytes 24584 | tf_op jit(solution)/shard_map/ppermute | solution.py:504
  14.1 4.3 %collective-permute-start.10 = (f32[16,128]{1,0:T(8,128)S(1)}, f32[16,128]{1,0:T(8,128)S(1)}, u32[]{:S(2)}, u32[]{:S(2)}) collective-permute-start(f32[16,128]{1,0:T(8,128)S(1)} %concatenate.12.refs_4_), channel_id=1, source_target_pairs={{0,6},{1,7},{2,4},{3,5},{4,2},{5,3},{6,0},{7,1},{8,14},{9,15},{10,... | collective-permute-start | bytes 24584 | tf_op jit(solution)/shard_map/ppermute | solution.py:504
  14.1 4.3 %collective-permute-start.5 = (f32[2,32,256]{2,1,0:T(8,128)S(1)}, f32[2,32,256]{2,1,0:T(8,128)S(1)}, u32[]{:S(2)}, u32[]{:S(2)}) collective-permute-start(f32[2,32,256]{2,1,0:T(8,128)S(1)} %get-tuple-element.31), channel_id=1, source_target_pairs={{0,2},{1,3},{2,0},{3,1},{4,6},{5,7},{6,4},{7,5},{8,10},{9,11},{10,... | collective-permute-start | bytes 196616 | tf_op jit(solution)/shard_map/ppermute | solution.py:504
  14.4 5.8 %collective-permute-start.6 = (f32[2,32,256]{2,1,0:T(8,128)S(1)}, f32[2,32,256]{2,1,0:T(8,128)S(1)}, u32[]{:S(2)}, u32[]{:S(2)}) collective-permute-start(f32[2,32,256]{2,1,0:T(8,128)S(1)} %get-tuple-element.32), channel_id=1, source_target_pairs={{0,4},{1,5},{2,6},{3,7},{4,0},{5,1},{6,2},{7,3},{8,12},{9,13},{10,... | collective-permute-start | bytes 196616 | tf_op jit(solution)/shard_map/ppermute | solution.py:504
  17.6 5.6 %collective-permute-start.7 = (f32[2,32,256]{2,1,0:T(8,128)S(1)}, f32[2,32,256]{2,1,0:T(8,128)S(1)}, u32[]{:S(2)}, u32[]{:S(2)}) collective-permute-start(f32[2,32,256]{2,1,0:T(8,128)S(1)} %get-tuple-element.33), channel_id=1, source_target_pairs={{0,6},{1,7},{2,4},{3,5},{4,2},{5,3},{6,0},{7,1},{8,14},{9,15},{10,... | collective-permute-start | bytes 196616 | tf_op jit(solution)/shard_map/ppermute | solution.py:504
  32.4 6.2 %copy-start.1 = (s32[3,2048]{1,0:T(4,128)S(1)}, s32[3,2048]{1,0:T(4,128)}, u32[]{:S(2)}) copy-start(s32[3,2048]{1,0:T(4,128)} %cells) | copy-start | bytes 73732
  32.4 30.2 %all-to-all-start = ((f32[32,16,256]{2,1,0:T(8,128)}), f32[32,16,256]{2,1,0:T(8,128)S(1)}, u32[]{:S(2)}, u32[]{:S(2)}) async-start(f32[32,16,256]{2,1,0:T(8,128)} %bitcast.13), calls=%async_computation | async-start | bytes 1048576 | tf_op jit(solution)/shard_map/all_to_all | solution.py:600
  48.2 4.9 %collective-permute-start.11 = (f32[16,256]{1,0:T(8,128)S(1)}, f32[16,256]{1,0:T(8,128)S(1)}, u32[]{:S(2)}, u32[]{:S(2)}) collective-permute-start(f32[16,256]{1,0:T(8,128)S(1)} %get-tuple-element.41), channel_id=1, source_target_pairs={{0,1},{1,0},{2,3},{3,2},{4,5},{5,4},{6,7},{7,6},{8,9},{9,8},{10,11... | collective-permute-start | bytes 49160 | tf_op jit(solution)/shard_map/ppermute | solution.py:604
  48.7 7.7 %collective-permute-start.12 = (f32[16,256]{1,0:T(8,128)S(1)}, f32[16,256]{1,0:T(8,128)S(1)}, u32[]{:S(2)}, u32[]{:S(2)}) collective-permute-start(f32[16,256]{1,0:T(8,128)S(1)} %get-tuple-element.42), channel_id=1, source_target_pairs={{0,2},{1,3},{2,0},{3,1},{4,6},{5,7},{6,4},{7,5},{8,10},{9,11},{10,... | collective-permute-start | bytes 49160 | tf_op jit(solution)/shard_map/ppermute | solution.py:604
  50.1 6.6 %collective-permute-start.13 = (f32[16,256]{1,0:T(8,128)S(1)}, f32[16,256]{1,0:T(8,128)S(1)}, u32[]{:S(2)}, u32[]{:S(2)}) collective-permute-start(f32[16,256]{1,0:T(8,128)S(1)} %get-tuple-element.43), channel_id=1, source_target_pairs={{0,3},{1,2},{2,1},{3,0},{4,7},{5,6},{6,5},{7,4},{8,11},{9,10},{10,... | collective-permute-start | bytes 49160 | tf_op jit(solution)/shard_map/ppermute | solution.py:604
  50.4 6.3 %collective-permute-start.14 = (f32[16,256]{1,0:T(8,128)S(1)}, f32[16,256]{1,0:T(8,128)S(1)}, u32[]{:S(2)}, u32[]{:S(2)}) collective-permute-start(f32[16,256]{1,0:T(8,128)S(1)} %get-tuple-element.44), channel_id=1, source_target_pairs={{0,4},{1,5},{2,6},{3,7},{4,0},{5,1},{6,2},{7,3},{8,12},{9,13},{10,... | collective-permute-start | bytes 49160 | tf_op jit(solution)/shard_map/ppermute | solution.py:604
  52.9 4.1 %collective-permute-start.15 = (f32[16,256]{1,0:T(8,128)S(1)}, f32[16,256]{1,0:T(8,128)S(1)}, u32[]{:S(2)}, u32[]{:S(2)}) collective-permute-start(f32[16,256]{1,0:T(8,128)S(1)} %get-tuple-element.45), channel_id=1, source_target_pairs={{0,5},{1,4},{2,7},{3,6},{4,1},{5,0},{6,3},{7,2},{8,13},{9,12},{10,... | collective-permute-start | bytes 49160 | tf_op jit(solution)/shard_map/ppermute | solution.py:604
  53.1 4.6 %collective-permute-start.16 = (f32[16,256]{1,0:T(8,128)S(1)}, f32[16,256]{1,0:T(8,128)S(1)}, u32[]{:S(2)}, u32[]{:S(2)}) collective-permute-start(f32[16,256]{1,0:T(8,128)S(1)} %get-tuple-element.46), channel_id=1, source_target_pairs={{0,6},{1,7},{2,4},{3,5},{4,2},{5,3},{6,0},{7,1},{8,14},{9,15},{10,... | collective-permute-start | bytes 49160 | tf_op jit(solution)/shard_map/ppermute | solution.py:604
  56.4 5.0 %collective-permute-start.17 = (f32[16,256]{1,0:T(8,128)S(1)}, f32[16,256]{1,0:T(8,128)S(1)}, u32[]{:S(2)}, u32[]{:S(2)}) collective-permute-start(f32[16,256]{1,0:T(8,128)S(1)} %get-tuple-element.47), channel_id=1, source_target_pairs={{0,7},{1,6},{2,5},{3,4},{4,3},{5,2},{6,1},{7,0},{8,15},{9,14},{10,... | collective-permute-start | bytes 49160 | tf_op jit(solution)/shard_map/ppermute | solution.py:604

commit v3 on v2

--- a/solution.py
+++ b/solution.py
@@ -13,6 +13,7 @@
 SWEEPS = 2
 ADJ_SWEEPS = 4
 BIG = 1000000.0
+LANES = 128
 
 HALO = ROUNDS * SWEEPS + ADJ_SWEEPS
 ADJ_HALO = ADJ_SWEEPS + 1
@@ -50,21 +51,30 @@
     out[:, at : at + 3] = station[...].astype(jnp.float32)
     for source in (active, active_other):
         for part in range(ROUNDS):
-            at += 128
+            at += LANES
             out[:, at : at + source.shape[-1]] = source[part].astype(jnp.float32)
 
 
-def pack_kernel(rows, own_rows, scal, own, other, *outs):
+def pack_kernel(rows, own_rows, slots, scal, own, other, *refs):
     line_row, chip, core = scal[0], scal[1], scal[2]
+    pays, outs = refs[:slots], refs[slots:]
     total = own.shape[0]
     chunk = math.gcd(own_rows, 8)
+    at = pays[0].shape[1] - 2 * ROUNDS * LANES
     for j, out in enumerate(outs):
         first = line_row + ((chip ^ j) * 2 + core) * own_rows - HALO
         for piece in range(rows // chunk):
             start = jnp.clip(first + piece * chunk, 0, total - chunk)
             start = pl.multiple_of(start, chunk)
-            out[0, piece * chunk : (piece + 1) * chunk, :] = own[pl.ds(start, chunk), :]
-            out[1, piece * chunk : (piece + 1) * chunk, :] = other[pl.ds(start, chunk), :]
+            out[piece * chunk : (piece + 1) * chunk, :] = own[pl.ds(start, chunk), :]
+            out[rows + piece * chunk : rows + (piece + 1) * chunk, :] = other[pl.ds(start, chunk), :]
+        out[2 * rows :, :] = jnp.zeros_like(out[2 * rows :, :])
+        for slot, pay in enumerate(pays):
+            for part in range(ROUNDS):
+                row = 2 * rows + slot * ROUNDS + part
+                for c in range(2):
+                    tile = at + (c * ROUNDS + part) * LANES
+                    out[row : row + 1, c * LANES : (c + 1) * LANES] = pay[:, tile : tile + LANES]
 
 
 def scatter_kernel(layers, events, scal, cells, *refs):
@@ -106,9 +116,6 @@
     count[...] = jnp.zeros_like(count)
     delay_sum[...] = jnp.zeros_like(delay_sum)
     lax.fori_loop(0, events // chunk, step, 0)
-
-
-LANES = 128
 
 
 def get(ref, row, size, *lead):
@@ -251,7 +258,6 @@
     depth = refs[0].shape[-1]
     parts = depth // LANES
     vel_in, refs = refs[:chips], refs[chips:]
-    act_in, refs = refs[:chips], refs[chips:]
     times_out, final, speed, refs = refs[0], refs[1], refs[2], refs[3:]
     cost, twice, one_half, ping, pong, acts, mask, flat = refs
     flat = Flat(flat, layers)
@@ -261,11 +267,12 @@
     for j in range(chips):
         for c in range(2):
             place = (chip ^ j) * 2 + (core ^ c)
-            flat.put_layer(place, rows, vel_in[j][c])
+            flat.put_layer(place, rows, vel_in[j][c * rows : (c + 1) * rows, :])
             for slot in range(slots):
                 for part in range(ROUNDS):
-                    acts[slot * ROUNDS + part, pl.ds(place, 1), :] = act_in[j][
-                        pl.ds((slot * 2 + c) * ROUNDS + part, 1), :
+                    row = 2 * rows + slot * ROUNDS + part
+                    acts[slot * ROUNDS + part, pl.ds(place, 1), :] = vel_in[j][
+                        row : row + 1, c * LANES : (c + 1) * LANES
                     ]
 
     def prepare(row, size):
@@ -530,26 +537,18 @@
     )
     pays = [payload] + [to_line(payload, j) for j in range(1, slots)]
 
+    height = 2 * rows + -(-slots * ROUNDS // 8) * 8
     packed = call(
-        functools.partial(pack_kernel, rows, own_rows),
+        functools.partial(pack_kernel, rows, own_rows, slots),
         "pack",
-        [out(2, rows, depth)] * chips,
-        [here, velocity[0], other],
+        [out(height, depth)] * chips,
+        [here, velocity[0], other, *pays],
     )
-    vel = [to_chip(packed[j], j) for j in range(1, chips)]
-
-    pays, cells, own_block = lax.optimization_barrier((pays, event_cells, packed[0]))
-    act = jnp.concatenate(
-        [
-            p[:, at : at + LANES]
-            for p in pays
-            for at in range(events + LANES, payload.shape[1], LANES)
-        ]
-    )
-    acts = [act] + [to_chip(act, j) for j in range(1, chips)]
+    vel = [packed[0]] + [to_chip(packed[j], j) for j in range(1, chips)]
+
+    pays, cells, _ = lax.optimization_barrier((pays, event_cells, packed[0]))
     stations = jnp.concatenate([p[0, events : events + 3] for p in pays]).astype(jnp.int32)
     scal = jnp.concatenate([here, stations])
-
     count, delay_sum = call(
         functools.partial(scatter_kernel, layers, events),
         "events",
@@ -557,6 +556,8 @@
         [here, cells, *pays],
         microseconds=4.0,
     )
+
+    scal, count, delay_sum = lax.optimization_barrier((scal, count, delay_sum))
 
     together = min(slots, 4)
     flat = scratch(depth // LANES, rows * layers, LANES)
@@ -568,7 +569,7 @@
             out(*field(slots, adj_rows)),
             out(*field(rows)),
         ],
-        [scal, own_block, *vel, *acts],
+        [scal, *vel],
         [
             scratch(*field(rows)),
             scratch(*field(rows)),

time: 64.1 us -> 56.8 us (0.89)
  waiting for transfers between devices: 13.1 us -> 9.46 us
  starting transfers between devices: 25.7 us -> 22.2 us
    ppermute x6 -> x3, waiting for transfers between devices: 5.47 us -> 1.23 us  [to_chip(): return lax.ppermute(array, 'space', [(i, i ^ 2 * j) for i in range(layers)])]
    ppermute x6 -> x3, starting transfers between devices: 7.22 us -> 3.67 us  [to_chip(): return lax.ppermute(array, 'space', [(i, i ^ 2 * j) for i in range(layers)])]
    ppermute x3, waiting for transfers between devices: 1.67 us -> 2.32 us  [to_line(): return lax.ppermute(array, 'src', [(i, i ^ j) for i in range(slots)])]
  transfers between devices with their start and end apart: 19 -> 16, of which waited for: 8 -> 8; matrix products, arithmetic and copies ran while one was open for 0% -> 0% of each run, Pallas kernels for 18% -> 19%
where the time goes in v3:
time: 56.8 us; the launch traced here: 56.2 us
  starting transfers between devices  22.2 us (39%)
  Pallas kernels  20.4 us (36%)
  waiting for transfers between devices  9.46 us (17%)
  local copies, waits for them, and re-layouts  3.25 us (6%)
  between operations  0.72 us (1%)
    pallas_call x6, Pallas kernels, call(): pl.pallas_call(body, out_shape=list(outs), in_specs=[spec(SMEM if a.ndim...  20.4 us
    ppermute x7, starting transfers between devices, per_device(): lax.ppermute(kernel[m], 'space', [(i, i ^ m) for i in range(layers)])  8.4 us
    all_to_all x1, starting transfers between devices, per_device(): lax.all_to_all(times.reshape(slots * layers, own_rows, depth), ('src', 's...  6.3 us
    ppermute x7, waiting for transfers between devices, per_device(): lax.ppermute(kernel[m], 'space', [(i, i ^ m) for i in range(layers)])  4.67 us
    ppermute x3, starting transfers between devices, to_line(): return lax.ppermute(array, 'src', [(i, i ^ j) for i in range(slots)])  3.67 us
    ppermute x3, starting transfers between devices, to_chip(): return lax.ppermute(array, 'space', [(i, i ^ 2 * j) for i in range(layers)])  3.67 us
    unnamed x11, local copies, waits for them, and re-layouts  3.08 us
    ppermute x3, waiting for transfers between devices, to_line(): return lax.ppermute(array, 'src', [(i, i ^ j) for i in range(slots)])  2.32 us
  transfers between devices with their start and end apart: 16, of which 8 were waited for; matrix products, arithmetic and copies ran while one was open for 0% of the time, Pallas kernels for 19%

profile of v3, /device:TPU:1, one launch (start us, length us, event | category | flops | bytes accessed | tf_op | source)
XLA Modules:
  0.0 56.2 jit_solution(4736748012606184382)
XLA Ops:
  0.6 0.0 copy-start.3
  0.6 0.0 copy-start.4
  0.7 0.1 collective-permute-start.4
  0.8 0.5 copy-done.3
  1.3 0.1 collective-permute-start
  1.4 1.2 %collective-permute-done.active_other = s32[2,1,16]{2,1,0:T(1,128)S(1)} collective-permute-done((s32[2,1,16]{2,1,0:T(1,128)S(1)}, s32[2,1,16]{2,1,0:T(1,128)S(1)}, u32[]{:S(2)}, u32[]{:S(2)}) %collective-permute-start) | collective-permute-done | bytes 160 | tf_op jit(solution)/shard_map/ppermute | solution.py:514
  2.6 0.0 copy-done.4
  2.6 0.7 %copy-done.2 = f32[1,2048]{1,0:T(1,128)S(1)} copy-done((f32[1,2048]{1,0:T(1,128)S(1)}, f32[1,2048]{1,0:T(1,128)}, u32[]{:S(2)}) %copy-start.2) | copy-done | bytes 8216
  3.3 3.3 %collective-permute-start.3 = (f32[1,2688]{1,0:T(1,128)S(1)}, f32[1,2688]{1,0:T(1,128)S(1)}, u32[]{:S(2)}, u32[]{:S(2)}) collective-permute-start(f32[1,2688]{1,0:T(1,128)S(1)} %head.1.refs_0_), channel_id=1, source_target_pairs={{0,24},{8,16},{16,8},{24,0},{1,25},{9,17},{17,9},{25,1},{2,26},{10... | collective-permute-start | bytes 32264 | tf_op jit(solution)/shard_map/ppermute | solution.py:508
  6.6 0.2 collective-permute-start.2
  6.9 0.1 collective-permute-start.1
  7.0 0.1 stack.23.scal
  7.1 0.6 %collective-permute-done.3.refs_3_ = f32[1,2688]{1,0:T(1,128)S(1)} collective-permute-done((f32[1,2688]{1,0:T(1,128)S(1)}, f32[1,2688]{1,0:T(1,128)S(1)}, u32[]{:S(2)}, u32[]{:S(2)}) %collective-permute-start.3) | collective-permute-done | bytes 10784 | tf_op jit(solution)/shard_map/ppermute | solution.py:508
  7.7 1.5 %collective-permute-done.2.refs_2_ = f32[1,2688]{1,0:T(1,128)S(1)} collective-permute-done((f32[1,2688]{1,0:T(1,128)S(1)}, f32[1,2688]{1,0:T(1,128)S(1)}, u32[]{:S(2)}, u32[]{:S(2)}) %collective-permute-start.2) | collective-permute-done | bytes 10784 | tf_op jit(solution)/shard_map/ppermute | solution.py:508
  9.2 0.2 collective-permute-done.1.refs_1_
  9.4 0.0 collective-permute-done.4.other
  9.4 1.0 %copy-done = f32[1,512,256]{2,1,0:T(8,128)S(1)} copy-done((f32[1,512,256]{2,1,0:T(8,128)S(1)}, f32[1,512,256]{2,1,0:T(8,128)}, u32[]{:S(2)}) %copy-start) | copy-done | bytes 524312
  10.4 0.6 %pack.1 = (f32[72,256]{1,0:T(8,128)S(1)}, f32[72,256]{1,0:T(8,128)S(1)}, f32[72,256]{1,0:T(8,128)S(1)}, f32[72,256]{1,0:T(8,128)S(1)}) custom-call(s32[6]{0:T(128)S(1)} %stack.23.scal, f32[512,256]{1,0:T(8,128)S(1)} %bitcast.20, f32[512,256]{1,0:T(8,128)S(1)} %collective-permute-done.4.other, f32[1,2688]{1,0:T(1,128)S(1)} %head.1.refs_0_, ...), custom_call_target="tpu_custom_call" | custom-call | bytes 3500000 | tf_op jit(solution)/shard_map/pack/pallas_call | solution.py:32
  11.0 1.4 %collective-permute-start.5 = (f32[72,256]{1,0:T(8,128)S(1)}, f32[72,256]{1,0:T(8,128)S(1)}, u32[]{:S(2)}, u32[]{:S(2)}) collective-permute-start(f32[72,256]{1,0:T(8,128)S(1)} %get-tuple-element.36), channel_id=1, source_target_pairs={{0,2},{1,3},{2,0},{3,1},{4,6},{5,7},{6,4},{7,5},{8,10},{9,11},{10,... | collective-permute-start | bytes 221192 | tf_op jit(solution)/shard_map/ppermute | solution.py:511
  12.4 2.3 %collective-permute-start.6 = (f32[72,256]{1,0:T(8,128)S(1)}, f32[72,256]{1,0:T(8,128)S(1)}, u32[]{:S(2)}, u32[]{:S(2)}) collective-permute-start(f32[72,256]{1,0:T(8,128)S(1)} %get-tuple-element.37), channel_id=1, source_target_pairs={{0,4},{1,5},{2,6},{3,7},{4,0},{5,1},{6,2},{7,3},{8,12},{9,13},{10,... | collective-permute-start | bytes 221192 | tf_op jit(solution)/shard_map/ppermute | solution.py:511
  14.7 0.0 collective-permute-start.7
  14.7 0.1 maximum_convert_fusion
  14.8 0.1 concatenate.8.scal
  14.9 0.0 copy-done.1
  14.9 4.4 %events.1 = (f32[208,256]{1,0:T(8,128)S(1)}, f32[4,208,256]{2,1,0:T(8,128)S(1)}) custom-call(s32[6]{0:T(128)S(1)} %stack.23.scal, s32[3,2048]{1,0:T(4,128)S(1)} %copy-done.1, f32[1,2688]{1,0:T(1,128)S(1)} %head.1.refs_0_, f32[1,2688]{1,0:T(1,128)S(1)} %collective-permute-done.1.refs_1_, f32[1,2688]{1,0:T(1,128)S(1)} %collective-permute-done.2.refs_2_, ...), custom_call_target="tpu_custom_call" | custom-call | bytes 14000000 | tf_op jit(solution)/shard_map/events/pallas_call | solution.py:32
  19.3 0.0 collective-permute-done.5.refs_1_
  19.3 0.0 collective-permute-done.6.refs_2_
  19.3 1.2 %collective-permute-done.7.refs_3_ = f32[72,256]{1,0:T(8,128)S(1)} collective-permute-done((f32[72,256]{1,0:T(8,128)S(1)}, f32[72,256]{1,0:T(8,128)S(1)}, u32[]{:S(2)}, u32[]{:S(2)}) %collective-permute-start.7) | collective-permute-done | bytes 73760 | tf_op jit(solution)/shard_map/ppermute | solution.py:511
  20.5 9.2 %sweeps.1 = (f32[4,8,16,256]{3,2,1,0:T(8,128)}, f32[4,26,8,256]{3,2,1,0:T(8,128)S(1)}, f32[32,8,256]{2,1,0:T(8,128)S(1)}) custom-call(s32[18]{0:T(128)S(1)} %concatenate.8.scal, f32[72,256]{1,0:T(8,128)S(1)} %get-tuple-element.27.refs_0_, f32[72,256]{1,0:T(8,128)S(1)} %collective-permute-done.5.refs_1_, f32[72,256]{1,0:T(8,128)S(1)} %collective-permute-done.6.refs_2_, ...), custom_call_target="tpu_custom_call" | custom-call | bytes 35000000 | tf_op jit(solution)/shard_map/sweeps/pallas_call | solution.py:32
  29.7 6.3 %all-to-all-start = ((f32[32,16,256]{2,1,0:T(8,128)}), f32[32,16,256]{2,1,0:T(8,128)S(1)}, u32[]{:S(2)}, u32[]{:S(2)}) async-start(f32[32,16,256]{2,1,0:T(8,128)} %bitcast.13), calls=%async_computation | async-start | bytes 1048576 | tf_op jit(solution)/shard_map/all_to_all | solution.py:601
  36.0 5.1 %adjoint.1 = (f32[16,256]{1,0:T(8,128)S(1)}, f32[16,256]{1,0:T(8,128)S(1)}, f32[16,256]{1,0:T(8,128)S(1)}, f32[16,256]{1,0:T(8,128)S(1)}, f32[16,256]{1,0:T(8,12...) custom-call(s32[18]{0:T(128)S(1)} %concatenate.8.scal, ...), custom_call_target="tpu_custom_call" | custom-call | bytes 24500000 | tf_op jit(solution)/shard_map/adjoint/pallas_call | solution.py:32
  41.1 0.3 collective-permute-start.8
  41.4 1.5 %collective-permute-start.9 = (f32[16,256]{1,0:T(8,128)S(1)}, f32[16,256]{1,0:T(8,128)S(1)}, u32[]{:S(2)}, u32[]{:S(2)}) collective-permute-start(f32[16,256]{1,0:T(8,128)S(1)} %get-tuple-element.46), channel_id=1, source_target_pairs={{0,2},{1,3},{2,0},{3,1},{4,6},{5,7},{6,4},{7,5},{8,10},{9,11},{10,... | collective-permute-start | bytes 49160 | tf_op jit(solution)/shard_map/ppermute | solution.py:605
  42.9 0.4 collective-permute-start.10
  43.3 2.3 %collective-permute-start.11 = (f32[16,256]{1,0:T(8,128)S(1)}, f32[16,256]{1,0:T(8,128)S(1)}, u32[]{:S(2)}, u32[]{:S(2)}) collective-permute-start(f32[16,256]{1,0:T(8,128)S(1)} %get-tuple-element.48), channel_id=1, source_target_pairs={{0,4},{1,5},{2,6},{3,7},{4,0},{5,1},{6,2},{7,3},{8,12},{9,13},{10,... | collective-permute-start | bytes 49160 | tf_op jit(solution)/shard_map/ppermute | solution.py:605
  45.6 0.3 collective-permute-start.12
  45.9 0.0 collective-permute-done.8.refs_1_
  45.9 3.3 %collective-permute-start.13 = (f32[16,256]{1,0:T(8,128)S(1)}, f32[16,256]{1,0:T(8,128)S(1)}, u32[]{:S(2)}, u32[]{:S(2)}) collective-permute-start(f32[16,256]{1,0:T(8,128)S(1)} %get-tuple-element.50), channel_id=1, source_target_pairs={{0,6},{1,7},{2,4},{3,5},{4,2},{5,3},{6,0},{7,1},{8,14},{9,15},{10,... | collective-permute-start | bytes 49160 | tf_op jit(solution)/shard_map/ppermute | solution.py:605
  49.1 0.0 collective-permute-done.9.refs_2_
  49.1 0.3 collective-permute-start.14
  49.5 0.0 collective-permute-done.10.refs_3_
  49.5 2.0 %collective-permute-done.11.refs_4_ = f32[16,256]{1,0:T(8,128)S(1)} collective-permute-done((f32[16,256]{1,0:T(8,128)S(1)}, f32[16,256]{1,0:T(8,128)S(1)}, u32[]{:S(2)}, u32[]{:S(2)}) %collective-permute-start.11) | collective-permute-done | bytes 16416 | tf_op jit(solution)/shard_map/ppermute | solution.py:605
  51.5 1.5 %collective-permute-done.12.refs_5_ = f32[16,256]{1,0:T(8,128)S(1)} collective-permute-done((f32[16,256]{1,0:T(8,128)S(1)}, f32[16,256]{1,0:T(8,128)S(1)}, u32[]{:S(2)}, u32[]{:S(2)}) %collective-permute-start.12) | collective-permute-done | bytes 16416 | tf_op jit(solution)/shard_map/ppermute | solution.py:605
  53.0 0.0 collective-permute-done.13.refs_6_
  53.0 1.2 %collective-permute-done.14.refs_7_ = f32[16,256]{1,0:T(8,128)S(1)} collective-permute-done((f32[16,256]{1,0:T(8,128)S(1)}, f32[16,256]{1,0:T(8,128)S(1)}, u32[]{:S(2)}, u32[]{:S(2)}) %collective-permute-start.14) | collective-permute-done | bytes 16416 | tf_op jit(solution)/shard_map/ppermute | solution.py:605
  54.2 1.2 %join.1 = f32[1,128,256]{2,1,0:T(8,128)} custom-call(s32[6]{0:T(128)S(1)} %stack.23.scal, f32[16,256]{1,0:T(8,128)S(1)} %get-tuple-element.44.refs_0_, f32[16,256]{1,0:T(8,128)S(1)} %collective-permute-done.8.refs_1_, f32[16,256]{1,0:T(8,128)S(1)} %collective-permute-done.9.refs_2_, f32[16,256]{1,0:T(8,128)S(1)} %collective-permute-done.10.refs_3_, ...), custom_call_target="tpu_custom_call" | custom-call | bytes 3500000 | tf_op jit(solution)/shard_map/join/pallas_call | solution.py:32
  55.4 0.0 all-to-all-done
  55.4 0.8 %copy.10 = f32[1,1,512,256]{3,2,1,0:T(8,128)} copy(f32[1,1,512,256]{3,2,1,0:T(8,128)S(1)} %bitcast.23) | data formatting | bytes 1048576
  (6 shorter events, 0.0 us)
Async XLA Ops:
  0.6 0.7 %copy-start.3 = (s32[2,1,1,16]{3,2,1,0:T(1,128)S(1)}, s32[2,1,1,16]{3,2,1,0:T(1,128)}, u32[]{:S(2)}) copy-start(s32[2,1,1,16]{3,2,1,0:T(1,128)} %param.9) | copy-start | bytes 388
  0.6 2.0 %copy-start.4 = (s32[1,3]{1,0:T(1,128)S(1)}, s32[1,3]{1,0:T(1,128)}, u32[]{:S(2)}) copy-start(s32[1,3]{1,0:T(1,128)} %station.1) | copy-start | bytes 40
  0.7 8.7 %collective-permute-start.4 = (f32[512,256]{1,0:T(8,128)}, f32[512,256]{1,0:T(8,128)S(1)}, u32[]{:S(2)}, u32[]{:S(2)}) collective-permute-start(f32[512,256]{1,0:T(8,128)} %bitcast.19), channel_id=1, source_target_pairs={{0,1},{1,0},{2,3},{3,2},{4,5},{5,4},{6,7},{7,6},{8,9},{9,8},{10,11... | collective-permute-start | bytes 1572872 | tf_op jit(solution)/shard_map/ppermute | solution.py:514
  1.3 1.3 %collective-permute-start = (s32[2,1,16]{2,1,0:T(1,128)S(1)}, s32[2,1,16]{2,1,0:T(1,128)S(1)}, u32[]{:S(2)}, u32[]{:S(2)}) collective-permute-start(s32[2,1,16]{2,1,0:T(1,128)S(1)} %bitcast.21), channel_id=1, source_target_pairs={{0,1},{1,0},{2,3},{3,2},{4,5},{5,4},{6,7},{7,6},{8,9},{9,8},{10,11... | collective-permute-start | bytes 392 | tf_op jit(solution)/shard_map/ppermute | solution.py:514
  2.6 0.7 %copy-start.2 = (f32[1,2048]{1,0:T(1,128)S(1)}, f32[1,2048]{1,0:T(1,128)}, u32[]{:S(2)}) copy-start(f32[1,2048]{1,0:T(1,128)} %delays.1) | copy-start | bytes 24580
  3.3 4.4 %collective-permute-start.3 = (f32[1,2688]{1,0:T(1,128)S(1)}, f32[1,2688]{1,0:T(1,128)S(1)}, u32[]{:S(2)}, u32[]{:S(2)}) collective-permute-start(f32[1,2688]{1,0:T(1,128)S(1)} %head.1.refs_0_), channel_id=1, source_target_pairs={{0,24},{8,16},{16,8},{24,0},{1,25},{9,17},{17,9},{25,1},{2,26},{10... | collective-permute-start | bytes 32264 | tf_op jit(solution)/shard_map/ppermute | solution.py:508
  6.6 2.5 %collective-permute-start.2 = (f32[1,2688]{1,0:T(1,128)S(1)}, f32[1,2688]{1,0:T(1,128)S(1)}, u32[]{:S(2)}, u32[]{:S(2)}) collective-permute-start(f32[1,2688]{1,0:T(1,128)S(1)} %head.1.refs_0_), channel_id=1, source_target_pairs={{0,16},{8,24},{16,0},{24,8},{1,17},{9,25},{17,1},{25,9},{2,18},{10... | collective-permute-start | bytes 32264 | tf_op jit(solution)/shard_map/ppermute | solution.py:508
  6.9 2.5 %collective-permute-start.1 = (f32[1,2688]{1,0:T(1,128)S(1)}, f32[1,2688]{1,0:T(1,128)S(1)}, u32[]{:S(2)}, u32[]{:S(2)}) collective-permute-start(f32[1,2688]{1,0:T(1,128)S(1)} %head.1.refs_0_), channel_id=1, source_target_pairs={{0,8},{8,0},{16,24},{24,16},{1,9},{9,1},{17,25},{25,17},{2,10},{10... | collective-permute-start | bytes 32264 | tf_op jit(solution)/shard_map/ppermute | solution.py:508
  9.4 1.0 %copy-start = (f32[1,512,256]{2,1,0:T(8,128)S(1)}, f32[1,512,256]{2,1,0:T(8,128)}, u32[]{:S(2)}) copy-start(f32[1,512,256]{2,1,0:T(8,128)} %param.5) | copy-start | bytes 1572868
  10.4 4.5 %copy-start.1 = (s32[3,2048]{1,0:T(4,128)S(1)}, s32[3,2048]{1,0:T(4,128)}, u32[]{:S(2)}) copy-start(s32[3,2048]{1,0:T(4,128)} %cells) | copy-start | bytes 73732
  11.0 8.2 %collective-permute-start.5 = (f32[72,256]{1,0:T(8,128)S(1)}, f32[72,256]{1,0:T(8,128)S(1)}, u32[]{:S(2)}, u32[]{:S(2)}) collective-permute-start(f32[72,256]{1,0:T(8,128)S(1)} %get-tuple-element.36), channel_id=1, source_target_pairs={{0,2},{1,3},{2,0},{3,1},{4,6},{5,7},{6,4},{7,5},{8,10},{9,11},{10,... | collective-permute-start | bytes 221192 | tf_op jit(solution)/shard_map/ppermute | solution.py:511
  12.4 6.9 %collective-permute-start.6 = (f32[72,256]{1,0:T(8,128)S(1)}, f32[72,256]{1,0:T(8,128)S(1)}, u32[]{:S(2)}, u32[]{:S(2)}) collective-permute-start(f32[72,256]{1,0:T(8,128)S(1)} %get-tuple-element.37), channel_id=1, source_target_pairs={{0,4},{1,5},{2,6},{3,7},{4,0},{5,1},{6,2},{7,3},{8,12},{9,13},{10,... | collective-permute-start | bytes 221192 | tf_op jit(solution)/shard_map/ppermute | solution.py:511
  14.7 5.8 %collective-permute-start.7 = (f32[72,256]{1,0:T(8,128)S(1)}, f32[72,256]{1,0:T(8,128)S(1)}, u32[]{:S(2)}, u32[]{:S(2)}) collective-permute-start(f32[72,256]{1,0:T(8,128)S(1)} %get-tuple-element.38), channel_id=1, source_target_pairs={{0,6},{1,7},{2,4},{3,5},{4,2},{5,3},{6,0},{7,1},{8,14},{9,15},{10,... | collective-permute-start | bytes 221192 | tf_op jit(solution)/shard_map/ppermute | solution.py:511
  29.7 25.7 %all-to-all-start = ((f32[32,16,256]{2,1,0:T(8,128)}), f32[32,16,256]{2,1,0:T(8,128)S(1)}, u32[]{:S(2)}, u32[]{:S(2)}) async-start(f32[32,16,256]{2,1,0:T(8,128)} %bitcast.13), calls=%async_computation | async-start | bytes 1048576 | tf_op jit(solution)/shard_map/all_to_all | solution.py:601
  41.1 4.8 %collective-permute-start.8 = (f32[16,256]{1,0:T(8,128)S(1)}, f32[16,256]{1,0:T(8,128)S(1)}, u32[]{:S(2)}, u32[]{:S(2)}) collective-permute-start(f32[16,256]{1,0:T(8,128)S(1)} %get-tuple-element.45), channel_id=1, source_target_pairs={{0,1},{1,0},{2,3},{3,2},{4,5},{5,4},{6,7},{7,6},{8,9},{9,8},{10,11... | collective-permute-start | bytes 49160 | tf_op jit(solution)/shard_map/ppermute | solution.py:605
  41.4 7.7 %collective-permute-start.9 = (f32[16,256]{1,0:T(8,128)S(1)}, f32[16,256]{1,0:T(8,128)S(1)}, u32[]{:S(2)}, u32[]{:S(2)}) collective-permute-start(f32[16,256]{1,0:T(8,128)S(1)} %get-tuple-element.46), channel_id=1, source_target_pairs={{0,2},{1,3},{2,0},{3,1},{4,6},{5,7},{6,4},{7,5},{8,10},{9,11},{10,... | collective-permute-start | bytes 49160 | tf_op jit(solution)/shard_map/ppermute | solution.py:605
  42.9 6.6 %collective-permute-start.10 = (f32[16,256]{1,0:T(8,128)S(1)}, f32[16,256]{1,0:T(8,128)S(1)}, u32[]{:S(2)}, u32[]{:S(2)}) collective-permute-start(f32[16,256]{1,0:T(8,128)S(1)} %get-tuple-element.47), channel_id=1, source_target_pairs={{0,3},{1,2},{2,1},{3,0},{4,7},{5,6},{6,5},{7,4},{8,11},{9,10},{10,... | collective-permute-start | bytes 49160 | tf_op jit(solution)/shard_map/ppermute | solution.py:605
  43.3 8.2 %collective-permute-start.11 = (f32[16,256]{1,0:T(8,128)S(1)}, f32[16,256]{1,0:T(8,128)S(1)}, u32[]{:S(2)}, u32[]{:S(2)}) collective-permute-start(f32[16,256]{1,0:T(8,128)S(1)} %get-tuple-element.48), channel_id=1, source_target_pairs={{0,4},{1,5},{2,6},{3,7},{4,0},{5,1},{6,2},{7,3},{8,12},{9,13},{10,... | collective-permute-start | bytes 49160 | tf_op jit(solution)/shard_map/ppermute | solution.py:605
  45.6 7.4 %collective-permute-start.12 = (f32[16,256]{1,0:T(8,128)S(1)}, f32[16,256]{1,0:T(8,128)S(1)}, u32[]{:S(2)}, u32[]{:S(2)}) collective-permute-start(f32[16,256]{1,0:T(8,128)S(1)} %get-tuple-element.49), channel_id=1, source_target_pairs={{0,5},{1,4},{2,7},{3,6},{4,1},{5,0},{6,3},{7,2},{8,13},{9,12},{10,... | collective-permute-start | bytes 49160 | tf_op jit(solution)/shard_map/ppermute | solution.py:605
  45.9 7.1 %collective-permute-start.13 = (f32[16,256]{1,0:T(8,128)S(1)}, f32[16,256]{1,0:T(8,128)S(1)}, u32[]{:S(2)}, u32[]{:S(2)}) collective-permute-start(f32[16,256]{1,0:T(8,128)S(1)} %get-tuple-element.50), channel_id=1, source_target_pairs={{0,6},{1,7},{2,4},{3,5},{4,2},{5,3},{6,0},{7,1},{8,14},{9,15},{10,... | collective-permute-start | bytes 49160 | tf_op jit(solution)/shard_map/ppermute | solution.py:605
  49.1 5.0 %collective-permute-start.14 = (f32[16,256]{1,0:T(8,128)S(1)}, f32[16,256]{1,0:T(8,128)S(1)}, u32[]{:S(2)}, u32[]{:S(2)}) collective-permute-start(f32[16,256]{1,0:T(8,128)S(1)} %get-tuple-element.51), channel_id=1, source_target_pairs={{0,7},{1,6},{2,5},{3,4},{4,3},{5,2},{6,1},{7,0},{8,15},{9,14},{10,... | collective-permute-start | bytes 49160 | tf_op jit(solution)/shard_map/ppermute | solution.py:605

commit v4 on v3

--- a/solution.py
+++ b/solution.py
@@ -26,26 +26,39 @@
     return pl.BlockSpec(memory_space=space)
 
 
-def call(body, name, outs, operands, scratch=(), microseconds=1.0):
-    held = [*operands, *outs, *scratch]
+def call(body, name, outs, operands, scratch=(), microseconds=1.0, in_place=(), hbm_in=(), hbm_out=()):
+    held = [a for a in (*operands, *outs, *scratch) if len(a.shape) > 1]
     limit = 4 * 2**20 + sum(4 * math.prod((*a.shape[:-2], -(-math.prod(a.shape[-2:-1]) // 8) * 8, max(a.shape[-1], 128))) for a in held)
     return pl.pallas_call(
         body,
         out_shape=list(outs),
-        in_specs=[spec(SMEM if a.ndim == 1 else VMEM) for a in operands],
-        out_specs=[spec(VMEM)] * len(outs),
+        in_specs=[
+            spec(
+                pltpu.HBM if i in hbm_in else pl.ANY if i in in_place else SMEM if a.ndim == 1 else VMEM
+            )
+            for i, a in enumerate(operands)
+        ],
+        out_specs=[spec(pltpu.HBM if i in hbm_out else VMEM) for i in range(len(outs))],
         scratch_shapes=list(scratch),
         compiler_params=pltpu.CompilerParams(vmem_limit_bytes=limit),
         cost_estimate=pl.CostEstimate(
             flops=0, bytes_accessed=int(microseconds * 3.5e6), transcendentals=0
         ),
         name=name,
-    )(*operands)
-
-
-def head_kernel(delays, station, active, active_other, out):
+    )(*[
+        pltpu.with_memory_space_constraint(a, pltpu.HBM) if i in hbm_in else a
+        for i, a in enumerate(operands)
+    ])
+
+
+def head_kernel(delays, velocity, station, active, active_other, out, layer, sems):
     events = delays.shape[1]
-    out[:, :events] = delays[...]
+    copies = [
+        pltpu.make_async_copy(delays, out.at[:, pl.ds(0, events)], sems.at[0]),
+        pltpu.make_async_copy(velocity, layer, sems.at[1]),
+    ]
+    for copy in copies:
+        copy.start()
     out[:, events:] = jnp.zeros((1, out.shape[1] - events), jnp.float32)
     at = events
     out[:, at : at + 3] = station[...].astype(jnp.float32)
@@ -53,6 +66,8 @@
         for part in range(ROUNDS):
             at += LANES
             out[:, at : at + source.shape[-1]] = source[part].astype(jnp.float32)
+    for copy in copies:
+        copy.wait()
 
 
 def pack_kernel(rows, own_rows, slots, scal, own, other, *refs):
@@ -77,14 +92,16 @@
                     out[row : row + 1, c * LANES : (c + 1) * LANES] = pay[:, tile : tile + LANES]
 
 
+EVENT_CHUNK = 2048
+
+
 def scatter_kernel(layers, events, scal, cells, *refs):
-    slots = len(refs) - 2
-    pays, count, delay_sum = refs[:slots], refs[slots], refs[slots + 1]
+    slots = len(refs) - 3
+    pays, count, delay_sum, left = refs[:slots], refs[slots], refs[slots + 1], refs[slots + 2]
     first_row = scal[3] + HALO - ADJ_HALO
     height, width = count.shape
-    chunk = min(events, 512)
-    cells_iota = lax.broadcasted_iota(jnp.int32, (height, chunk), 0)
-    depth_iota = lax.broadcasted_iota(jnp.int32, (width, chunk), 0)
+    chunk = left.shape[1]
+    steps = events // chunk
     contract = (((1,), (1,)), ((), ()))
 
     def step(index, carry):
@@ -93,29 +110,37 @@
         where_y = cells[1:2, pl.ds(start, chunk)] - first_row
         where_z = cells[2:3, pl.ds(start, chunk)]
         at = jnp.where(where_y >= 0, where_y * layers + where_x, -1)
-        hit = (cells_iota == at).astype(jnp.bfloat16)
-        depth = (depth_iota == where_z).astype(jnp.bfloat16)
-
-        def add(ref_index, value):
-            if ref_index is None:
-                count[...] += value
-            else:
-                delay_sum[ref_index] += value
-
-        def dot(left):
-            return lax.dot_general(left, depth, contract, preferred_element_type=jnp.float32)
-
-        add(None, dot(hit))
+        hit = lax.broadcasted_iota(jnp.int32, (height, chunk), 0) == at
+        hit = hit.astype(jnp.bfloat16)
+        left[:height, :] = hit
         for slot in range(slots):
             delay = pays[slot][:, pl.ds(start, chunk)]
             high = delay.astype(jnp.bfloat16)
             low = (delay - high.astype(jnp.float32)).astype(jnp.bfloat16)
-            add(slot, dot(hit * high) + dot(hit * low))
+            for half, factor in enumerate((high, low)):
+                row = (1 + 2 * slot + half) * height
+                left[row : row + height, :] = hit * factor
+        depth = lax.broadcasted_iota(jnp.int32, (width, chunk), 0) == where_z
+        depth = depth.astype(jnp.bfloat16)
+        value = lax.dot_general(left[...], depth, contract, preferred_element_type=jnp.float32)
+        pieces = [value[i * height : (i + 1) * height] for i in range(1 + 2 * slots)]
+        sums = [pieces[1 + 2 * slot] + pieces[2 + 2 * slot] for slot in range(slots)]
+        if steps == 1:
+            count[...] = pieces[0]
+            for slot in range(slots):
+                delay_sum[slot] = sums[slot]
+        else:
+            count[...] += pieces[0]
+            for slot in range(slots):
+                delay_sum[slot] += sums[slot]
         return carry
 
-    count[...] = jnp.zeros_like(count)
-    delay_sum[...] = jnp.zeros_like(delay_sum)
-    lax.fori_loop(0, events // chunk, step, 0)
+    if steps == 1:
+        step(0, 0)
+    else:
+        count[...] = jnp.zeros_like(count)
+        delay_sum[...] = jnp.zeros_like(delay_sum)
+        lax.fori_loop(0, steps, step, 0)
 
 
 def get(ref, row, size, *lead):
@@ -222,14 +247,22 @@
     return value * lax.rsqrt(value)
 
 
-def distance(layers, at, y, grid_rows, size, row, piece):
-    shape = (size, layers, LANES)
-    dx = (lax.broadcasted_iota(jnp.int32, shape, 1) - at[0]).astype(jnp.float32)
-    dz = (lax.broadcasted_iota(jnp.int32, shape, 2) + (piece * LANES - at[2])).astype(jnp.float32)
-    here = lax.broadcasted_iota(jnp.int32, shape, 0) + (y + row)
-    dy = (here - at[1]).astype(jnp.float32)
-    far = jnp.sqrt(dx * dx + dy * dy + dz * dz)
-    return jnp.where((here >= 0) & (here < grid_rows), far, BIG)
+class Straight:
+    def __init__(self, layers, parts, at, grid_rows):
+        shape = (1, layers, LANES)
+        self.at_y, self.grid_rows = at[1], grid_rows
+        dx = (lax.broadcasted_iota(jnp.int32, shape, 1) - at[0]).astype(jnp.float32)
+        self.across = []
+        for p in range(parts):
+            dz = lax.broadcasted_iota(jnp.int32, shape, 2) + (p * LANES - at[2])
+            dz = dz.astype(jnp.float32)
+            self.across.append(dx * dx + dz * dz)
+
+    def row(self, y):
+        gap = y - self.at_y
+        far = (gap * gap).astype(jnp.float32)
+        inside = (y >= 0) & (y < self.grid_rows)
+        return [jnp.where(inside, root_of(a + far), BIG) for a in self.across]
 
 
 def local_solve(near_x, near_y, near_z, cost, twice, one_half):
@@ -285,15 +318,14 @@
 
     loop(0, rows, 4, prepare)
 
+    straight = [Straight(layers, parts, stations[slot], grid_rows) for slot in range(slots)]
+
     def fill(row, size):
-        for slot in range(slots):
-            value = [
-                distance(layers, stations[slot], y_first - 1, grid_rows, size, row, piece)
-                for piece in range(parts)
-            ]
-            put(ping, row, size, value, slot)
-
-    loop(0, rows + 2, 2, fill)
+        for i in range(size):
+            for slot in range(slots):
+                put(ping, row + i, 1, straight[slot].row(y_first - 1 + row + i), slot)
+
+    loop(0, rows + 2, 4, fill)
 
     lane_iota = lax.broadcasted_iota(jnp.int32, (layers, LANES), 1)
     tile_first = (y_first + TY) // TY - 1
@@ -377,6 +409,7 @@
     flat = Flat(flat, layers)
     y_first, grid_rows = scal[3], scal[5]
     stations = [[scal[6 + 3 * slot + i] for i in range(3)] for slot in range(slots)]
+    straight = [Straight(layers, parts, stations[slot], grid_rows) for slot in range(slots)]
     shift = HALO - ADJ_HALO
     rows = own_rows + 2 * ADJ_HALO
 
@@ -388,20 +421,17 @@
         ]
 
     def make_source(group, row, size):
-        number = sums(count, row, size)
-        for slot in group:
-            straight = [
-                distance(layers, stations[slot], y_first + shift, grid_rows, size, row, piece)
-                for piece in range(parts)
-            ]
-            value = each(
-                lambda n, t, d, s: n * (t - d) - s,
-                number,
-                get(final, row, size, slot),
-                straight,
-                sums(delay_sum, row, size, slot),
-            )
-            put(src, row, size, value, slot - group[0])
+        for i in range(size):
+            number = sums(count, row + i, 1)
+            for slot in group:
+                value = each(
+                    lambda n, t, d, s: n * (t - d) - s,
+                    number,
+                    get(final, row + i, 1, slot),
+                    straight[slot].row(y_first + shift + row + i),
+                    sums(delay_sum, row + i, 1, slot),
+                )
+                put(src, row + i, 1, value, slot - group[0])
 
     def make_weight(group, row, size):
         grid = Grid(size, layers, depth)
@@ -467,7 +497,7 @@
 
     for first in range(0, slots, together):
         group = range(first, min(first + together, slots))
-        loop(0, rows, 2, functools.partial(make_source, group))
+        loop(0, rows, 4, functools.partial(make_source, group))
         loop(1, rows - 1, 2, functools.partial(make_weight, group))
         fields = [src] + [(adj_a, adj_b)[i % 2] for i in range(ADJ_SWEEPS - 1)] + [None]
         for index in range(ADJ_SWEEPS):
@@ -485,11 +515,17 @@
         out[...] = flat.get_layer(scal[1] * 2 + scal[2] ^ m, own_rows)
 
 
-def join_kernel(scal, *refs):
-    blocks, out = refs[:-1], refs[-1]
+def join_kernel(scal, times, *refs):
+    blocks, (times_out, out, sems) = refs[:-3], refs[-3:]
     rows = blocks[0].shape[0]
+    copies = [pltpu.make_async_copy(times, times_out, sems.at[0])]
     for m, block in enumerate(blocks):
-        out[0, pl.ds(pl.multiple_of(((scal[1] * 2 + scal[2]) ^ m) * rows, rows), rows), :] = block[...]
+        start = pl.multiple_of(((scal[1] * 2 + scal[2]) ^ m) * rows, rows)
+        copies.append(pltpu.make_async_copy(block, out.at[pl.ds(start, rows)], sems.at[m + 1]))
+    for copy in copies:
+        copy.start()
+    for copy in copies:
+        copy.wait()
 
 
 def per_device(velocity, station_cells, event_cells, delays, active):
@@ -529,11 +565,13 @@
 
     other = to_core(velocity[0])
     active_other = to_core(active[:, 0])
-    (payload,) = call(
+    payload, layer = call(
         head_kernel,
         "head",
-        [out(1, events + LANES * (1 + 2 * ROUNDS))],
-        [delays, station_cells, active[:, 0], active_other],
+        [out(1, events + LANES * (1 + 2 * ROUNDS)), out(grid_rows, depth)],
+        [delays, velocity[0], station_cells, active[:, 0], active_other],
+        [pltpu.SemaphoreType.DMA((2,))],
+        hbm_in=(0, 1),
     )
     pays = [payload] + [to_line(payload, j) for j in range(1, slots)]
 
@@ -542,19 +580,23 @@
         functools.partial(pack_kernel, rows, own_rows, slots),
         "pack",
         [out(height, depth)] * chips,
-        [here, velocity[0], other, *pays],
+        [here, layer, other, *pays],
     )
     vel = [packed[0]] + [to_chip(packed[j], j) for j in range(1, chips)]
 
     pays, cells, _ = lax.optimization_barrier((pays, event_cells, packed[0]))
     stations = jnp.concatenate([p[0, events : events + 3] for p in pays]).astype(jnp.int32)
     scal = jnp.concatenate([here, stations])
+    chunk = events
+    while (1 + 2 * slots) * adj_rows * layers * chunk > EVENT_CHUNK * 2**11:
+        chunk //= 2
     count, delay_sum = call(
         functools.partial(scatter_kernel, layers, events),
         "events",
         [out(adj_rows * layers, depth), out(slots, adj_rows * layers, depth)],
         [here, cells, *pays],
-        microseconds=4.0,
+        [pltpu.VMEM(((1 + 2 * slots) * adj_rows * layers, chunk), jnp.bfloat16)],
+        microseconds=3.0,
     )
 
     scal, count, delay_sum = lax.optimization_barrier((scal, count, delay_sum))
@@ -605,8 +647,16 @@
         lax.ppermute(kernel[m], "space", [(i, i ^ m) for i in range(layers)])
         for m in range(1, layers)
     ]
-    (kernel,) = call(join_kernel, "join", [out(1, line_rows, depth)], [here, *blocks])
-    return (times.reshape(1, 1, grid_rows, depth), kernel)
+    times, kernel = call(
+        join_kernel,
+        "join",
+        [out(grid_rows, depth), out(line_rows, depth)],
+        [here, times.reshape(grid_rows, depth), *blocks],
+        [pltpu.SemaphoreType.DMA((1 + layers,))],
+        in_place=range(1, 2 + layers),
+        hbm_out=(0, 1),
+    )
+    return (times.reshape(1, 1, grid_rows, depth), kernel.reshape(1, line_rows, depth))
 
 
 def solution(mesh):

time: 56.8 us -> 54.2 us (0.954)
  local copies, waits for them, and re-layouts: 3.25 us -> 0.72 us
  waiting for transfers between devices: 9.46 us -> 11 us
  starting transfers between devices: 22.2 us -> 21.3 us
  Pallas kernels: 20.4 us -> 19.6 us
    unnamed x11 -> x6, local copies, waits for them, and re-layouts: 3.08 us -> 0.55 us
    ppermute x3, waiting for transfers between devices: 1.23 us -> 2.76 us  [to_chip(): return lax.ppermute(array, 'space', [(i, i ^ 2 * j) for i in range(layers)])]
    all_to_all x1, starting transfers between devices: 6.3 us -> 5.35 us  [per_device(): lax.all_to_all(times.reshape(slots * layers, own_rows, depth), ('src', 's...]
    pallas_call x6, Pallas kernels: 20.4 us -> 19.6 us  [call(): pl.pallas_call(body, out_shape=list(outs), in_specs=[spec(pltpu.HBM if i...]
  transfers between devices with their start and end apart: 16 -> 16, of which waited for: 8 -> 8; matrix products, arithmetic and copies ran while one was open for 0% -> 0% of each run, Pallas kernels for 19% -> 16%
where the time goes in v4:
time: 54.2 us; the launch traced here: 53.5 us
  starting transfers between devices  21.3 us (39%)
  Pallas kernels  19.6 us (36%)
  waiting for transfers between devices  11 us (20%)
  local copies, waits for them, and re-layouts  0.72 us (1%)
  between operations  0.72 us (1%)
    pallas_call x6, Pallas kernels, call(): pl.pallas_call(body, out_shape=list(outs), in_specs=[spec(pltpu.HBM if i...  19.6 us
    ppermute x7, starting transfers between devices, per_device(): lax.ppermute(kernel[m], 'space', [(i, i ^ m) for i in range(layers)])  8.4 us
    all_to_all x1, starting transfers between devices, per_device(): lax.all_to_all(times.reshape(slots * layers, own_rows, depth), ('src', 's...  5.35 us
    ppermute x7, waiting for transfers between devices, per_device(): lax.ppermute(kernel[m], 'space', [(i, i ^ m) for i in range(layers)])  4.67 us
    ppermute x3, starting transfers between devices, to_line(): return lax.ppermute(array, 'src', [(i, i ^ j) for i in range(slots)])  3.75 us
    ppermute x3, starting transfers between devices, to_chip(): return lax.ppermute(array, 'space', [(i, i ^ 2 * j) for i in range(layers)])  3.67 us
    ppermute x3, waiting for transfers between devices, to_chip(): return lax.ppermute(array, 'space', [(i, i ^ 2 * j) for i in range(layers)])  2.76 us
    ppermute x3, waiting for transfers between devices, to_line(): return lax.ppermute(array, 'src', [(i, i ^ j) for i in range(slots)])  2.31 us
  transfers between devices with their start and end apart: 16, of which 8 were waited for; matrix products, arithmetic and copies ran while one was open for 0% of the time, Pallas kernels for 16%

profile of v4, /device:TPU:1, one launch (start us, length us, event | category | flops | bytes accessed | tf_op | source)
XLA Modules:
  0.0 53.5 jit_solution(13636851681858516349)
XLA Ops:
  0.6 0.0 copy-start.1
  0.6 0.0 copy-start.2
  0.7 0.1 collective-permute-start.4
  0.8 0.5 %copy-done.1 = s32[2,1,1,16]{3,2,1,0:T(1,128)S(1)} copy-done((s32[2,1,1,16]{3,2,1,0:T(1,128)S(1)}, s32[2,1,1,16]{3,2,1,0:T(1,128)}, u32[]{:S(2)}) %copy-start.1) | copy-done | bytes 152
  1.3 0.1 collective-permute-start
  1.4 1.2 %collective-permute-done.active_other = s32[2,1,16]{2,1,0:T(1,128)S(1)} collective-permute-done((s32[2,1,16]{2,1,0:T(1,128)S(1)}, s32[2,1,16]{2,1,0:T(1,128)S(1)}, u32[]{:S(2)}, u32[]{:S(2)}) %collective-permute-start) | collective-permute-done | bytes 160 | tf_op jit(solution)/shard_map/ppermute | solution.py:550
  2.6 0.0 copy-done.2
  2.6 1.1 %head.1 = (f32[1,2688]{1,0:T(1,128)S(1)}, f32[512,256]{1,0:T(8,128)S(1)}) custom-call(f32[1,2048]{1,0:T(1,128)} %delays.1, f32[512,256]{1,0:T(8,128)} %bitcast.25, s32[1,3]{1,0:T(1,128)S(1)} %copy-done.2, s32[2,1,16]{2,1,0:T(1,128)S(1)} %bitcast.23, s32[2,1,16]{2,1,0:T(1,128)S(1)} %collective-permute-done.active_other), custom_call_target="tpu_custom_call" | custom-call | bytes 3500000 | tf_op jit(solution)/shard_map/head/pallas_call | solution.py:32
  3.7 3.4 %collective-permute-start.3 = (f32[1,2688]{1,0:T(1,128)S(1)}, f32[1,2688]{1,0:T(1,128)S(1)}, u32[]{:S(2)}, u32[]{:S(2)}) collective-permute-start(f32[1,2688]{1,0:T(1,128)S(1)} %get-tuple-element.34.refs_0_), channel_id=1, source_target_pairs={{0,24},{8,16},{16,8},{24,0},{1,25},{9,17},{17,9},{25,1},{2,26},{10... | collective-permute-start | bytes 32264 | tf_op jit(solution)/shard_map/ppermute | solution.py:544
  7.1 0.2 collective-permute-start.2
  7.3 0.1 collective-permute-start.1
  7.4 0.1 stack.23.scal
  7.5 0.6 %collective-permute-done.3.refs_3_ = f32[1,2688]{1,0:T(1,128)S(1)} collective-permute-done((f32[1,2688]{1,0:T(1,128)S(1)}, f32[1,2688]{1,0:T(1,128)S(1)}, u32[]{:S(2)}, u32[]{:S(2)}) %collective-permute-start.3) | collective-permute-done | bytes 10784 | tf_op jit(solution)/shard_map/ppermute | solution.py:544
  8.1 1.5 %collective-permute-done.2.refs_2_ = f32[1,2688]{1,0:T(1,128)S(1)} collective-permute-done((f32[1,2688]{1,0:T(1,128)S(1)}, f32[1,2688]{1,0:T(1,128)S(1)}, u32[]{:S(2)}, u32[]{:S(2)}) %collective-permute-start.2) | collective-permute-done | bytes 10784 | tf_op jit(solution)/shard_map/ppermute | solution.py:544
  9.6 0.2 collective-permute-done.1.refs_1_
  9.8 0.0 collective-permute-done.4.other
  9.8 0.0 copy-start
  9.8 0.6 %pack.1 = (f32[72,256]{1,0:T(8,128)S(1)}, f32[72,256]{1,0:T(8,128)S(1)}, f32[72,256]{1,0:T(8,128)S(1)}, f32[72,256]{1,0:T(8,128)S(1)}) custom-call(s32[6]{0:T(128)S(1)} %stack.23.scal, f32[512,256]{1,0:T(8,128)S(1)} %get-tuple-element.32.own, f32[512,256]{1,0:T(8,128)S(1)} %collective-permute-done.4.other, f32[1,2688]{1,0:T(1,128)S(1)} %get-tuple-element.34.refs_0_, ...), custom_call_target="tpu_custom_call" | custom-call | bytes 3500000 | tf_op jit(solution)/shard_map/pack/pallas_call | solution.py:32
  10.4 1.4 %collective-permute-start.5 = (f32[72,256]{1,0:T(8,128)S(1)}, f32[72,256]{1,0:T(8,128)S(1)}, u32[]{:S(2)}, u32[]{:S(2)}) collective-permute-start(f32[72,256]{1,0:T(8,128)S(1)} %get-tuple-element.42), channel_id=1, source_target_pairs={{0,2},{1,3},{2,0},{3,1},{4,6},{5,7},{6,4},{7,5},{8,10},{9,11},{10,... | collective-permute-start | bytes 221192 | tf_op jit(solution)/shard_map/ppermute | solution.py:547
  11.8 2.3 %collective-permute-start.6 = (f32[72,256]{1,0:T(8,128)S(1)}, f32[72,256]{1,0:T(8,128)S(1)}, u32[]{:S(2)}, u32[]{:S(2)}) collective-permute-start(f32[72,256]{1,0:T(8,128)S(1)} %get-tuple-element.43), channel_id=1, source_target_pairs={{0,4},{1,5},{2,6},{3,7},{4,0},{5,1},{6,2},{7,3},{8,12},{9,13},{10,... | collective-permute-start | bytes 221192 | tf_op jit(solution)/shard_map/ppermute | solution.py:547
  14.1 0.0 collective-permute-start.7
  14.1 0.1 maximum_convert_fusion
  14.2 0.1 concatenate.8.scal
  14.3 0.0 copy-done
  14.3 2.9 %events.1 = (f32[208,256]{1,0:T(8,128)S(1)}, f32[4,208,256]{2,1,0:T(8,128)S(1)}) custom-call(s32[6]{0:T(128)S(1)} %stack.23.scal, s32[3,2048]{1,0:T(4,128)S(1)} %copy-done, f32[1,2688]{1,0:T(1,128)S(1)} %get-tuple-element.34.refs_0_, f32[1,2688]{1,0:T(1,128)S(1)} %collective-permute-done.1.refs_1_, f32[1,2688]{1,0:T(1,128)S(1)} %collective-permute-done.2.refs_2_, ...), custom_call_target="tpu_custom_call" | custom-call | bytes 10500000 | tf_op jit(solution)/shard_map/events/pallas_call | solution.py:32
  17.2 0.0 collective-permute-done.5.refs_1_
  17.2 0.0 collective-permute-done.6.refs_2_
  17.2 2.8 %collective-permute-done.7.refs_3_ = f32[72,256]{1,0:T(8,128)S(1)} collective-permute-done((f32[72,256]{1,0:T(8,128)S(1)}, f32[72,256]{1,0:T(8,128)S(1)}, u32[]{:S(2)}, u32[]{:S(2)}) %collective-permute-start.7) | collective-permute-done | bytes 73760 | tf_op jit(solution)/shard_map/ppermute | solution.py:547
  19.9 8.8 %sweeps.1 = (f32[4,8,16,256]{3,2,1,0:T(8,128)}, f32[4,26,8,256]{3,2,1,0:T(8,128)S(1)}, f32[32,8,256]{2,1,0:T(8,128)S(1)}) custom-call(s32[18]{0:T(128)S(1)} %concatenate.8.scal, f32[72,256]{1,0:T(8,128)S(1)} %get-tuple-element.33.refs_0_, f32[72,256]{1,0:T(8,128)S(1)} %collective-permute-done.5.refs_1_, f32[72,256]{1,0:T(8,128)S(1)} %collective-permute-done.6.refs_2_, ...), custom_call_target="tpu_custom_call" | custom-call | bytes 35000000 | tf_op jit(solution)/shard_map/sweeps/pallas_call | solution.py:32
  28.8 5.3 %all-to-all-start = ((f32[32,16,256]{2,1,0:T(8,128)}), f32[32,16,256]{2,1,0:T(8,128)S(1)}, u32[]{:S(2)}, u32[]{:S(2)}) async-start(f32[32,16,256]{2,1,0:T(8,128)} %bitcast.13), calls=%async_computation | async-start | bytes 1048576 | tf_op jit(solution)/shard_map/all_to_all | solution.py:643
  34.1 4.8 %adjoint.1 = (f32[16,256]{1,0:T(8,128)S(1)}, f32[16,256]{1,0:T(8,128)S(1)}, f32[16,256]{1,0:T(8,128)S(1)}, f32[16,256]{1,0:T(8,128)S(1)}, f32[16,256]{1,0:T(8,12...) custom-call(s32[18]{0:T(128)S(1)} %concatenate.8.scal, ...), custom_call_target="tpu_custom_call" | custom-call | bytes 24500000 | tf_op jit(solution)/shard_map/adjoint/pallas_call | solution.py:32
  39.0 0.3 collective-permute-start.8
  39.3 1.5 %collective-permute-start.9 = (f32[16,256]{1,0:T(8,128)S(1)}, f32[16,256]{1,0:T(8,128)S(1)}, u32[]{:S(2)}, u32[]{:S(2)}) collective-permute-start(f32[16,256]{1,0:T(8,128)S(1)} %get-tuple-element.52), channel_id=1, source_target_pairs={{0,2},{1,3},{2,0},{3,1},{4,6},{5,7},{6,4},{7,5},{8,10},{9,11},{10,... | collective-permute-start | bytes 49160 | tf_op jit(solution)/shard_map/ppermute | solution.py:647
  40.8 0.4 collective-permute-start.10
  41.2 2.3 %collective-permute-start.11 = (f32[16,256]{1,0:T(8,128)S(1)}, f32[16,256]{1,0:T(8,128)S(1)}, u32[]{:S(2)}, u32[]{:S(2)}) collective-permute-start(f32[16,256]{1,0:T(8,128)S(1)} %get-tuple-element.54), channel_id=1, source_target_pairs={{0,4},{1,5},{2,6},{3,7},{4,0},{5,1},{6,2},{7,3},{8,12},{9,13},{10,... | collective-permute-start | bytes 49160 | tf_op jit(solution)/shard_map/ppermute | solution.py:647
  43.5 0.3 collective-permute-start.12
  43.8 0.0 collective-permute-done.8.refs_1_
  43.8 3.3 %collective-permute-start.13 = (f32[16,256]{1,0:T(8,128)S(1)}, f32[16,256]{1,0:T(8,128)S(1)}, u32[]{:S(2)}, u32[]{:S(2)}) collective-permute-start(f32[16,256]{1,0:T(8,128)S(1)} %get-tuple-element.56), channel_id=1, source_target_pairs={{0,6},{1,7},{2,4},{3,5},{4,2},{5,3},{6,0},{7,1},{8,14},{9,15},{10,... | collective-permute-start | bytes 49160 | tf_op jit(solution)/shard_map/ppermute | solution.py:647
  47.0 0.0 collective-permute-done.9.refs_2_
  47.0 0.3 collective-permute-start.14
  47.4 0.0 collective-permute-done.10.refs_3_
  47.4 2.2 %collective-permute-done.11.refs_4_ = f32[16,256]{1,0:T(8,128)S(1)} collective-permute-done((f32[16,256]{1,0:T(8,128)S(1)}, f32[16,256]{1,0:T(8,128)S(1)}, u32[]{:S(2)}, u32[]{:S(2)}) %collective-permute-start.11) | collective-permute-done | bytes 16416 | tf_op jit(solution)/shard_map/ppermute | solution.py:647
  49.6 1.5 %collective-permute-done.12.refs_5_ = f32[16,256]{1,0:T(8,128)S(1)} collective-permute-done((f32[16,256]{1,0:T(8,128)S(1)}, f32[16,256]{1,0:T(8,128)S(1)}, u32[]{:S(2)}, u32[]{:S(2)}) %collective-permute-start.12) | collective-permute-done | bytes 16416 | tf_op jit(solution)/shard_map/ppermute | solution.py:647
  51.1 0.0 collective-permute-done.13.refs_6_
  51.1 1.0 %collective-permute-done.14.refs_7_ = f32[16,256]{1,0:T(8,128)S(1)} collective-permute-done((f32[16,256]{1,0:T(8,128)S(1)}, f32[16,256]{1,0:T(8,128)S(1)}, u32[]{:S(2)}, u32[]{:S(2)}) %collective-permute-start.14) | collective-permute-done | bytes 16416 | tf_op jit(solution)/shard_map/ppermute | solution.py:647
  52.0 0.0 all-to-all-done
  52.1 1.4 %join.1 = (f32[512,256]{1,0:T(8,128)}, f32[128,256]{1,0:T(8,128)}) custom-call(s32[6]{0:T(128)S(1)} %stack.23.scal, f32[512,256]{1,0:T(8,128)S(1)} %bitcast.21, f32[16,256]{1,0:T(8,128)S(1)} %get-tuple-element.50.refs_0_, f32[16,256]{1,0:T(8,128)S(1)} %collective-permute-done.8.refs_1_, f32[16,256]{1,0:T(8,128)S(1)} %collective-permute-done.9.refs_2_, ...), custom_call_target="tpu_custom_call" | custom-call | bytes 3500000 | tf_op jit(solution)/shard_map/join/pallas_call | solution.py:32
  (2 shorter events, 0.0 us)
Async XLA Ops:
  0.6 0.7 %copy-start.1 = (s32[2,1,1,16]{3,2,1,0:T(1,128)S(1)}, s32[2,1,1,16]{3,2,1,0:T(1,128)}, u32[]{:S(2)}) copy-start(s32[2,1,1,16]{3,2,1,0:T(1,128)} %param.9) | copy-start | bytes 388
  0.6 2.0 %copy-start.2 = (s32[1,3]{1,0:T(1,128)S(1)}, s32[1,3]{1,0:T(1,128)}, u32[]{:S(2)}) copy-start(s32[1,3]{1,0:T(1,128)} %station.1) | copy-start | bytes 40
  0.7 9.2 %collective-permute-start.4 = (f32[512,256]{1,0:T(8,128)}, f32[512,256]{1,0:T(8,128)S(1)}, u32[]{:S(2)}, u32[]{:S(2)}) collective-permute-start(f32[512,256]{1,0:T(8,128)} %bitcast.24), channel_id=1, source_target_pairs={{0,1},{1,0},{2,3},{3,2},{4,5},{5,4},{6,7},{7,6},{8,9},{9,8},{10,11... | collective-permute-start | bytes 1572872 | tf_op jit(solution)/shard_map/ppermute | solution.py:550
  1.3 1.3 %collective-permute-start = (s32[2,1,16]{2,1,0:T(1,128)S(1)}, s32[2,1,16]{2,1,0:T(1,128)S(1)}, u32[]{:S(2)}, u32[]{:S(2)}) collective-permute-start(s32[2,1,16]{2,1,0:T(1,128)S(1)} %bitcast.22), channel_id=1, source_target_pairs={{0,1},{1,0},{2,3},{3,2},{4,5},{5,4},{6,7},{7,6},{8,9},{9,8},{10,11... | collective-permute-start | bytes 392 | tf_op jit(solution)/shard_map/ppermute | solution.py:550
  3.7 4.5 %collective-permute-start.3 = (f32[1,2688]{1,0:T(1,128)S(1)}, f32[1,2688]{1,0:T(1,128)S(1)}, u32[]{:S(2)}, u32[]{:S(2)}) collective-permute-start(f32[1,2688]{1,0:T(1,128)S(1)} %get-tuple-element.34.refs_0_), channel_id=1, source_target_pairs={{0,24},{8,16},{16,8},{24,0},{1,25},{9,17},{17,9},{25,1},{2,26},{10... | collective-permute-start | bytes 32264 | tf_op jit(solution)/shard_map/ppermute | solution.py:544
  7.1 2.5 %collective-permute-start.2 = (f32[1,2688]{1,0:T(1,128)S(1)}, f32[1,2688]{1,0:T(1,128)S(1)}, u32[]{:S(2)}, u32[]{:S(2)}) collective-permute-start(f32[1,2688]{1,0:T(1,128)S(1)} %get-tuple-element.34.refs_0_), channel_id=1, source_target_pairs={{0,16},{8,24},{16,0},{24,8},{1,17},{9,25},{17,1},{25,9},{2,18},{10... | collective-permute-start | bytes 32264 | tf_op jit(solution)/shard_map/ppermute | solution.py:544
  7.3 2.5 %collective-permute-start.1 = (f32[1,2688]{1,0:T(1,128)S(1)}, f32[1,2688]{1,0:T(1,128)S(1)}, u32[]{:S(2)}, u32[]{:S(2)}) collective-permute-start(f32[1,2688]{1,0:T(1,128)S(1)} %get-tuple-element.34.refs_0_), channel_id=1, source_target_pairs={{0,8},{8,0},{16,24},{24,16},{1,9},{9,1},{17,25},{25,17},{2,10},{10... | collective-permute-start | bytes 32264 | tf_op jit(solution)/shard_map/ppermute | solution.py:544
  9.8 4.5 %copy-start = (s32[3,2048]{1,0:T(4,128)S(1)}, s32[3,2048]{1,0:T(4,128)}, u32[]{:S(2)}) copy-start(s32[3,2048]{1,0:T(4,128)} %cells) | copy-start | bytes 73732
  10.4 6.7 %collective-permute-start.5 = (f32[72,256]{1,0:T(8,128)S(1)}, f32[72,256]{1,0:T(8,128)S(1)}, u32[]{:S(2)}, u32[]{:S(2)}) collective-permute-start(f32[72,256]{1,0:T(8,128)S(1)} %get-tuple-element.42), channel_id=1, source_target_pairs={{0,2},{1,3},{2,0},{3,1},{4,6},{5,7},{6,4},{7,5},{8,10},{9,11},{10,... | collective-permute-start | bytes 221192 | tf_op jit(solution)/shard_map/ppermute | solution.py:547
  11.8 5.4 %collective-permute-start.6 = (f32[72,256]{1,0:T(8,128)S(1)}, f32[72,256]{1,0:T(8,128)S(1)}, u32[]{:S(2)}, u32[]{:S(2)}) collective-permute-start(f32[72,256]{1,0:T(8,128)S(1)} %get-tuple-element.43), channel_id=1, source_target_pairs={{0,4},{1,5},{2,6},{3,7},{4,0},{5,1},{6,2},{7,3},{8,12},{9,13},{10,... | collective-permute-start | bytes 221192 | tf_op jit(solution)/shard_map/ppermute | solution.py:547
  14.1 5.8 %collective-permute-start.7 = (f32[72,256]{1,0:T(8,128)S(1)}, f32[72,256]{1,0:T(8,128)S(1)}, u32[]{:S(2)}, u32[]{:S(2)}) collective-permute-start(f32[72,256]{1,0:T(8,128)S(1)} %get-tuple-element.44), channel_id=1, source_target_pairs={{0,6},{1,7},{2,4},{3,5},{4,2},{5,3},{6,0},{7,1},{8,14},{9,15},{10,... | collective-permute-start | bytes 221192 | tf_op jit(solution)/shard_map/ppermute | solution.py:547
  28.8 23.3 %all-to-all-start = ((f32[32,16,256]{2,1,0:T(8,128)}), f32[32,16,256]{2,1,0:T(8,128)S(1)}, u32[]{:S(2)}, u32[]{:S(2)}) async-start(f32[32,16,256]{2,1,0:T(8,128)} %bitcast.13), calls=%async_computation | async-start | bytes 1048576 | tf_op jit(solution)/shard_map/all_to_all | solution.py:643
  39.0 4.8 %collective-permute-start.8 = (f32[16,256]{1,0:T(8,128)S(1)}, f32[16,256]{1,0:T(8,128)S(1)}, u32[]{:S(2)}, u32[]{:S(2)}) collective-permute-start(f32[16,256]{1,0:T(8,128)S(1)} %get-tuple-element.51), channel_id=1, source_target_pairs={{0,1},{1,0},{2,3},{3,2},{4,5},{5,4},{6,7},{7,6},{8,9},{9,8},{10,11... | collective-permute-start | bytes 49160 | tf_op jit(solution)/shard_map/ppermute | solution.py:647
  39.3 7.7 %collective-permute-start.9 = (f32[16,256]{1,0:T(8,128)S(1)}, f32[16,256]{1,0:T(8,128)S(1)}, u32[]{:S(2)}, u32[]{:S(2)}) collective-permute-start(f32[16,256]{1,0:T(8,128)S(1)} %get-tuple-element.52), channel_id=1, source_target_pairs={{0,2},{1,3},{2,0},{3,1},{4,6},{5,7},{6,4},{7,5},{8,10},{9,11},{10,... | collective-permute-start | bytes 49160 | tf_op jit(solution)/shard_map/ppermute | solution.py:647
  40.8 6.6 %collective-permute-start.10 = (f32[16,256]{1,0:T(8,128)S(1)}, f32[16,256]{1,0:T(8,128)S(1)}, u32[]{:S(2)}, u32[]{:S(2)}) collective-permute-start(f32[16,256]{1,0:T(8,128)S(1)} %get-tuple-element.53), channel_id=1, source_target_pairs={{0,3},{1,2},{2,1},{3,0},{4,7},{5,6},{6,5},{7,4},{8,11},{9,10},{10,... | collective-permute-start | bytes 49160 | tf_op jit(solution)/shard_map/ppermute | solution.py:647
  41.2 8.4 %collective-permute-start.11 = (f32[16,256]{1,0:T(8,128)S(1)}, f32[16,256]{1,0:T(8,128)S(1)}, u32[]{:S(2)}, u32[]{:S(2)}) collective-permute-start(f32[16,256]{1,0:T(8,128)S(1)} %get-tuple-element.54), channel_id=1, source_target_pairs={{0,4},{1,5},{2,6},{3,7},{4,0},{5,1},{6,2},{7,3},{8,12},{9,13},{10,... | collective-permute-start | bytes 49160 | tf_op jit(solution)/shard_map/ppermute | solution.py:647
  43.5 7.6 %collective-permute-start.12 = (f32[16,256]{1,0:T(8,128)S(1)}, f32[16,256]{1,0:T(8,128)S(1)}, u32[]{:S(2)}, u32[]{:S(2)}) collective-permute-start(f32[16,256]{1,0:T(8,128)S(1)} %get-tuple-element.55), channel_id=1, source_target_pairs={{0,5},{1,4},{2,7},{3,6},{4,1},{5,0},{6,3},{7,2},{8,13},{9,12},{10,... | collective-permute-start | bytes 49160 | tf_op jit(solution)/shard_map/ppermute | solution.py:647
  43.8 7.3 %collective-permute-start.13 = (f32[16,256]{1,0:T(8,128)S(1)}, f32[16,256]{1,0:T(8,128)S(1)}, u32[]{:S(2)}, u32[]{:S(2)}) collective-permute-start(f32[16,256]{1,0:T(8,128)S(1)} %get-tuple-element.56), channel_id=1, source_target_pairs={{0,6},{1,7},{2,4},{3,5},{4,2},{5,3},{6,0},{7,1},{8,14},{9,15},{10,... | collective-permute-start | bytes 49160 | tf_op jit(solution)/shard_map/ppermute | solution.py:647
  47.0 5.0 %collective-permute-start.14 = (f32[16,256]{1,0:T(8,128)S(1)}, f32[16,256]{1,0:T(8,128)S(1)}, u32[]{:S(2)}, u32[]{:S(2)}) collective-permute-start(f32[16,256]{1,0:T(8,128)S(1)} %get-tuple-element.57), channel_id=1, source_target_pairs={{0,7},{1,6},{2,5},{3,4},{4,3},{5,2},{6,1},{7,0},{8,15},{9,14},{10,... | collective-permute-start | bytes 49160 | tf_op jit(solution)/shard_map/ppermute | solution.py:647

commit v5 on v4

--- a/solution.py
+++ b/solution.py
@@ -51,14 +51,25 @@
     ])
 
 
-def head_kernel(delays, velocity, station, active, active_other, out, layer, sems):
-    events = delays.shape[1]
-    copies = [
-        pltpu.make_async_copy(delays, out.at[:, pl.ds(0, events)], sems.at[0]),
-        pltpu.make_async_copy(velocity, layer, sems.at[1]),
-    ]
+def where_am_i(own_rows):
+    place = lax.axis_index("space")
+    line_row = lax.axis_index("src") * (lax.axis_size("space") * own_rows)
+    first = line_row + place * own_rows - HALO
+    return lax.div(place, 2), lax.rem(place, 2), line_row, first
+
+
+def fetch_kernel(*refs):
+    ins, (*outs, sems) = refs[: len(refs) // 2], refs[len(refs) // 2 :]
+    copies = [pltpu.make_async_copy(a, b, sems.at[i]) for i, (a, b) in enumerate(zip(ins, outs))]
     for copy in copies:
         copy.start()
+    for copy in copies:
+        copy.wait()
+
+
+def head_kernel(delays, station, active, active_other, out):
+    events = delays.shape[1]
+    out[:, :events] = delays[...]
     out[:, events:] = jnp.zeros((1, out.shape[1] - events), jnp.float32)
     at = events
     out[:, at : at + 3] = station[...].astype(jnp.float32)
@@ -66,12 +77,10 @@
         for part in range(ROUNDS):
             at += LANES
             out[:, at : at + source.shape[-1]] = source[part].astype(jnp.float32)
-    for copy in copies:
-        copy.wait()
-
-
-def pack_kernel(rows, own_rows, slots, scal, own, other, *refs):
-    line_row, chip, core = scal[0], scal[1], scal[2]
+
+
+def pack_kernel(rows, own_rows, slots, own, other, *refs):
+    chip, core, line_row, _ = where_am_i(own_rows)
     pays, outs = refs[:slots], refs[slots:]
     total = own.shape[0]
     chunk = math.gcd(own_rows, 8)
@@ -95,10 +104,10 @@
 EVENT_CHUNK = 2048
 
 
-def scatter_kernel(layers, events, scal, cells, *refs):
+def scatter_kernel(layers, own_rows, events, cells, *refs):
     slots = len(refs) - 3
     pays, count, delay_sum, left = refs[:slots], refs[slots], refs[slots + 1], refs[slots + 2]
-    first_row = scal[3] + HALO - ADJ_HALO
+    first_row = where_am_i(own_rows)[3] + HALO - ADJ_HALO
     height, width = count.shape
     chunk = left.shape[1]
     steps = events // chunk
@@ -160,15 +169,18 @@
     return [function(*pieces) for pieces in zip(*values)]
 
 
-def loop(low, high, size, body, unroll=1):
+def loop(low, high, size, body, unroll=16):
     steps = (high - low) // size
-    if steps:
+    if steps <= unroll:
+        for i in range(steps):
+            body(low + i * size, size)
+    else:
         lax.fori_loop(
             0,
             steps,
             lambda i, carry: (body(low + i * size, size), carry)[1],
             0,
-            unroll=min(unroll, steps),
+            unroll=unroll,
         )
     if low + steps * size < high:
         loop(low + steps * size, high, max(size // 2, 1), body)
@@ -283,10 +295,10 @@
 
 
 SWEEP_ROWS = 4
-SWEEP_UNROLL = 2
-
-
-def sweep_kernel(layers, own_rows, slots, chips, scal, *refs):
+SWEEP_UNROLL = 8
+
+
+def sweep_kernel(layers, own_rows, grid_rows, slots, chips, scal, *refs):
     rows = own_rows + 2 * HALO
     depth = refs[0].shape[-1]
     parts = depth // LANES
@@ -294,8 +306,9 @@
     times_out, final, speed, refs = refs[0], refs[1], refs[2], refs[3:]
     cost, twice, one_half, ping, pong, acts, mask, flat = refs
     flat = Flat(flat, layers)
-    line, chip, core, y_first, grid_rows = scal[4], scal[1], scal[2], scal[3], scal[5]
-    stations = [[scal[6 + 3 * slot + i] for i in range(3)] for slot in range(slots)]
+    line = lax.axis_index("src")
+    chip, core, _, y_first = where_am_i(own_rows)
+    stations = [[scal[3 * slot + i] for i in range(3)] for slot in range(slots)]
 
     for j in range(chips):
         for c in range(2):
@@ -370,7 +383,7 @@
                     slot,
                 )
 
-        loop(low, high, SWEEP_ROWS, body, SWEEP_UNROLL)
+        loop(low, high, SWEEP_ROWS, body, SWEEP_UNROLL if slots <= 4 else 1)
         for slot in range(slots):
             at_x, at_y, at_z = stations[slot]
             local = at_y - y_first
@@ -397,18 +410,18 @@
 
 
 ADJ_ROWS = 4
-ADJ_UNROLL = 2
-
-
-def adjoint_kernel(layers, own_rows, slots, scal, final, speed, count, delay_sum, *refs):
+ADJ_UNROLL = 8
+
+
+def adjoint_kernel(layers, own_rows, grid_rows, slots, scal, final, speed, count, delay_sum, *refs):
     depth = final.shape[-1]
     parts = depth // LANES
     kernel_out, refs = refs[:layers], refs[layers:]
     weight, src, adj_a, adj_b, density, flat = refs
     together = weight.shape[0]
     flat = Flat(flat, layers)
-    y_first, grid_rows = scal[3], scal[5]
-    stations = [[scal[6 + 3 * slot + i] for i in range(3)] for slot in range(slots)]
+    y_first = where_am_i(own_rows)[3]
+    stations = [[scal[3 * slot + i] for i in range(3)] for slot in range(slots)]
     straight = [Straight(layers, parts, stations[slot], grid_rows) for slot in range(slots)]
     shift = HALO - ADJ_HALO
     rows = own_rows + 2 * ADJ_HALO
@@ -493,12 +506,12 @@
                     total = each(smooth, low, value, high)
                 put(density, row, size, total)
 
-        loop(low, high, ADJ_ROWS, body, ADJ_UNROLL)
+        loop(low, high, ADJ_ROWS, body, ADJ_UNROLL if slots <= 4 else 1)
 
     for first in range(0, slots, together):
         group = range(first, min(first + together, slots))
         loop(0, rows, 4, functools.partial(make_source, group))
-        loop(1, rows - 1, 2, functools.partial(make_weight, group))
+        loop(1, rows - 1, 4, functools.partial(make_weight, group))
         fields = [src] + [(adj_a, adj_b)[i % 2] for i in range(ADJ_SWEEPS - 1)] + [None]
         for index in range(ADJ_SWEEPS):
             sweep(group, fields[index], fields[index + 1], index + 1, rows - 1 - index)
@@ -512,15 +525,15 @@
 
     loop(0, own_rows, 4, finish)
     for m, out in enumerate(kernel_out):
-        out[...] = flat.get_layer(scal[1] * 2 + scal[2] ^ m, own_rows)
-
-
-def join_kernel(scal, times, *refs):
+        out[...] = flat.get_layer(lax.axis_index("space") ^ m, own_rows)
+
+
+def join_kernel(times, *refs):
     blocks, (times_out, out, sems) = refs[:-3], refs[-3:]
     rows = blocks[0].shape[0]
     copies = [pltpu.make_async_copy(times, times_out, sems.at[0])]
     for m, block in enumerate(blocks):
-        start = pl.multiple_of(((scal[1] * 2 + scal[2]) ^ m) * rows, rows)
+        start = pl.multiple_of((lax.axis_index("space") ^ m) * rows, rows)
         copies.append(pltpu.make_async_copy(block, out.at[pl.ds(start, rows)], sems.at[m + 1]))
     for copy in copies:
         copy.start()
@@ -537,8 +550,6 @@
     own_rows = line_rows // layers
     rows = own_rows + 2 * HALO
     adj_rows = own_rows + 2 * ADJ_HALO
-    line, place = lax.axis_index("src"), lax.axis_index("space")
-    chip, core = place // 2, place % 2
 
     def to_line(array, j):
         return lax.ppermute(array, "src", [(i, i ^ j) for i in range(slots)])
@@ -559,19 +570,22 @@
     def field(*lead):
         return (*lead, layers, depth)
 
-    y_first = line * line_rows + place * own_rows - HALO
-    here = jnp.stack([line * line_rows, chip, core, y_first, line, jnp.int32(grid_rows)])
-    here = here.astype(jnp.int32)
-
     other = to_core(velocity[0])
     active_other = to_core(active[:, 0])
-    payload, layer = call(
+    mine = [velocity[0], delays, station_cells, active[:, 0]]
+    layer, delays, station_cells, active = call(
+        fetch_kernel,
+        "fetch",
+        [jax.ShapeDtypeStruct(a.shape, a.dtype) for a in mine],
+        mine,
+        [pltpu.SemaphoreType.DMA((len(mine),))],
+        hbm_in=range(len(mine)),
+    )
+    (payload,) = call(
         head_kernel,
         "head",
-        [out(1, events + LANES * (1 + 2 * ROUNDS)), out(grid_rows, depth)],
-        [delays, velocity[0], station_cells, active[:, 0], active_other],
-        [pltpu.SemaphoreType.DMA((2,))],
-        hbm_in=(0, 1),
+        [out(1, events + LANES * (1 + 2 * ROUNDS))],
+        [delays, station_cells, active, active_other],
     )
     pays = [payload] + [to_line(payload, j) for j in range(1, slots)]
 
@@ -580,21 +594,20 @@
         functools.partial(pack_kernel, rows, own_rows, slots),
         "pack",
         [out(height, depth)] * chips,
-        [here, layer, other, *pays],
+        [layer, other, *pays],
     )
     vel = [packed[0]] + [to_chip(packed[j], j) for j in range(1, chips)]
 
     pays, cells, _ = lax.optimization_barrier((pays, event_cells, packed[0]))
-    stations = jnp.concatenate([p[0, events : events + 3] for p in pays]).astype(jnp.int32)
-    scal = jnp.concatenate([here, stations])
+    scal = jnp.concatenate([p[0, events : events + 3] for p in pays]).astype(jnp.int32)
     chunk = events
     while (1 + 2 * slots) * adj_rows * layers * chunk > EVENT_CHUNK * 2**11:
         chunk //= 2
     count, delay_sum = call(
-        functools.partial(scatter_kernel, layers, events),
+        functools.partial(scatter_kernel, layers, own_rows, events),
         "events",
         [out(adj_rows * layers, depth), out(slots, adj_rows * layers, depth)],
-        [here, cells, *pays],
+        [cells, *pays],
         [pltpu.VMEM(((1 + 2 * slots) * adj_rows * layers, chunk), jnp.bfloat16)],
         microseconds=3.0,
     )
@@ -604,7 +617,7 @@
     together = min(slots, 4)
     flat = scratch(depth // LANES, rows * layers, LANES)
     times, final, speed = call(
-        functools.partial(sweep_kernel, layers, own_rows, slots, chips),
+        functools.partial(sweep_kernel, layers, own_rows, grid_rows, slots, chips),
         "sweeps",
         [
             out(slots, layers, own_rows, depth),
@@ -625,7 +638,7 @@
         microseconds=10.0,
     )
     kernel = call(
-        functools.partial(adjoint_kernel, layers, own_rows, slots),
+        functools.partial(adjoint_kernel, layers, own_rows, grid_rows, slots),
         "adjoint",
         [out(own_rows, depth)] * layers,
         [scal, final, speed, count, delay_sum],
@@ -651,9 +664,9 @@
         join_kernel,
         "join",
         [out(grid_rows, depth), out(line_rows, depth)],
-        [here, times.reshape(grid_rows, depth), *blocks],
+        [times.reshape(grid_rows, depth), *blocks],
         [pltpu.SemaphoreType.DMA((1 + layers,))],
-        in_place=range(1, 2 + layers),
+        in_place=range(1 + layers),
         hbm_out=(0, 1),
     )
     return (times.reshape(1, 1, grid_rows, depth), kernel.reshape(1, line_rows, depth))

time: 54.2 us -> 50.3 us (0.928)
  Pallas kernels: 19.6 us -> 15.4 us
  starting transfers between devices: 21.3 us -> 23.2 us
  waiting for transfers between devices: 11 us -> 9.57 us
    pallas_call x6 -> x7, Pallas kernels: 19.6 us -> 15.4 us  [call(): pl.pallas_call(body, out_shape=list(outs), in_specs=[spec(pltpu.HBM if i...]
    ppermute x7, starting transfers between devices: 8.4 us -> 9.92 us  [per_device(): lax.ppermute(kernel[m], 'space', [(i, i ^ m) for i in range(layers)])]
    ppermute x2, waiting for transfers between devices: 1.24 us -> 0.14 us  [to_core(): return lax.ppermute(array, 'space', [(i, i ^ 1) for i in range(layers)])]
    ppermute x7, waiting for transfers between devices: 4.67 us -> 3.91 us  [per_device(): lax.ppermute(kernel[m], 'space', [(i, i ^ m) for i in range(layers)])]
  transfers between devices with their start and end apart: 16 -> 16, of which waited for: 8 -> 8; matrix products, arithmetic and copies ran while one was open for 0% -> 0% of each run, Pallas kernels for 16% -> 14%
where the time goes in v5:
time: 50.3 us; the launch traced here: 49.7 us
  starting transfers between devices  23.2 us (46%)
  Pallas kernels  15.4 us (31%)
  waiting for transfers between devices  9.57 us (19%)
  between operations  0.87 us (2%)
  local copies, waits for them, and re-layouts  0.56 us (1%)
    pallas_call x7, Pallas kernels, call(): pl.pallas_call(body, out_shape=list(outs), in_specs=[spec(pltpu.HBM if i...  15.4 us
    ppermute x7, starting transfers between devices, per_device(): lax.ppermute(kernel[m], 'space', [(i, i ^ m) for i in range(layers)])  9.92 us
    all_to_all x1, starting transfers between devices, per_device(): lax.all_to_all(times.reshape(slots * layers, own_rows, depth), ('src', 's...  5.48 us
    ppermute x3, starting transfers between devices, to_line(): return lax.ppermute(array, 'src', [(i, i ^ j) for i in range(slots)])  3.94 us
    ppermute x7, waiting for transfers between devices, per_device(): lax.ppermute(kernel[m], 'space', [(i, i ^ m) for i in range(layers)])  3.91 us
    ppermute x3, starting transfers between devices, to_chip(): return lax.ppermute(array, 'space', [(i, i ^ 2 * j) for i in range(layers)])  3.67 us
    ppermute x3, waiting for transfers between devices, to_chip(): return lax.ppermute(array, 'space', [(i, i ^ 2 * j) for i in range(layers)])  3.12 us
    ppermute x3, waiting for transfers between devices, to_line(): return lax.ppermute(array, 'src', [(i, i ^ j) for i in range(slots)])  2.4 us
  transfers between devices with their start and end apart: 16, of which 8 were waited for; matrix products, arithmetic and copies ran while one was open for 0% of the time, Pallas kernels for 14%

profile of v5, /device:TPU:1, one launch (start us, length us, event | category | flops | bytes accessed | tf_op | source)
XLA Modules:
  0.0 49.7 jit_solution(13881851872822195358)
XLA Ops:
  0.6 0.0 copy-start.1
  0.6 0.1 collective-permute-start.4
  0.8 0.5 %copy-done.1 = s32[2,1,1,16]{3,2,1,0:T(1,128)S(1)} copy-done((s32[2,1,1,16]{3,2,1,0:T(1,128)S(1)}, s32[2,1,1,16]{3,2,1,0:T(1,128)}, u32[]{:S(2)}) %copy-start.1) | copy-done | bytes 152
  1.3 0.1 collective-permute-start
  1.4 1.1 %fetch.1 = (f32[512,256]{1,0:T(8,128)S(1)}, f32[1,2048]{1,0:T(1,128)S(1)}, s32[1,3]{1,0:T(1,128)S(1)}, s32[2,1,16]{2,1,0:T(1,128)S(1)}) custom-call(f32[512,256]{1,0:T(8,128)} %bitcast.18, f32[1,2048]{1,0:T(1,128)} %refs_1_.1, s32[1,3]{1,0:T(1,128)} %refs_2_.1, s32[2,1,16]{2,1,0:T(1,128)} %bitcast.19), custom_call_target="tpu_custom_call" | custom-call | bytes 3500000 | tf_op jit(solution)/shard_map/fetch/pallas_call | solution.py:32
  2.5 0.1 collective-permute-done.active_other
  2.6 3.6 %collective-permute-start.3 = (f32[1,2688]{1,0:T(1,128)S(1)}, f32[1,2688]{1,0:T(1,128)S(1)}, u32[]{:S(2)}, u32[]{:S(2)}) collective-permute-start(f32[1,2688]{1,0:T(1,128)S(1)} %head.1.refs_0_), channel_id=1, source_target_pairs={{0,24},{8,16},{16,8},{24,0},{1,25},{9,17},{17,9},{25,1},{2,26},{10... | collective-permute-start | bytes 32264 | tf_op jit(solution)/shard_map/ppermute | solution.py:555
  6.2 0.2 collective-permute-start.2
  6.4 0.1 collective-permute-start.1
  6.5 0.7 %collective-permute-done.3.refs_3_ = f32[1,2688]{1,0:T(1,128)S(1)} collective-permute-done((f32[1,2688]{1,0:T(1,128)S(1)}, f32[1,2688]{1,0:T(1,128)S(1)}, u32[]{:S(2)}, u32[]{:S(2)}) %collective-permute-start.3) | collective-permute-done | bytes 10784 | tf_op jit(solution)/shard_map/ppermute | solution.py:555
  7.2 1.5 %collective-permute-done.2.refs_2_ = f32[1,2688]{1,0:T(1,128)S(1)} collective-permute-done((f32[1,2688]{1,0:T(1,128)S(1)}, f32[1,2688]{1,0:T(1,128)S(1)}, u32[]{:S(2)}, u32[]{:S(2)}) %collective-permute-start.2) | collective-permute-done | bytes 10784 | tf_op jit(solution)/shard_map/ppermute | solution.py:555
  8.7 0.2 collective-permute-done.1.refs_1_
  8.9 0.0 collective-permute-done.4.other
  9.0 0.0 copy-start
  9.0 0.1 pack.1
  9.0 1.4 %collective-permute-start.5 = (f32[72,256]{1,0:T(8,128)S(1)}, f32[72,256]{1,0:T(8,128)S(1)}, u32[]{:S(2)}, u32[]{:S(2)}) collective-permute-start(f32[72,256]{1,0:T(8,128)S(1)} %get-tuple-element.46), channel_id=1, source_target_pairs={{0,2},{1,3},{2,0},{3,1},{4,6},{5,7},{6,4},{7,5},{8,10},{9,11},{10,... | collective-permute-start | bytes 221192 | tf_op jit(solution)/shard_map/ppermute | solution.py:558
  10.4 2.3 %collective-permute-start.6 = (f32[72,256]{1,0:T(8,128)S(1)}, f32[72,256]{1,0:T(8,128)S(1)}, u32[]{:S(2)}, u32[]{:S(2)}) collective-permute-start(f32[72,256]{1,0:T(8,128)S(1)} %get-tuple-element.47), channel_id=1, source_target_pairs={{0,4},{1,5},{2,6},{3,7},{4,0},{5,1},{6,2},{7,3},{8,12},{9,13},{10,... | collective-permute-start | bytes 221192 | tf_op jit(solution)/shard_map/ppermute | solution.py:558
  12.7 0.0 collective-permute-start.7
  12.7 0.0 copy-done
  12.7 2.3 %events.1 = (f32[208,256]{1,0:T(8,128)S(1)}, f32[4,208,256]{2,1,0:T(8,128)S(1)}) custom-call(s32[3,2048]{1,0:T(4,128)S(1)} %copy-done, f32[1,2688]{1,0:T(1,128)S(1)} %head.1.refs_0_, f32[1,2688]{1,0:T(1,128)S(1)} %collective-permute-done.1.refs_1_, f32[1,2688]{1,0:T(1,128)S(1)} %collective-permute-done.2.refs_2_, f32[1,2688]{1,0:T(1,128)S(1)} %collective-permute-done.3.refs_3_), custom_call_target="tpu_custom_call" | custom-call | bytes 10500000 | tf_op jit(solution)/shard_map/events/pallas_call | solution.py:32
  15.0 0.1 maximum_convert_fusion.scal
  15.1 0.0 collective-permute-done.5.refs_1_
  15.1 0.1 collective-permute-done.6.refs_2_
  15.3 3.0 %collective-permute-done.7.refs_3_ = f32[72,256]{1,0:T(8,128)S(1)} collective-permute-done((f32[72,256]{1,0:T(8,128)S(1)}, f32[72,256]{1,0:T(8,128)S(1)}, u32[]{:S(2)}, u32[]{:S(2)}) %collective-permute-start.7) | collective-permute-done | bytes 73760 | tf_op jit(solution)/shard_map/ppermute | solution.py:558
  18.2 7.6 %sweeps.1 = (f32[4,8,16,256]{3,2,1,0:T(8,128)}, f32[4,26,8,256]{3,2,1,0:T(8,128)S(1)}, f32[32,8,256]{2,1,0:T(8,128)S(1)}) custom-call(s32[12]{0:T(128)S(1)} %maximum_convert_fusion.scal, f32[72,256]{1,0:T(8,128)S(1)} %get-tuple-element.37.refs_0_, f32[72,256]{1,0:T(8,128)S(1)} %collective-permute-done.5.refs_1_, ...), custom_call_target="tpu_custom_call" | custom-call | bytes 35000000 | tf_op jit(solution)/shard_map/sweeps/pallas_call | solution.py:32
  25.9 5.5 %all-to-all-start = ((f32[32,16,256]{2,1,0:T(8,128)}), f32[32,16,256]{2,1,0:T(8,128)S(1)}, u32[]{:S(2)}, u32[]{:S(2)}) async-start(f32[32,16,256]{2,1,0:T(8,128)} %bitcast.8), calls=%async_computation | async-start | bytes 1048576 | tf_op jit(solution)/shard_map/all_to_all | solution.py:656
  31.3 3.4 %adjoint.1 = (f32[16,256]{1,0:T(8,128)S(1)}, f32[16,256]{1,0:T(8,128)S(1)}, f32[16,256]{1,0:T(8,128)S(1)}, f32[16,256]{1,0:T(8,128)S(1)}, f32[16,256]{1,0:T(8,12...) custom-call(s32[12]{0:T(128)S(1)} %maximum_convert_fusion.scal, ...), custom_call_target="tpu_custom_call" | custom-call | bytes 24500000 | tf_op jit(solution)/shard_map/adjoint/pallas_call | solution.py:32
  34.8 0.5 %collective-permute-start.8 = (f32[16,256]{1,0:T(8,128)S(1)}, f32[16,256]{1,0:T(8,128)S(1)}, u32[]{:S(2)}, u32[]{:S(2)}) collective-permute-start(f32[16,256]{1,0:T(8,128)S(1)} %get-tuple-element.55), channel_id=1, source_target_pairs={{0,1},{1,0},{2,3},{3,2},{4,5},{5,4},{6,7},{7,6},{8,9},{9,8},{10,11... | collective-permute-start | bytes 49160 | tf_op jit(solution)/shard_map/ppermute | solution.py:660
  35.3 1.3 %collective-permute-start.9 = (f32[16,256]{1,0:T(8,128)S(1)}, f32[16,256]{1,0:T(8,128)S(1)}, u32[]{:S(2)}, u32[]{:S(2)}) collective-permute-start(f32[16,256]{1,0:T(8,128)S(1)} %get-tuple-element.56), channel_id=1, source_target_pairs={{0,2},{1,3},{2,0},{3,1},{4,6},{5,7},{6,4},{7,5},{8,10},{9,11},{10,... | collective-permute-start | bytes 49160 | tf_op jit(solution)/shard_map/ppermute | solution.py:660
  36.6 0.4 collective-permute-start.10
  37.0 2.3 %collective-permute-start.11 = (f32[16,256]{1,0:T(8,128)S(1)}, f32[16,256]{1,0:T(8,128)S(1)}, u32[]{:S(2)}, u32[]{:S(2)}) collective-permute-start(f32[16,256]{1,0:T(8,128)S(1)} %get-tuple-element.58), channel_id=1, source_target_pairs={{0,4},{1,5},{2,6},{3,7},{4,0},{5,1},{6,2},{7,3},{8,12},{9,13},{10,... | collective-permute-start | bytes 49160 | tf_op jit(solution)/shard_map/ppermute | solution.py:660
  39.3 0.4 collective-permute-start.12
  39.7 0.0 collective-permute-done.8.refs_1_
  39.7 3.2 %collective-permute-start.13 = (f32[16,256]{1,0:T(8,128)S(1)}, f32[16,256]{1,0:T(8,128)S(1)}, u32[]{:S(2)}, u32[]{:S(2)}) collective-permute-start(f32[16,256]{1,0:T(8,128)S(1)} %get-tuple-element.60), channel_id=1, source_target_pairs={{0,6},{1,7},{2,4},{3,5},{4,2},{5,3},{6,0},{7,1},{8,14},{9,15},{10,... | collective-permute-start | bytes 49160 | tf_op jit(solution)/shard_map/ppermute | solution.py:660
  42.8 0.0 collective-permute-done.9.refs_2_
  42.8 1.9 %collective-permute-start.14 = (f32[16,256]{1,0:T(8,128)S(1)}, f32[16,256]{1,0:T(8,128)S(1)}, u32[]{:S(2)}, u32[]{:S(2)}) collective-permute-start(f32[16,256]{1,0:T(8,128)S(1)} %get-tuple-element.61), channel_id=1, source_target_pairs={{0,7},{1,6},{2,5},{3,4},{4,3},{5,2},{6,1},{7,0},{8,15},{9,14},{10,... | collective-permute-start | bytes 49160 | tf_op jit(solution)/shard_map/ppermute | solution.py:660
  44.7 0.0 collective-permute-done.10.refs_3_
  44.7 2.1 %collective-permute-done.11.refs_4_ = f32[16,256]{1,0:T(8,128)S(1)} collective-permute-done((f32[16,256]{1,0:T(8,128)S(1)}, f32[16,256]{1,0:T(8,128)S(1)}, u32[]{:S(2)}, u32[]{:S(2)}) %collective-permute-start.11) | collective-permute-done | bytes 16416 | tf_op jit(solution)/shard_map/ppermute | solution.py:660
  46.8 1.8 %collective-permute-done.12.refs_5_ = f32[16,256]{1,0:T(8,128)S(1)} collective-permute-done((f32[16,256]{1,0:T(8,128)S(1)}, f32[16,256]{1,0:T(8,128)S(1)}, u32[]{:S(2)}, u32[]{:S(2)}) %collective-permute-start.12) | collective-permute-done | bytes 16416 | tf_op jit(solution)/shard_map/ppermute | solution.py:660
  48.6 0.0 collective-permute-done.13.refs_6_
  48.6 0.0 collective-permute-done.14.refs_7_
  48.6 0.0 all-to-all-done
  48.6 0.9 %join.1 = (f32[512,256]{1,0:T(8,128)}, f32[128,256]{1,0:T(8,128)}) custom-call(f32[512,256]{1,0:T(8,128)S(1)} %bitcast.16, f32[16,256]{1,0:T(8,128)S(1)} %get-tuple-element.54.refs_0_, f32[16,256]{1,0:T(8,128)S(1)} %collective-permute-done.8.refs_1_, f32[16,256]{1,0:T(8,128)S(1)} %collective-permute-done.9.refs_2_, ...), custom_call_target="tpu_custom_call" | custom-call | bytes 3500000 | tf_op jit(solution)/shard_map/join/pallas_call | solution.py:32
  (3 shorter events, 0.0 us)
Async XLA Ops:
  0.6 0.7 %copy-start.1 = (s32[2,1,1,16]{3,2,1,0:T(1,128)S(1)}, s32[2,1,1,16]{3,2,1,0:T(1,128)}, u32[]{:S(2)}) copy-start(s32[2,1,1,16]{3,2,1,0:T(1,128)} %param.9) | copy-start | bytes 388
  0.6 8.3 %collective-permute-start.4 = (f32[512,256]{1,0:T(8,128)}, f32[512,256]{1,0:T(8,128)S(1)}, u32[]{:S(2)}, u32[]{:S(2)}) collective-permute-start(f32[512,256]{1,0:T(8,128)} %bitcast.17), channel_id=1, source_target_pairs={{0,1},{1,0},{2,3},{3,2},{4,5},{5,4},{6,7},{7,6},{8,9},{9,8},{10,11... | collective-permute-start | bytes 1572872 | tf_op jit(solution)/shard_map/ppermute | solution.py:561
  1.3 1.3 %collective-permute-start = (s32[2,1,16]{2,1,0:T(1,128)S(1)}, s32[2,1,16]{2,1,0:T(1,128)S(1)}, u32[]{:S(2)}, u32[]{:S(2)}) collective-permute-start(s32[2,1,16]{2,1,0:T(1,128)S(1)} %bitcast.20), channel_id=1, source_target_pairs={{0,1},{1,0},{2,3},{3,2},{4,5},{5,4},{6,7},{7,6},{8,9},{9,8},{10,11... | collective-permute-start | bytes 392 | tf_op jit(solution)/shard_map/ppermute | solution.py:561
  2.6 4.6 %collective-permute-start.3 = (f32[1,2688]{1,0:T(1,128)S(1)}, f32[1,2688]{1,0:T(1,128)S(1)}, u32[]{:S(2)}, u32[]{:S(2)}) collective-permute-start(f32[1,2688]{1,0:T(1,128)S(1)} %head.1.refs_0_), channel_id=1, source_target_pairs={{0,24},{8,16},{16,8},{24,0},{1,25},{9,17},{17,9},{25,1},{2,26},{10... | collective-permute-start | bytes 32264 | tf_op jit(solution)/shard_map/ppermute | solution.py:555
  6.2 2.5 %collective-permute-start.2 = (f32[1,2688]{1,0:T(1,128)S(1)}, f32[1,2688]{1,0:T(1,128)S(1)}, u32[]{:S(2)}, u32[]{:S(2)}) collective-permute-start(f32[1,2688]{1,0:T(1,128)S(1)} %head.1.refs_0_), channel_id=1, source_target_pairs={{0,16},{8,24},{16,0},{24,8},{1,17},{9,25},{17,1},{25,9},{2,18},{10... | collective-permute-start | bytes 32264 | tf_op jit(solution)/shard_map/ppermute | solution.py:555
  6.4 2.5 %collective-permute-start.1 = (f32[1,2688]{1,0:T(1,128)S(1)}, f32[1,2688]{1,0:T(1,128)S(1)}, u32[]{:S(2)}, u32[]{:S(2)}) collective-permute-start(f32[1,2688]{1,0:T(1,128)S(1)} %head.1.refs_0_), channel_id=1, source_target_pairs={{0,8},{8,0},{16,24},{24,16},{1,9},{9,1},{17,25},{25,17},{2,10},{10... | collective-permute-start | bytes 32264 | tf_op jit(solution)/shard_map/ppermute | solution.py:555
  9.0 3.8 %copy-start = (s32[3,2048]{1,0:T(4,128)S(1)}, s32[3,2048]{1,0:T(4,128)}, u32[]{:S(2)}) copy-start(s32[3,2048]{1,0:T(4,128)} %cells) | copy-start | bytes 73732
  9.0 6.1 %collective-permute-start.5 = (f32[72,256]{1,0:T(8,128)S(1)}, f32[72,256]{1,0:T(8,128)S(1)}, u32[]{:S(2)}, u32[]{:S(2)}) collective-permute-start(f32[72,256]{1,0:T(8,128)S(1)} %get-tuple-element.46), channel_id=1, source_target_pairs={{0,2},{1,3},{2,0},{3,1},{4,6},{5,7},{6,4},{7,5},{8,10},{9,11},{10,... | collective-permute-start | bytes 221192 | tf_op jit(solution)/shard_map/ppermute | solution.py:558
  10.4 4.9 %collective-permute-start.6 = (f32[72,256]{1,0:T(8,128)S(1)}, f32[72,256]{1,0:T(8,128)S(1)}, u32[]{:S(2)}, u32[]{:S(2)}) collective-permute-start(f32[72,256]{1,0:T(8,128)S(1)} %get-tuple-element.47), channel_id=1, source_target_pairs={{0,4},{1,5},{2,6},{3,7},{4,0},{5,1},{6,2},{7,3},{8,12},{9,13},{10,... | collective-permute-start | bytes 221192 | tf_op jit(solution)/shard_map/ppermute | solution.py:558
  12.7 5.6 %collective-permute-start.7 = (f32[72,256]{1,0:T(8,128)S(1)}, f32[72,256]{1,0:T(8,128)S(1)}, u32[]{:S(2)}, u32[]{:S(2)}) collective-permute-start(f32[72,256]{1,0:T(8,128)S(1)} %get-tuple-element.48), channel_id=1, source_target_pairs={{0,6},{1,7},{2,4},{3,5},{4,2},{5,3},{6,0},{7,1},{8,14},{9,15},{10,... | collective-permute-start | bytes 221192 | tf_op jit(solution)/shard_map/ppermute | solution.py:558
  25.9 22.8 %all-to-all-start = ((f32[32,16,256]{2,1,0:T(8,128)}), f32[32,16,256]{2,1,0:T(8,128)S(1)}, u32[]{:S(2)}, u32[]{:S(2)}) async-start(f32[32,16,256]{2,1,0:T(8,128)} %bitcast.8), calls=%async_computation | async-start | bytes 1048576 | tf_op jit(solution)/shard_map/all_to_all | solution.py:656
  34.8 4.9 %collective-permute-start.8 = (f32[16,256]{1,0:T(8,128)S(1)}, f32[16,256]{1,0:T(8,128)S(1)}, u32[]{:S(2)}, u32[]{:S(2)}) collective-permute-start(f32[16,256]{1,0:T(8,128)S(1)} %get-tuple-element.55), channel_id=1, source_target_pairs={{0,1},{1,0},{2,3},{3,2},{4,5},{5,4},{6,7},{7,6},{8,9},{9,8},{10,11... | collective-permute-start | bytes 49160 | tf_op jit(solution)/shard_map/ppermute | solution.py:660
  35.3 7.6 %collective-permute-start.9 = (f32[16,256]{1,0:T(8,128)S(1)}, f32[16,256]{1,0:T(8,128)S(1)}, u32[]{:S(2)}, u32[]{:S(2)}) collective-permute-start(f32[16,256]{1,0:T(8,128)S(1)} %get-tuple-element.56), channel_id=1, source_target_pairs={{0,2},{1,3},{2,0},{3,1},{4,6},{5,7},{6,4},{7,5},{8,10},{9,11},{10,... | collective-permute-start | bytes 49160 | tf_op jit(solution)/shard_map/ppermute | solution.py:660
  36.6 8.1 %collective-permute-start.10 = (f32[16,256]{1,0:T(8,128)S(1)}, f32[16,256]{1,0:T(8,128)S(1)}, u32[]{:S(2)}, u32[]{:S(2)}) collective-permute-start(f32[16,256]{1,0:T(8,128)S(1)} %get-tuple-element.57), channel_id=1, source_target_pairs={{0,3},{1,2},{2,1},{3,0},{4,7},{5,6},{6,5},{7,4},{8,11},{9,10},{10,... | collective-permute-start | bytes 49160 | tf_op jit(solution)/shard_map/ppermute | solution.py:660
  37.0 9.8 %collective-permute-start.11 = (f32[16,256]{1,0:T(8,128)S(1)}, f32[16,256]{1,0:T(8,128)S(1)}, u32[]{:S(2)}, u32[]{:S(2)}) collective-permute-start(f32[16,256]{1,0:T(8,128)S(1)} %get-tuple-element.58), channel_id=1, source_target_pairs={{0,4},{1,5},{2,6},{3,7},{4,0},{5,1},{6,2},{7,3},{8,12},{9,13},{10,... | collective-permute-start | bytes 49160 | tf_op jit(solution)/shard_map/ppermute | solution.py:660
  39.3 9.3 %collective-permute-start.12 = (f32[16,256]{1,0:T(8,128)S(1)}, f32[16,256]{1,0:T(8,128)S(1)}, u32[]{:S(2)}, u32[]{:S(2)}) collective-permute-start(f32[16,256]{1,0:T(8,128)S(1)} %get-tuple-element.59), channel_id=1, source_target_pairs={{0,5},{1,4},{2,7},{3,6},{4,1},{5,0},{6,3},{7,2},{8,13},{9,12},{10,... | collective-permute-start | bytes 49160 | tf_op jit(solution)/shard_map/ppermute | solution.py:660
  39.7 8.9 %collective-permute-start.13 = (f32[16,256]{1,0:T(8,128)S(1)}, f32[16,256]{1,0:T(8,128)S(1)}, u32[]{:S(2)}, u32[]{:S(2)}) collective-permute-start(f32[16,256]{1,0:T(8,128)S(1)} %get-tuple-element.60), channel_id=1, source_target_pairs={{0,6},{1,7},{2,4},{3,5},{4,2},{5,3},{6,0},{7,1},{8,14},{9,15},{10,... | collective-permute-start | bytes 49160 | tf_op jit(solution)/shard_map/ppermute | solution.py:660
  42.8 5.8 %collective-permute-start.14 = (f32[16,256]{1,0:T(8,128)S(1)}, f32[16,256]{1,0:T(8,128)S(1)}, u32[]{:S(2)}, u32[]{:S(2)}) collective-permute-start(f32[16,256]{1,0:T(8,128)S(1)} %get-tuple-element.61), channel_id=1, source_target_pairs={{0,7},{1,6},{2,5},{3,4},{4,3},{5,2},{6,1},{7,0},{8,15},{9,14},{10,... | collective-permute-start | bytes 49160 | tf_op jit(solution)/shard_map/ppermute | solution.py:660

commit v6 on v5

--- a/solution.py
+++ b/solution.py
@@ -56,6 +56,11 @@
     line_row = lax.axis_index("src") * (lax.axis_size("space") * own_rows)
     first = line_row + place * own_rows - HALO
     return lax.div(place, 2), lax.rem(place, 2), line_row, first
+
+
+def station_of(pay, events):
+    cell = pay[0:1, events : events + LANES].astype(jnp.int32)
+    return [cell[0, i] for i in range(3)]
 
 
 def fetch_kernel(*refs):
@@ -298,17 +303,18 @@
 SWEEP_UNROLL = 8
 
 
-def sweep_kernel(layers, own_rows, grid_rows, slots, chips, scal, *refs):
+def sweep_kernel(layers, own_rows, grid_rows, slots, chips, events, *refs):
     rows = own_rows + 2 * HALO
+    pays, refs = refs[:slots], refs[slots:]
     depth = refs[0].shape[-1]
     parts = depth // LANES
     vel_in, refs = refs[:chips], refs[chips:]
     times_out, final, speed, refs = refs[0], refs[1], refs[2], refs[3:]
-    cost, twice, one_half, ping, pong, acts, mask, flat = refs
+    cost, twice, one_half, ping, pong, acts, mask, flat, staged, sems = refs
     flat = Flat(flat, layers)
     line = lax.axis_index("src")
     chip, core, _, y_first = where_am_i(own_rows)
-    stations = [[scal[3 * slot + i] for i in range(3)] for slot in range(slots)]
+    stations = [station_of(pay, events) for pay in pays]
 
     for j in range(chips):
         for c in range(2):
@@ -357,11 +363,11 @@
                     value = jnp.where(y_first + i >= (tile_first + t) * TY, columns[t], value)
                 mask[slot, part, i] = value
 
-    def sweep(source, target, low, high, part, shift):
+    def sweep(source, target, low, high, part, shift, group):
         def body(row, size):
             grid = Grid(size, layers, depth)
             costs = get(cost, row, size), get(twice, row, size), get(one_half, row, size)
-            for slot in range(slots):
+            for slot in group:
                 field = get(source, row, size + 2, slot)
                 here = each(lambda f: f[1 : size + 1], field)
                 near_y = each(lambda f: jnp.minimum(f[:size], f[2:]), field)
@@ -384,7 +390,7 @@
                 )
 
         loop(low, high, SWEEP_ROWS, body, SWEEP_UNROLL if slots <= 4 else 1)
-        for slot in range(slots):
+        for slot in group:
             at_x, at_y, at_z = stations[slot]
             local = at_y - y_first
 
@@ -399,21 +405,27 @@
 
     fields = [ping, pong]
     last = ROUNDS * SWEEPS - 1
+    every = range(slots)
     for index in range(last):
-        sweep(fields[index % 2], fields[(index + 1) % 2], index, rows - index, index // SWEEPS, 1)
-    sweep(fields[last % 2], final, last, rows - last, last // SWEEPS, -last)
-
-    for slot in range(slots):
+        sweep(fields[index % 2], fields[(index + 1) % 2], index, rows - index, index // SWEEPS, 1, every)
+    copies = []
+    for slot in every:
+        sweep(fields[last % 2], final, last, rows - last, last // SWEEPS, -last, [slot])
         loop(0, own_rows, 4, lambda row, size: flat.put(row, size, get(final, row + ADJ_HALO, size, slot)))
         for place in range(layers):
-            times_out[line ^ slot, place] = flat.get_layer(place, own_rows)
+            staged[slot, place] = flat.get_layer(place, own_rows)
+        copies.append(pltpu.make_async_copy(staged.at[slot], times_out.at[line ^ slot], sems.at[slot]))
+        copies[-1].start()
+    for copy in copies:
+        copy.wait()
 
 
 ADJ_ROWS = 4
 ADJ_UNROLL = 8
 
 
-def adjoint_kernel(layers, own_rows, grid_rows, slots, scal, final, speed, count, delay_sum, *refs):
+def adjoint_kernel(layers, own_rows, grid_rows, slots, events, *refs):
+    pays, (final, speed, count, delay_sum), refs = refs[:slots], refs[slots : slots + 4], refs[slots + 4 :]
     depth = final.shape[-1]
     parts = depth // LANES
     kernel_out, refs = refs[:layers], refs[layers:]
@@ -421,7 +433,7 @@
     together = weight.shape[0]
     flat = Flat(flat, layers)
     y_first = where_am_i(own_rows)[3]
-    stations = [[scal[3 * slot + i] for i in range(3)] for slot in range(slots)]
+    stations = [station_of(pay, events) for pay in pays]
     straight = [Straight(layers, parts, stations[slot], grid_rows) for slot in range(slots)]
     shift = HALO - ADJ_HALO
     rows = own_rows + 2 * ADJ_HALO
@@ -599,7 +611,6 @@
     vel = [packed[0]] + [to_chip(packed[j], j) for j in range(1, chips)]
 
     pays, cells, _ = lax.optimization_barrier((pays, event_cells, packed[0]))
-    scal = jnp.concatenate([p[0, events : events + 3] for p in pays]).astype(jnp.int32)
     chunk = events
     while (1 + 2 * slots) * adj_rows * layers * chunk > EVENT_CHUNK * 2**11:
         chunk //= 2
@@ -612,19 +623,19 @@
         microseconds=3.0,
     )
 
-    scal, count, delay_sum = lax.optimization_barrier((scal, count, delay_sum))
+    pays, count, delay_sum = lax.optimization_barrier((pays, count, delay_sum))
 
     together = min(slots, 4)
     flat = scratch(depth // LANES, rows * layers, LANES)
     times, final, speed = call(
-        functools.partial(sweep_kernel, layers, own_rows, grid_rows, slots, chips),
+        functools.partial(sweep_kernel, layers, own_rows, grid_rows, slots, chips, events),
         "sweeps",
         [
             out(slots, layers, own_rows, depth),
             out(*field(slots, adj_rows)),
             out(*field(rows)),
         ],
-        [scal, *vel],
+        [*pays, *vel],
         [
             scratch(*field(rows)),
             scratch(*field(rows)),
@@ -634,14 +645,17 @@
             scratch(slots * ROUNDS, layers, LANES),
             scratch(slots, ROUNDS, rows, layers, LANES),
             flat,
+            scratch(slots, layers, own_rows, depth),
+            pltpu.SemaphoreType.DMA((slots,)),
         ],
+        hbm_out=(0,),
         microseconds=10.0,
     )
     kernel = call(
-        functools.partial(adjoint_kernel, layers, own_rows, grid_rows, slots),
+        functools.partial(adjoint_kernel, layers, own_rows, grid_rows, slots, events),
         "adjoint",
         [out(own_rows, depth)] * layers,
-        [scal, final, speed, count, delay_sum],
+        [*pays, final, speed, count, delay_sum],
         [
             scratch(*field(together, 6, adj_rows)),
             scratch(*field(together, adj_rows)),

time: 50.3 us -> 49.9 us (level)
  Pallas kernels: 15.4 us -> 14.3 us
  starting transfers between devices: 23.2 us -> 23.8 us
    pallas_call x7, Pallas kernels: 15.4 us -> 14.3 us  [call(): pl.pallas_call(body, out_shape=list(outs), in_specs=[spec(pltpu.HBM if i...]
    ppermute x7, starting transfers between devices: 9.92 us -> 10.5 us  [per_device(): lax.ppermute(kernel[m], 'space', [(i, i ^ m) for i in range(layers)])]
  transfers between devices with their start and end apart: 16 -> 16, of which waited for: 8 -> 9; matrix products, arithmetic and copies ran while one was open for 0% -> 0% of each run, Pallas kernels for 14% -> 13%
where the time goes in v6:
time: 49.9 us; the launch traced here: 49.3 us
  starting transfers between devices  23.8 us (48%)
  Pallas kernels  14.3 us (29%)
  waiting for transfers between devices  9.73 us (19%)
  between operations  0.87 us (2%)
  local copies, waits for them, and re-layouts  0.55 us (1%)
    pallas_call x7, Pallas kernels, call(): pl.pallas_call(body, out_shape=list(outs), in_specs=[spec(pltpu.HBM if i...  14.3 us
    ppermute x7, starting transfers between devices, per_device(): lax.ppermute(kernel[m], 'space', [(i, i ^ m) for i in range(layers)])  10.5 us
    all_to_all x1, starting transfers between devices, per_device(): lax.all_to_all(times.reshape(slots * layers, own_rows, depth), ('src', 's...  5.49 us
    ppermute x3, starting transfers between devices, to_line(): return lax.ppermute(array, 'src', [(i, i ^ j) for i in range(slots)])  3.94 us
    ppermute x7, waiting for transfers between devices, per_device(): lax.ppermute(kernel[m], 'space', [(i, i ^ m) for i in range(layers)])  3.91 us
    ppermute x3, starting transfers between devices, to_chip(): return lax.ppermute(array, 'space', [(i, i ^ 2 * j) for i in range(layers)])  3.67 us
    ppermute x3, waiting for transfers between devices, to_chip(): return lax.ppermute(array, 'space', [(i, i ^ 2 * j) for i in range(layers)])  3.21 us
    ppermute x3, waiting for transfers between devices, to_line(): return lax.ppermute(array, 'src', [(i, i ^ j) for i in range(slots)])  2.4 us
  transfers between devices with their start and end apart: 16, of which 9 were waited for; matrix products, arithmetic and copies ran while one was open for 0% of the time, Pallas kernels for 13%

profile of v6, /device:TPU:1, one launch (start us, length us, event | category | flops | bytes accessed | tf_op | source)
XLA Modules:
  0.0 49.3 jit_solution(6199826189223836092)
XLA Ops:
  0.6 0.0 copy-start.1
  0.6 0.1 collective-permute-start.4
  0.8 0.5 %copy-done.1 = s32[2,1,1,16]{3,2,1,0:T(1,128)S(1)} copy-done((s32[2,1,1,16]{3,2,1,0:T(1,128)S(1)}, s32[2,1,1,16]{3,2,1,0:T(1,128)}, u32[]{:S(2)}) %copy-start.1) | copy-done | bytes 152
  1.3 0.1 collective-permute-start
  1.4 1.1 %fetch.1 = (f32[512,256]{1,0:T(8,128)S(1)}, f32[1,2048]{1,0:T(1,128)S(1)}, s32[1,3]{1,0:T(1,128)S(1)}, s32[2,1,16]{2,1,0:T(1,128)S(1)}) custom-call(f32[512,256]{1,0:T(8,128)} %bitcast.10, f32[1,2048]{1,0:T(1,128)} %refs_1_.1, s32[1,3]{1,0:T(1,128)} %refs_2_.1, s32[2,1,16]{2,1,0:T(1,128)} %bitcast.11), custom_call_target="tpu_custom_call" | custom-call | bytes 3500000 | tf_op jit(solution)/shard_map/fetch/pallas_call | solution.py:32
  2.5 0.1 collective-permute-done.active_other
  2.6 3.6 %collective-permute-start.3 = (f32[1,2688]{1,0:T(1,128)S(1)}, f32[1,2688]{1,0:T(1,128)S(1)}, u32[]{:S(2)}, u32[]{:S(2)}) collective-permute-start(f32[1,2688]{1,0:T(1,128)S(1)} %head.1.refs_0_), channel_id=1, source_target_pairs={{0,24},{8,16},{16,8},{24,0},{1,25},{9,17},{17,9},{25,1},{2,26},{10... | collective-permute-start | bytes 32264 | tf_op jit(solution)/shard_map/ppermute | solution.py:567
  6.2 0.2 collective-permute-start.2
  6.4 0.1 collective-permute-start.1
  6.5 0.7 %collective-permute-done.3.refs_3_ = f32[1,2688]{1,0:T(1,128)S(1)} collective-permute-done((f32[1,2688]{1,0:T(1,128)S(1)}, f32[1,2688]{1,0:T(1,128)S(1)}, u32[]{:S(2)}, u32[]{:S(2)}) %collective-permute-start.3) | collective-permute-done | bytes 10784 | tf_op jit(solution)/shard_map/ppermute | solution.py:567
  7.2 1.5 %collective-permute-done.2.refs_2_ = f32[1,2688]{1,0:T(1,128)S(1)} collective-permute-done((f32[1,2688]{1,0:T(1,128)S(1)}, f32[1,2688]{1,0:T(1,128)S(1)}, u32[]{:S(2)}, u32[]{:S(2)}) %collective-permute-start.2) | collective-permute-done | bytes 10784 | tf_op jit(solution)/shard_map/ppermute | solution.py:567
  8.7 0.2 collective-permute-done.1.refs_1_
  8.9 0.0 collective-permute-done.4.other
  9.0 0.0 copy-start
  9.0 0.1 pack.1
  9.0 1.4 %collective-permute-start.5 = (f32[72,256]{1,0:T(8,128)S(1)}, f32[72,256]{1,0:T(8,128)S(1)}, u32[]{:S(2)}, u32[]{:S(2)}) collective-permute-start(f32[72,256]{1,0:T(8,128)S(1)} %get-tuple-element.52), channel_id=1, source_target_pairs={{0,2},{1,3},{2,0},{3,1},{4,6},{5,7},{6,4},{7,5},{8,10},{9,11},{10,... | collective-permute-start | bytes 221192 | tf_op jit(solution)/shard_map/ppermute | solution.py:570
  10.4 2.3 %collective-permute-start.6 = (f32[72,256]{1,0:T(8,128)S(1)}, f32[72,256]{1,0:T(8,128)S(1)}, u32[]{:S(2)}, u32[]{:S(2)}) collective-permute-start(f32[72,256]{1,0:T(8,128)S(1)} %get-tuple-element.53), channel_id=1, source_target_pairs={{0,4},{1,5},{2,6},{3,7},{4,0},{5,1},{6,2},{7,3},{8,12},{9,13},{10,... | collective-permute-start | bytes 221192 | tf_op jit(solution)/shard_map/ppermute | solution.py:570
  12.7 0.0 collective-permute-start.7
  12.7 0.0 copy-done
  12.7 2.3 %events.1 = (f32[208,256]{1,0:T(8,128)S(1)}, f32[4,208,256]{2,1,0:T(8,128)S(1)}) custom-call(s32[3,2048]{1,0:T(4,128)S(1)} %copy-done, f32[1,2688]{1,0:T(1,128)S(1)} %head.1.refs_0_, f32[1,2688]{1,0:T(1,128)S(1)} %collective-permute-done.1.refs_1_, f32[1,2688]{1,0:T(1,128)S(1)} %collective-permute-done.2.refs_2_, f32[1,2688]{1,0:T(1,128)S(1)} %collective-permute-done.3.refs_3_), custom_call_target="tpu_custom_call" | custom-call | bytes 10500000 | tf_op jit(solution)/shard_map/events/pallas_call | solution.py:32
  15.0 0.0 collective-permute-done.5.refs_5_
  15.0 0.2 collective-permute-done.6.refs_6_
  15.3 3.0 %collective-permute-done.7.refs_7_ = f32[72,256]{1,0:T(8,128)S(1)} collective-permute-done((f32[72,256]{1,0:T(8,128)S(1)}, f32[72,256]{1,0:T(8,128)S(1)}, u32[]{:S(2)}, u32[]{:S(2)}) %collective-permute-start.7) | collective-permute-done | bytes 73760 | tf_op jit(solution)/shard_map/ppermute | solution.py:570
  18.2 7.1 %sweeps.1 = (f32[4,8,16,256]{3,2,1,0:T(8,128)}, f32[4,26,8,256]{3,2,1,0:T(8,128)S(1)}, f32[32,8,256]{2,1,0:T(8,128)S(1)}) custom-call(f32[1,2688]{1,0:T(1,128)S(1)} %head.1.refs_0_, f32[1,2688]{1,0:T(1,128)S(1)} %collective-permute-done.1.refs_1_, f32[1,2688]{1,0:T(1,128)S(1)} %collective-permute-done.2.refs_2_, ...), custom_call_target="tpu_custom_call" | custom-call | bytes 35000000 | tf_op jit(solution)/shard_map/sweeps/pallas_call | solution.py:32
  25.4 5.5 %all-to-all-start = ((f32[32,16,256]{2,1,0:T(8,128)}), f32[32,16,256]{2,1,0:T(8,128)S(1)}, u32[]{:S(2)}, u32[]{:S(2)}) async-start(f32[32,16,256]{2,1,0:T(8,128)} %bitcast.4), calls=%async_computation | async-start | bytes 1048576 | tf_op jit(solution)/shard_map/all_to_all | solution.py:670
  30.9 2.8 %adjoint.1 = (f32[16,256]{1,0:T(8,128)S(1)}, f32[16,256]{1,0:T(8,128)S(1)}, f32[16,256]{1,0:T(8,128)S(1)}, f32[16,256]{1,0:T(8,128)S(1)}, f32[16,256]{1,0:T(8,12...) custom-call(f32[1,2688]{1,0:T(1,128)S(1)} %head.1.refs_0_, ...), custom_call_target="tpu_custom_call" | custom-call | bytes 24500000 | tf_op jit(solution)/shard_map/adjoint/pallas_call | solution.py:32
  33.7 0.5 %collective-permute-start.8 = (f32[16,256]{1,0:T(8,128)S(1)}, f32[16,256]{1,0:T(8,128)S(1)}, u32[]{:S(2)}, u32[]{:S(2)}) collective-permute-start(f32[16,256]{1,0:T(8,128)S(1)} %get-tuple-element.61), channel_id=1, source_target_pairs={{0,1},{1,0},{2,3},{3,2},{4,5},{5,4},{6,7},{7,6},{8,9},{9,8},{10,11... | collective-permute-start | bytes 49160 | tf_op jit(solution)/shard_map/ppermute | solution.py:674
  34.2 1.3 %collective-permute-start.9 = (f32[16,256]{1,0:T(8,128)S(1)}, f32[16,256]{1,0:T(8,128)S(1)}, u32[]{:S(2)}, u32[]{:S(2)}) collective-permute-start(f32[16,256]{1,0:T(8,128)S(1)} %get-tuple-element.62), channel_id=1, source_target_pairs={{0,2},{1,3},{2,0},{3,1},{4,6},{5,7},{6,4},{7,5},{8,10},{9,11},{10,... | collective-permute-start | bytes 49160 | tf_op jit(solution)/shard_map/ppermute | solution.py:674
  35.5 0.4 collective-permute-start.10
  35.9 2.3 %collective-permute-start.11 = (f32[16,256]{1,0:T(8,128)S(1)}, f32[16,256]{1,0:T(8,128)S(1)}, u32[]{:S(2)}, u32[]{:S(2)}) collective-permute-start(f32[16,256]{1,0:T(8,128)S(1)} %get-tuple-element.64), channel_id=1, source_target_pairs={{0,4},{1,5},{2,6},{3,7},{4,0},{5,1},{6,2},{7,3},{8,12},{9,13},{10,... | collective-permute-start | bytes 49160 | tf_op jit(solution)/shard_map/ppermute | solution.py:674
  38.2 0.4 collective-permute-start.12
  38.6 0.0 collective-permute-done.8.refs_1_
  38.6 3.2 %collective-permute-start.13 = (f32[16,256]{1,0:T(8,128)S(1)}, f32[16,256]{1,0:T(8,128)S(1)}, u32[]{:S(2)}, u32[]{:S(2)}) collective-permute-start(f32[16,256]{1,0:T(8,128)S(1)} %get-tuple-element.66), channel_id=1, source_target_pairs={{0,6},{1,7},{2,4},{3,5},{4,2},{5,3},{6,0},{7,1},{8,14},{9,15},{10,... | collective-permute-start | bytes 49160 | tf_op jit(solution)/shard_map/ppermute | solution.py:674
  41.8 0.0 collective-permute-done.9.refs_2_
  41.8 2.5 %collective-permute-start.14 = (f32[16,256]{1,0:T(8,128)S(1)}, f32[16,256]{1,0:T(8,128)S(1)}, u32[]{:S(2)}, u32[]{:S(2)}) collective-permute-start(f32[16,256]{1,0:T(8,128)S(1)} %get-tuple-element.67), channel_id=1, source_target_pairs={{0,7},{1,6},{2,5},{3,4},{4,3},{5,2},{6,1},{7,0},{8,15},{9,14},{10,... | collective-permute-start | bytes 49160 | tf_op jit(solution)/shard_map/ppermute | solution.py:674
  44.3 0.0 collective-permute-done.10.refs_3_
  44.3 2.4 %collective-permute-done.11.refs_4_ = f32[16,256]{1,0:T(8,128)S(1)} collective-permute-done((f32[16,256]{1,0:T(8,128)S(1)}, f32[16,256]{1,0:T(8,128)S(1)}, u32[]{:S(2)}, u32[]{:S(2)}) %collective-permute-start.11) | collective-permute-done | bytes 16416 | tf_op jit(solution)/shard_map/ppermute | solution.py:674
  46.7 1.5 %collective-permute-done.12.refs_5_ = f32[16,256]{1,0:T(8,128)S(1)} collective-permute-done((f32[16,256]{1,0:T(8,128)S(1)}, f32[16,256]{1,0:T(8,128)S(1)}, u32[]{:S(2)}, u32[]{:S(2)}) %collective-permute-start.12) | collective-permute-done | bytes 16416 | tf_op jit(solution)/shard_map/ppermute | solution.py:674
  48.2 0.0 collective-permute-done.13.refs_6_
  48.2 0.0 collective-permute-done.14.refs_7_
  48.2 0.1 all-to-all-done
  48.2 0.9 %join.1 = (f32[512,256]{1,0:T(8,128)}, f32[128,256]{1,0:T(8,128)}) custom-call(f32[512,256]{1,0:T(8,128)S(1)} %bitcast.8, f32[16,256]{1,0:T(8,128)S(1)} %get-tuple-element.60.refs_0_, f32[16,256]{1,0:T(8,128)S(1)} %collective-permute-done.8.refs_1_, f32[16,256]{1,0:T(8,128)S(1)} %collective-permute-done.9.refs_2_, ...), custom_call_target="tpu_custom_call" | custom-call | bytes 3500000 | tf_op jit(solution)/shard_map/join/pallas_call | solution.py:32
  (1 shorter events, 0.0 us)
Async XLA Ops:
  0.6 0.7 %copy-start.1 = (s32[2,1,1,16]{3,2,1,0:T(1,128)S(1)}, s32[2,1,1,16]{3,2,1,0:T(1,128)}, u32[]{:S(2)}) copy-start(s32[2,1,1,16]{3,2,1,0:T(1,128)} %param.9) | copy-start | bytes 388
  0.6 8.3 %collective-permute-start.4 = (f32[512,256]{1,0:T(8,128)}, f32[512,256]{1,0:T(8,128)S(1)}, u32[]{:S(2)}, u32[]{:S(2)}) collective-permute-start(f32[512,256]{1,0:T(8,128)} %bitcast.9), channel_id=1, source_target_pairs={{0,1},{1,0},{2,3},{3,2},{4,5},{5,4},{6,7},{7,6},{8,9},{9,8},{10,11... | collective-permute-start | bytes 1572872 | tf_op jit(solution)/shard_map/ppermute | solution.py:573
  1.3 1.3 %collective-permute-start = (s32[2,1,16]{2,1,0:T(1,128)S(1)}, s32[2,1,16]{2,1,0:T(1,128)S(1)}, u32[]{:S(2)}, u32[]{:S(2)}) collective-permute-start(s32[2,1,16]{2,1,0:T(1,128)S(1)} %bitcast.12), channel_id=1, source_target_pairs={{0,1},{1,0},{2,3},{3,2},{4,5},{5,4},{6,7},{7,6},{8,9},{9,8},{10,11... | collective-permute-start | bytes 392 | tf_op jit(solution)/shard_map/ppermute | solution.py:573
  2.6 4.6 %collective-permute-start.3 = (f32[1,2688]{1,0:T(1,128)S(1)}, f32[1,2688]{1,0:T(1,128)S(1)}, u32[]{:S(2)}, u32[]{:S(2)}) collective-permute-start(f32[1,2688]{1,0:T(1,128)S(1)} %head.1.refs_0_), channel_id=1, source_target_pairs={{0,24},{8,16},{16,8},{24,0},{1,25},{9,17},{17,9},{25,1},{2,26},{10... | collective-permute-start | bytes 32264 | tf_op jit(solution)/shard_map/ppermute | solution.py:567
  6.2 2.5 %collective-permute-start.2 = (f32[1,2688]{1,0:T(1,128)S(1)}, f32[1,2688]{1,0:T(1,128)S(1)}, u32[]{:S(2)}, u32[]{:S(2)}) collective-permute-start(f32[1,2688]{1,0:T(1,128)S(1)} %head.1.refs_0_), channel_id=1, source_target_pairs={{0,16},{8,24},{16,0},{24,8},{1,17},{9,25},{17,1},{25,9},{2,18},{10... | collective-permute-start | bytes 32264 | tf_op jit(solution)/shard_map/ppermute | solution.py:567
  6.4 2.5 %collective-permute-start.1 = (f32[1,2688]{1,0:T(1,128)S(1)}, f32[1,2688]{1,0:T(1,128)S(1)}, u32[]{:S(2)}, u32[]{:S(2)}) collective-permute-start(f32[1,2688]{1,0:T(1,128)S(1)} %head.1.refs_0_), channel_id=1, source_target_pairs={{0,8},{8,0},{16,24},{24,16},{1,9},{9,1},{17,25},{25,17},{2,10},{10... | collective-permute-start | bytes 32264 | tf_op jit(solution)/shard_map/ppermute | solution.py:567
  9.0 3.7 %copy-start = (s32[3,2048]{1,0:T(4,128)S(1)}, s32[3,2048]{1,0:T(4,128)}, u32[]{:S(2)}) copy-start(s32[3,2048]{1,0:T(4,128)} %cells) | copy-start | bytes 73732
  9.0 6.0 %collective-permute-start.5 = (f32[72,256]{1,0:T(8,128)S(1)}, f32[72,256]{1,0:T(8,128)S(1)}, u32[]{:S(2)}, u32[]{:S(2)}) collective-permute-start(f32[72,256]{1,0:T(8,128)S(1)} %get-tuple-element.52), channel_id=1, source_target_pairs={{0,2},{1,3},{2,0},{3,1},{4,6},{5,7},{6,4},{7,5},{8,10},{9,11},{10,... | collective-permute-start | bytes 221192 | tf_op jit(solution)/shard_map/ppermute | solution.py:570
  10.4 4.9 %collective-permute-start.6 = (f32[72,256]{1,0:T(8,128)S(1)}, f32[72,256]{1,0:T(8,128)S(1)}, u32[]{:S(2)}, u32[]{:S(2)}) collective-permute-start(f32[72,256]{1,0:T(8,128)S(1)} %get-tuple-element.53), channel_id=1, source_target_pairs={{0,4},{1,5},{2,6},{3,7},{4,0},{5,1},{6,2},{7,3},{8,12},{9,13},{10,... | collective-permute-start | bytes 221192 | tf_op jit(solution)/shard_map/ppermute | solution.py:570
  12.7 5.6 %collective-permute-start.7 = (f32[72,256]{1,0:T(8,128)S(1)}, f32[72,256]{1,0:T(8,128)S(1)}, u32[]{:S(2)}, u32[]{:S(2)}) collective-permute-start(f32[72,256]{1,0:T(8,128)S(1)} %get-tuple-element.54), channel_id=1, source_target_pairs={{0,6},{1,7},{2,4},{3,5},{4,2},{5,3},{6,0},{7,1},{8,14},{9,15},{10,... | collective-permute-start | bytes 221192 | tf_op jit(solution)/shard_map/ppermute | solution.py:570
  25.4 22.8 %all-to-all-start = ((f32[32,16,256]{2,1,0:T(8,128)}), f32[32,16,256]{2,1,0:T(8,128)S(1)}, u32[]{:S(2)}, u32[]{:S(2)}) async-start(f32[32,16,256]{2,1,0:T(8,128)} %bitcast.4), calls=%async_computation | async-start | bytes 1048576 | tf_op jit(solution)/shard_map/all_to_all | solution.py:670
  33.7 4.9 %collective-permute-start.8 = (f32[16,256]{1,0:T(8,128)S(1)}, f32[16,256]{1,0:T(8,128)S(1)}, u32[]{:S(2)}, u32[]{:S(2)}) collective-permute-start(f32[16,256]{1,0:T(8,128)S(1)} %get-tuple-element.61), channel_id=1, source_target_pairs={{0,1},{1,0},{2,3},{3,2},{4,5},{5,4},{6,7},{7,6},{8,9},{9,8},{10,11... | collective-permute-start | bytes 49160 | tf_op jit(solution)/shard_map/ppermute | solution.py:674
  34.2 7.6 %collective-permute-start.9 = (f32[16,256]{1,0:T(8,128)S(1)}, f32[16,256]{1,0:T(8,128)S(1)}, u32[]{:S(2)}, u32[]{:S(2)}) collective-permute-start(f32[16,256]{1,0:T(8,128)S(1)} %get-tuple-element.62), channel_id=1, source_target_pairs={{0,2},{1,3},{2,0},{3,1},{4,6},{5,7},{6,4},{7,5},{8,10},{9,11},{10,... | collective-permute-start | bytes 49160 | tf_op jit(solution)/shard_map/ppermute | solution.py:674
  35.5 8.7 %collective-permute-start.10 = (f32[16,256]{1,0:T(8,128)S(1)}, f32[16,256]{1,0:T(8,128)S(1)}, u32[]{:S(2)}, u32[]{:S(2)}) collective-permute-start(f32[16,256]{1,0:T(8,128)S(1)} %get-tuple-element.63), channel_id=1, source_target_pairs={{0,3},{1,2},{2,1},{3,0},{4,7},{5,6},{6,5},{7,4},{8,11},{9,10},{10,... | collective-permute-start | bytes 49160 | tf_op jit(solution)/shard_map/ppermute | solution.py:674
  35.9 10.8 %collective-permute-start.11 = (f32[16,256]{1,0:T(8,128)S(1)}, f32[16,256]{1,0:T(8,128)S(1)}, u32[]{:S(2)}, u32[]{:S(2)}) collective-permute-start(f32[16,256]{1,0:T(8,128)S(1)} %get-tuple-element.64), channel_id=1, source_target_pairs={{0,4},{1,5},{2,6},{3,7},{4,0},{5,1},{6,2},{7,3},{8,12},{9,13},{10,... | collective-permute-start | bytes 49160 | tf_op jit(solution)/shard_map/ppermute | solution.py:674
  38.2 9.9 %collective-permute-start.12 = (f32[16,256]{1,0:T(8,128)S(1)}, f32[16,256]{1,0:T(8,128)S(1)}, u32[]{:S(2)}, u32[]{:S(2)}) collective-permute-start(f32[16,256]{1,0:T(8,128)S(1)} %get-tuple-element.65), channel_id=1, source_target_pairs={{0,5},{1,4},{2,7},{3,6},{4,1},{5,0},{6,3},{7,2},{8,13},{9,12},{10,... | collective-permute-start | bytes 49160 | tf_op jit(solution)/shard_map/ppermute | solution.py:674
  38.6 9.6 %collective-permute-start.13 = (f32[16,256]{1,0:T(8,128)S(1)}, f32[16,256]{1,0:T(8,128)S(1)}, u32[]{:S(2)}, u32[]{:S(2)}) collective-permute-start(f32[16,256]{1,0:T(8,128)S(1)} %get-tuple-element.66), channel_id=1, source_target_pairs={{0,6},{1,7},{2,4},{3,5},{4,2},{5,3},{6,0},{7,1},{8,14},{9,15},{10,... | collective-permute-start | bytes 49160 | tf_op jit(solution)/shard_map/ppermute | solution.py:674
  41.8 6.4 %collective-permute-start.14 = (f32[16,256]{1,0:T(8,128)S(1)}, f32[16,256]{1,0:T(8,128)S(1)}, u32[]{:S(2)}, u32[]{:S(2)}) collective-permute-start(f32[16,256]{1,0:T(8,128)S(1)} %get-tuple-element.67), channel_id=1, source_target_pairs={{0,7},{1,6},{2,5},{3,4},{4,3},{5,2},{6,1},{7,0},{8,15},{9,14},{10,... | collective-permute-start | bytes 49160 | tf_op jit(solution)/shard_map/ppermute | solution.py:674

commit v7 on v6

--- a/solution.py
+++ b/solution.py
@@ -109,10 +109,22 @@
 EVENT_CHUNK = 2048
 
 
-def scatter_kernel(layers, own_rows, events, cells, *refs):
-    slots = len(refs) - 3
-    pays, count, delay_sum, left = refs[:slots], refs[slots], refs[slots + 1], refs[slots + 2]
-    first_row = where_am_i(own_rows)[3] + HALO - ADJ_HALO
+def scatter_kernel(layers, own_rows, grid_rows, events, cells, *refs):
+    slots = len(refs) - 4
+    pays, (count, delay_sum, start, left) = refs[:slots], refs[slots:]
+    y_first = where_am_i(own_rows)[3]
+    first_row = y_first + HALO - ADJ_HALO
+    rows, parts = own_rows + 2 * HALO, start.shape[-1] // LANES
+
+    straight = [Straight(layers, parts, station_of(pays[slot], events), grid_rows) for slot in range(slots)]
+
+    def fill(row, size):
+        for i in range(size):
+            for slot in range(slots):
+                put(start, row + i, 1, straight[slot].row(y_first - 1 + row + i), slot)
+
+    loop(0, rows + 2, 4, fill)
+
     height, width = count.shape
     chunk = left.shape[1]
     steps = events // chunk
@@ -291,24 +303,24 @@
     first_gap = middle - lowest
     second_gap = highest - lowest
     square = first_gap * first_gap
-    single = lowest + cost
-    double = lowest + 0.5 * (first_gap + root_of(twice - square))
+    double = 0.5 * (first_gap + root_of(twice - square))
     rest = square + second_gap * (second_gap - first_gap)
     root = root_of(one_half - rest)
-    triple = lowest + ((first_gap + second_gap) * (1.0 / 3.0) + root * (math.sqrt(2.0) / 3.0))
-    return jnp.where(single <= middle, single, jnp.where(double <= highest, double, triple))
-
-
-SWEEP_ROWS = 4
-SWEEP_UNROLL = 8
+    triple = (first_gap + second_gap) * (1.0 / 3.0) + root * (math.sqrt(2.0) / 3.0)
+    over = jnp.where(double <= second_gap, double, triple)
+    return lowest + jnp.where(cost <= first_gap, cost, over)
+
+
+SWEEP_ROWS = 2
+SWEEP_UNROLL = 16
 
 
 def sweep_kernel(layers, own_rows, grid_rows, slots, chips, events, *refs):
     rows = own_rows + 2 * HALO
-    pays, refs = refs[:slots], refs[slots:]
-    depth = refs[0].shape[-1]
+    pays, start, refs = refs[:slots], refs[slots], refs[slots + 1 :]
+    depth = start.shape[-1]
     parts = depth // LANES
-    vel_in, refs = refs[:chips], refs[chips:]
+    vel_in, refs = refs[:chips][::-1], refs[chips:]
     times_out, final, speed, refs = refs[0], refs[1], refs[2], refs[3:]
     cost, twice, one_half, ping, pong, acts, mask, flat, staged, sems = refs
     flat = Flat(flat, layers)
@@ -336,15 +348,6 @@
         put(one_half, row, size, each(lambda f: 1.5 * (f * f), slow))
 
     loop(0, rows, 4, prepare)
-
-    straight = [Straight(layers, parts, stations[slot], grid_rows) for slot in range(slots)]
-
-    def fill(row, size):
-        for i in range(size):
-            for slot in range(slots):
-                put(ping, row + i, 1, straight[slot].row(y_first - 1 + row + i), slot)
-
-    loop(0, rows + 2, 4, fill)
 
     lane_iota = lax.broadcasted_iota(jnp.int32, (layers, LANES), 1)
     tile_first = (y_first + TY) // TY - 1
@@ -403,14 +406,14 @@
                 here = slot, pl.ds(local + shift, 1)
                 target[here] = jnp.where(there, 0.0, target[here])
 
-    fields = [ping, pong]
+    fields = [start] + [(pong, ping)[i % 2] for i in range(ROUNDS * SWEEPS - 1)]
     last = ROUNDS * SWEEPS - 1
     every = range(slots)
     for index in range(last):
-        sweep(fields[index % 2], fields[(index + 1) % 2], index, rows - index, index // SWEEPS, 1, every)
+        sweep(fields[index], fields[index + 1], index, rows - index, index // SWEEPS, 1, every)
     copies = []
     for slot in every:
-        sweep(fields[last % 2], final, last, rows - last, last // SWEEPS, -last, [slot])
+        sweep(fields[last], final, last, rows - last, last // SWEEPS, -last, [slot])
         loop(0, own_rows, 4, lambda row, size: flat.put(row, size, get(final, row + ADJ_HALO, size, slot)))
         for place in range(layers):
             staged[slot, place] = flat.get_layer(place, own_rows)
@@ -608,22 +611,26 @@
         [out(height, depth)] * chips,
         [layer, other, *pays],
     )
-    vel = [packed[0]] + [to_chip(packed[j], j) for j in range(1, chips)]
+    vel = [to_chip(packed[j], j) for j in range(chips - 1, 0, -1)] + [packed[0]]
 
     pays, cells, _ = lax.optimization_barrier((pays, event_cells, packed[0]))
     chunk = events
     while (1 + 2 * slots) * adj_rows * layers * chunk > EVENT_CHUNK * 2**11:
         chunk //= 2
-    count, delay_sum = call(
-        functools.partial(scatter_kernel, layers, own_rows, events),
+    count, delay_sum, start = call(
+        functools.partial(scatter_kernel, layers, own_rows, grid_rows, events),
         "events",
-        [out(adj_rows * layers, depth), out(slots, adj_rows * layers, depth)],
+        [
+            out(adj_rows * layers, depth),
+            out(slots, adj_rows * layers, depth),
+            out(*field(slots, rows + 2)),
+        ],
         [cells, *pays],
         [pltpu.VMEM(((1 + 2 * slots) * adj_rows * layers, chunk), jnp.bfloat16)],
         microseconds=3.0,
     )
 
-    pays, count, delay_sum = lax.optimization_barrier((pays, count, delay_sum))
+    pays, count, delay_sum, start = lax.optimization_barrier((pays, count, delay_sum, start))
 
     together = min(slots, 4)
     flat = scratch(depth // LANES, rows * layers, LANES)
@@ -635,7 +642,7 @@
             out(*field(slots, adj_rows)),
             out(*field(rows)),
         ],
-        [*pays, *vel],
+        [*pays, start, *vel],
         [
             scratch(*field(rows)),
             scratch(*field(rows)),

time: 49.9 us -> 49.1 us (0.984)
  waiting for transfers between devices: 9.73 us -> 10.5 us
  starting transfers between devices: 23.8 us -> 23.2 us
  local copies, waits for them, and re-layouts: 0.55 us -> 0.01 us
    all_to_all x1, starting transfers between devices: 5.49 us -> 4.68 us  [per_device(): lax.all_to_all(times.reshape(slots * layers, own_rows, depth), ('src', 's...]
    unnamed x4 -> x2, local copies, waits for them, and re-layouts: 0.55 us -> 0.01 us
  transfers between devices with their start and end apart: 16 -> 16, of which waited for: 9 -> 8; matrix products, arithmetic and copies ran while one was open for 0% -> 0% of each run, Pallas kernels for 13% -> 13%
where the time goes in v7:
time: 49.1 us; the launch traced here: 48.6 us
  starting transfers between devices  23.2 us (47%)
  Pallas kernels  14 us (29%)
  waiting for transfers between devices  10.5 us (21%)
  between operations  0.87 us (2%)
    pallas_call x7, Pallas kernels, call(): pl.pallas_call(body, out_shape=list(outs), in_specs=[spec(pltpu.HBM if i...  14 us
    ppermute x7, starting transfers between devices, per_device(): lax.ppermute(kernel[m], 'space', [(i, i ^ m) for i in range(layers)])  10.5 us
    all_to_all x1, starting transfers between devices, per_device(): lax.all_to_all(times.reshape(slots * layers, own_rows, depth), ('src', 's...  4.68 us
    ppermute x7, waiting for transfers between devices, per_device(): lax.ppermute(kernel[m], 'space', [(i, i ^ m) for i in range(layers)])  3.91 us
    ppermute x3, starting transfers between devices, to_chip(): return lax.ppermute(array, 'space', [(i, i ^ 2 * j) for i in range(layers)])  3.75 us
    ppermute x3, starting transfers between devices, to_line(): return lax.ppermute(array, 'src', [(i, i ^ j) for i in range(slots)])  3.65 us
    ppermute x3, waiting for transfers between devices, to_chip(): return lax.ppermute(array, 'space', [(i, i ^ 2 * j) for i in range(layers)])  3.59 us
    ppermute x3, waiting for transfers between devices, to_line(): return lax.ppermute(array, 'src', [(i, i ^ j) for i in range(slots)])  2.41 us
  transfers between devices with their start and end apart: 16, of which 8 were waited for; matrix products, arithmetic and copies ran while one was open for 0% of the time, Pallas kernels for 13%

profile of v7, /device:TPU:1, one launch (start us, length us, event | category | flops | bytes accessed | tf_op | source)
XLA Modules:
  0.0 48.6 jit_solution(2201198688057179076)
XLA Ops:
  0.6 0.0 copy-start
  0.6 0.1 collective-permute-start.4
  0.8 0.5 collective-permute-start
  1.2 1.1 %fetch.1 = (f32[512,256]{1,0:T(8,128)S(1)}, f32[1,2048]{1,0:T(1,128)S(1)}, s32[1,3]{1,0:T(1,128)S(1)}, s32[2,1,16]{2,1,0:T(1,128)S(1)}) custom-call(f32[512,256]{1,0:T(8,128)} %bitcast.10, f32[1,2048]{1,0:T(1,128)} %refs_1_.1, s32[1,3]{1,0:T(1,128)} %refs_2_.1, s32[2,1,16]{2,1,0:T(1,128)} %bitcast.12), custom_call_target="tpu_custom_call" | custom-call | bytes 3500000 | tf_op jit(solution)/shard_map/fetch/pallas_call | solution.py:32
  2.3 0.5 %collective-permute-done.active_other = s32[2,1,16]{2,1,0:T(1,128)S(1)} collective-permute-done((s32[2,1,16]{2,1,0:T(1,128)}, s32[2,1,16]{2,1,0:T(1,128)S(1)}, u32[]{:S(2)}, u32[]{:S(2)}) %collective-permute-start) | collective-permute-done | bytes 160 | tf_op jit(solution)/shard_map/ppermute | solution.py:576
  2.8 3.3 %collective-permute-start.3 = (f32[1,2688]{1,0:T(1,128)S(1)}, f32[1,2688]{1,0:T(1,128)S(1)}, u32[]{:S(2)}, u32[]{:S(2)}) collective-permute-start(f32[1,2688]{1,0:T(1,128)S(1)} %head.1.refs_0_), channel_id=1, source_target_pairs={{0,24},{8,16},{16,8},{24,0},{1,25},{9,17},{17,9},{25,1},{2,26},{10... | collective-permute-start | bytes 32264 | tf_op jit(solution)/shard_map/ppermute | solution.py:570
  6.1 0.2 collective-permute-start.2
  6.4 0.1 collective-permute-start.1
  6.5 0.7 %collective-permute-done.3.refs_3_ = f32[1,2688]{1,0:T(1,128)S(1)} collective-permute-done((f32[1,2688]{1,0:T(1,128)S(1)}, f32[1,2688]{1,0:T(1,128)S(1)}, u32[]{:S(2)}, u32[]{:S(2)}) %collective-permute-start.3) | collective-permute-done | bytes 10784 | tf_op jit(solution)/shard_map/ppermute | solution.py:570
  7.2 1.5 %collective-permute-done.2.refs_2_ = f32[1,2688]{1,0:T(1,128)S(1)} collective-permute-done((f32[1,2688]{1,0:T(1,128)S(1)}, f32[1,2688]{1,0:T(1,128)S(1)}, u32[]{:S(2)}, u32[]{:S(2)}) %collective-permute-start.2) | collective-permute-done | bytes 10784 | tf_op jit(solution)/shard_map/ppermute | solution.py:570
  8.7 0.2 collective-permute-done.1.refs_1_
  8.9 0.0 collective-permute-done.4.other
  8.9 0.1 pack.1
  9.0 3.4 %collective-permute-start.5 = (f32[72,256]{1,0:T(8,128)S(1)}, f32[72,256]{1,0:T(8,128)S(1)}, u32[]{:S(2)}, u32[]{:S(2)}) collective-permute-start(f32[72,256]{1,0:T(8,128)S(1)} %get-tuple-element.56), channel_id=1, source_target_pairs={{0,6},{1,7},{2,4},{3,5},{4,2},{5,3},{6,0},{7,1},{8,14},{9,15},{10,... | collective-permute-start | bytes 221192 | tf_op jit(solution)/shard_map/ppermute | solution.py:573
  12.3 0.0 collective-permute-start.6
  12.3 0.4 collective-permute-start.7
  12.7 0.0 copy-done
  12.7 2.6 %events.1 = (f32[208,256]{1,0:T(8,128)S(1)}, f32[4,208,256]{2,1,0:T(8,128)S(1)}, f32[4,34,8,256]{3,2,1,0:T(8,128)S(1)}) custom-call(s32[3,2048]{1,0:T(4,128)S(1)} %copy-done, f32[1,2688]{1,0:T(1,128)S(1)} %head.1.refs_0_, f32[1,2688]{1,0:T(1,128)S(1)} %collective-permute-done.1.refs_1_, f32[1,2688]{1,0:T(1,128)S(1)} %collective-permute-done.2.refs_2_, ...), custom_call_target="tpu_custom_call" | custom-call | bytes 10500000 | tf_op jit(solution)/shard_map/events/pallas_call | solution.py:32
  15.3 0.0 collective-permute-done.5.refs_5_
  15.4 3.6 %collective-permute-done.6.refs_6_ = f32[72,256]{1,0:T(8,128)S(1)} collective-permute-done((f32[72,256]{1,0:T(8,128)S(1)}, f32[72,256]{1,0:T(8,128)S(1)}, u32[]{:S(2)}, u32[]{:S(2)}) %collective-permute-start.6) | collective-permute-done | bytes 73760 | tf_op jit(solution)/shard_map/ppermute | solution.py:573
  18.9 0.0 collective-permute-done.7.refs_7_
  18.9 6.6 %sweeps.1 = (f32[4,8,16,256]{3,2,1,0:T(8,128)}, f32[4,26,8,256]{3,2,1,0:T(8,128)S(1)}, f32[32,8,256]{2,1,0:T(8,128)S(1)}) custom-call(f32[1,2688]{1,0:T(1,128)S(1)} %head.1.refs_0_, f32[1,2688]{1,0:T(1,128)S(1)} %collective-permute-done.1.refs_1_, f32[1,2688]{1,0:T(1,128)S(1)} %collective-permute-done.2.refs_2_, ...), custom_call_target="tpu_custom_call" | custom-call | bytes 35000000 | tf_op jit(solution)/shard_map/sweeps/pallas_call | solution.py:32
  25.5 4.7 %all-to-all-start = ((f32[32,16,256]{2,1,0:T(8,128)}), f32[32,16,256]{2,1,0:T(8,128)S(1)}, u32[]{:S(2)}, u32[]{:S(2)}) async-start(f32[32,16,256]{2,1,0:T(8,128)} %bitcast.4), calls=%async_computation | async-start | bytes 1048576 | tf_op jit(solution)/shard_map/all_to_all | solution.py:677
  30.2 2.8 %adjoint.1 = (f32[16,256]{1,0:T(8,128)S(1)}, f32[16,256]{1,0:T(8,128)S(1)}, f32[16,256]{1,0:T(8,128)S(1)}, f32[16,256]{1,0:T(8,128)S(1)}, f32[16,256]{1,0:T(8,12...) custom-call(f32[1,2688]{1,0:T(1,128)S(1)} %head.1.refs_0_, ...), custom_call_target="tpu_custom_call" | custom-call | bytes 24500000 | tf_op jit(solution)/shard_map/adjoint/pallas_call | solution.py:32
  33.0 0.5 %collective-permute-start.8 = (f32[16,256]{1,0:T(8,128)S(1)}, f32[16,256]{1,0:T(8,128)S(1)}, u32[]{:S(2)}, u32[]{:S(2)}) collective-permute-start(f32[16,256]{1,0:T(8,128)S(1)} %get-tuple-element.65), channel_id=1, source_target_pairs={{0,1},{1,0},{2,3},{3,2},{4,5},{5,4},{6,7},{7,6},{8,9},{9,8},{10,11... | collective-permute-start | bytes 49160 | tf_op jit(solution)/shard_map/ppermute | solution.py:681
  33.5 1.3 %collective-permute-start.9 = (f32[16,256]{1,0:T(8,128)S(1)}, f32[16,256]{1,0:T(8,128)S(1)}, u32[]{:S(2)}, u32[]{:S(2)}) collective-permute-start(f32[16,256]{1,0:T(8,128)S(1)} %get-tuple-element.66), channel_id=1, source_target_pairs={{0,2},{1,3},{2,0},{3,1},{4,6},{5,7},{6,4},{7,5},{8,10},{9,11},{10,... | collective-permute-start | bytes 49160 | tf_op jit(solution)/shard_map/ppermute | solution.py:681
  34.8 0.4 collective-permute-start.10
  35.2 2.3 %collective-permute-start.11 = (f32[16,256]{1,0:T(8,128)S(1)}, f32[16,256]{1,0:T(8,128)S(1)}, u32[]{:S(2)}, u32[]{:S(2)}) collective-permute-start(f32[16,256]{1,0:T(8,128)S(1)} %get-tuple-element.68), channel_id=1, source_target_pairs={{0,4},{1,5},{2,6},{3,7},{4,0},{5,1},{6,2},{7,3},{8,12},{9,13},{10,... | collective-permute-start | bytes 49160 | tf_op jit(solution)/shard_map/ppermute | solution.py:681
  37.5 0.4 collective-permute-start.12
  37.9 0.0 collective-permute-done.8.refs_1_
  37.9 3.2 %collective-permute-start.13 = (f32[16,256]{1,0:T(8,128)S(1)}, f32[16,256]{1,0:T(8,128)S(1)}, u32[]{:S(2)}, u32[]{:S(2)}) collective-permute-start(f32[16,256]{1,0:T(8,128)S(1)} %get-tuple-element.70), channel_id=1, source_target_pairs={{0,6},{1,7},{2,4},{3,5},{4,2},{5,3},{6,0},{7,1},{8,14},{9,15},{10,... | collective-permute-start | bytes 49160 | tf_op jit(solution)/shard_map/ppermute | solution.py:681
  41.1 0.0 collective-permute-done.9.refs_2_
  41.1 2.5 %collective-permute-start.14 = (f32[16,256]{1,0:T(8,128)S(1)}, f32[16,256]{1,0:T(8,128)S(1)}, u32[]{:S(2)}, u32[]{:S(2)}) collective-permute-start(f32[16,256]{1,0:T(8,128)S(1)} %get-tuple-element.71), channel_id=1, source_target_pairs={{0,7},{1,6},{2,5},{3,4},{4,3},{5,2},{6,1},{7,0},{8,15},{9,14},{10,... | collective-permute-start | bytes 49160 | tf_op jit(solution)/shard_map/ppermute | solution.py:681
  43.6 0.0 collective-permute-done.10.refs_3_
  43.6 2.4 %collective-permute-done.11.refs_4_ = f32[16,256]{1,0:T(8,128)S(1)} collective-permute-done((f32[16,256]{1,0:T(8,128)S(1)}, f32[16,256]{1,0:T(8,128)S(1)}, u32[]{:S(2)}, u32[]{:S(2)}) %collective-permute-start.11) | collective-permute-done | bytes 16416 | tf_op jit(solution)/shard_map/ppermute | solution.py:681
  46.0 1.5 %collective-permute-done.12.refs_5_ = f32[16,256]{1,0:T(8,128)S(1)} collective-permute-done((f32[16,256]{1,0:T(8,128)S(1)}, f32[16,256]{1,0:T(8,128)S(1)}, u32[]{:S(2)}, u32[]{:S(2)}) %collective-permute-start.12) | collective-permute-done | bytes 16416 | tf_op jit(solution)/shard_map/ppermute | solution.py:681
  47.5 0.0 collective-permute-done.13.refs_6_
  47.5 0.0 collective-permute-done.14.refs_7_
  47.5 0.1 all-to-all-done
  47.5 0.9 %join.1 = (f32[512,256]{1,0:T(8,128)}, f32[128,256]{1,0:T(8,128)}) custom-call(f32[512,256]{1,0:T(8,128)S(1)} %bitcast.8, f32[16,256]{1,0:T(8,128)S(1)} %get-tuple-element.64.refs_0_, f32[16,256]{1,0:T(8,128)S(1)} %collective-permute-done.8.refs_1_, f32[16,256]{1,0:T(8,128)S(1)} %collective-permute-done.9.refs_2_, ...), custom_call_target="tpu_custom_call" | custom-call | bytes 3500000 | tf_op jit(solution)/shard_map/join/pallas_call | solution.py:32
  (1 shorter events, 0.0 us)
Async XLA Ops:
  0.6 12.1 %copy-start = (s32[3,2048]{1,0:T(4,128)S(1)}, s32[3,2048]{1,0:T(4,128)}, u32[]{:S(2)}) copy-start(s32[3,2048]{1,0:T(4,128)} %cells) | copy-start | bytes 73732
  0.6 8.3 %collective-permute-start.4 = (f32[512,256]{1,0:T(8,128)}, f32[512,256]{1,0:T(8,128)S(1)}, u32[]{:S(2)}, u32[]{:S(2)}) collective-permute-start(f32[512,256]{1,0:T(8,128)} %bitcast.9), channel_id=1, source_target_pairs={{0,1},{1,0},{2,3},{3,2},{4,5},{5,4},{6,7},{7,6},{8,9},{9,8},{10,11... | collective-permute-start | bytes 1572872 | tf_op jit(solution)/shard_map/ppermute | solution.py:576
  0.8 2.1 %collective-permute-start = (s32[2,1,16]{2,1,0:T(1,128)}, s32[2,1,16]{2,1,0:T(1,128)S(1)}, u32[]{:S(2)}, u32[]{:S(2)}) collective-permute-start(s32[2,1,16]{2,1,0:T(1,128)} %bitcast.11), channel_id=1, source_target_pairs={{0,1},{1,0},{2,3},{3,2},{4,5},{5,4},{6,7},{7,6},{8,9},{9,8},{10,11... | collective-permute-start | bytes 392 | tf_op jit(solution)/shard_map/ppermute | solution.py:576
  2.8 4.4 %collective-permute-start.3 = (f32[1,2688]{1,0:T(1,128)S(1)}, f32[1,2688]{1,0:T(1,128)S(1)}, u32[]{:S(2)}, u32[]{:S(2)}) collective-permute-start(f32[1,2688]{1,0:T(1,128)S(1)} %head.1.refs_0_), channel_id=1, source_target_pairs={{0,24},{8,16},{16,8},{24,0},{1,25},{9,17},{17,9},{25,1},{2,26},{10... | collective-permute-start | bytes 32264 | tf_op jit(solution)/shard_map/ppermute | solution.py:570
  6.1 2.5 %collective-permute-start.2 = (f32[1,2688]{1,0:T(1,128)S(1)}, f32[1,2688]{1,0:T(1,128)S(1)}, u32[]{:S(2)}, u32[]{:S(2)}) collective-permute-start(f32[1,2688]{1,0:T(1,128)S(1)} %head.1.refs_0_), channel_id=1, source_target_pairs={{0,16},{8,24},{16,0},{24,8},{1,17},{9,25},{17,1},{25,9},{2,18},{10... | collective-permute-start | bytes 32264 | tf_op jit(solution)/shard_map/ppermute | solution.py:570
  6.4 2.5 %collective-permute-start.1 = (f32[1,2688]{1,0:T(1,128)S(1)}, f32[1,2688]{1,0:T(1,128)S(1)}, u32[]{:S(2)}, u32[]{:S(2)}) collective-permute-start(f32[1,2688]{1,0:T(1,128)S(1)} %head.1.refs_0_), channel_id=1, source_target_pairs={{0,8},{8,0},{16,24},{24,16},{1,9},{9,1},{17,25},{25,17},{2,10},{10... | collective-permute-start | bytes 32264 | tf_op jit(solution)/shard_map/ppermute | solution.py:570
  9.0 6.4 %collective-permute-start.5 = (f32[72,256]{1,0:T(8,128)S(1)}, f32[72,256]{1,0:T(8,128)S(1)}, u32[]{:S(2)}, u32[]{:S(2)}) collective-permute-start(f32[72,256]{1,0:T(8,128)S(1)} %get-tuple-element.56), channel_id=1, source_target_pairs={{0,6},{1,7},{2,4},{3,5},{4,2},{5,3},{6,0},{7,1},{8,14},{9,15},{10,... | collective-permute-start | bytes 221192 | tf_op jit(solution)/shard_map/ppermute | solution.py:573
  12.3 6.6 %collective-permute-start.6 = (f32[72,256]{1,0:T(8,128)S(1)}, f32[72,256]{1,0:T(8,128)S(1)}, u32[]{:S(2)}, u32[]{:S(2)}) collective-permute-start(f32[72,256]{1,0:T(8,128)S(1)} %get-tuple-element.57), channel_id=1, source_target_pairs={{0,4},{1,5},{2,6},{3,7},{4,0},{5,1},{6,2},{7,3},{8,12},{9,13},{10,... | collective-permute-start | bytes 221192 | tf_op jit(solution)/shard_map/ppermute | solution.py:573
  12.3 6.6 %collective-permute-start.7 = (f32[72,256]{1,0:T(8,128)S(1)}, f32[72,256]{1,0:T(8,128)S(1)}, u32[]{:S(2)}, u32[]{:S(2)}) collective-permute-start(f32[72,256]{1,0:T(8,128)S(1)} %get-tuple-element.58), channel_id=1, source_target_pairs={{0,2},{1,3},{2,0},{3,1},{4,6},{5,7},{6,4},{7,5},{8,10},{9,11},{10,... | collective-permute-start | bytes 221192 | tf_op jit(solution)/shard_map/ppermute | solution.py:573
  25.5 22.0 %all-to-all-start = ((f32[32,16,256]{2,1,0:T(8,128)}), f32[32,16,256]{2,1,0:T(8,128)S(1)}, u32[]{:S(2)}, u32[]{:S(2)}) async-start(f32[32,16,256]{2,1,0:T(8,128)} %bitcast.4), calls=%async_computation | async-start | bytes 1048576 | tf_op jit(solution)/shard_map/all_to_all | solution.py:677
  33.0 4.9 %collective-permute-start.8 = (f32[16,256]{1,0:T(8,128)S(1)}, f32[16,256]{1,0:T(8,128)S(1)}, u32[]{:S(2)}, u32[]{:S(2)}) collective-permute-start(f32[16,256]{1,0:T(8,128)S(1)} %get-tuple-element.65), channel_id=1, source_target_pairs={{0,1},{1,0},{2,3},{3,2},{4,5},{5,4},{6,7},{7,6},{8,9},{9,8},{10,11... | collective-permute-start | bytes 49160 | tf_op jit(solution)/shard_map/ppermute | solution.py:681
  33.5 7.6 %collective-permute-start.9 = (f32[16,256]{1,0:T(8,128)S(1)}, f32[16,256]{1,0:T(8,128)S(1)}, u32[]{:S(2)}, u32[]{:S(2)}) collective-permute-start(f32[16,256]{1,0:T(8,128)S(1)} %get-tuple-element.66), channel_id=1, source_target_pairs={{0,2},{1,3},{2,0},{3,1},{4,6},{5,7},{6,4},{7,5},{8,10},{9,11},{10,... | collective-permute-start | bytes 49160 | tf_op jit(solution)/shard_map/ppermute | solution.py:681
  34.8 8.7 %collective-permute-start.10 = (f32[16,256]{1,0:T(8,128)S(1)}, f32[16,256]{1,0:T(8,128)S(1)}, u32[]{:S(2)}, u32[]{:S(2)}) collective-permute-start(f32[16,256]{1,0:T(8,128)S(1)} %get-tuple-element.67), channel_id=1, source_target_pairs={{0,3},{1,2},{2,1},{3,0},{4,7},{5,6},{6,5},{7,4},{8,11},{9,10},{10,... | collective-permute-start | bytes 49160 | tf_op jit(solution)/shard_map/ppermute | solution.py:681
  35.2 10.8 %collective-permute-start.11 = (f32[16,256]{1,0:T(8,128)S(1)}, f32[16,256]{1,0:T(8,128)S(1)}, u32[]{:S(2)}, u32[]{:S(2)}) collective-permute-start(f32[16,256]{1,0:T(8,128)S(1)} %get-tuple-element.68), channel_id=1, source_target_pairs={{0,4},{1,5},{2,6},{3,7},{4,0},{5,1},{6,2},{7,3},{8,12},{9,13},{10,... | collective-permute-start | bytes 49160 | tf_op jit(solution)/shard_map/ppermute | solution.py:681
  37.5 9.9 %collective-permute-start.12 = (f32[16,256]{1,0:T(8,128)S(1)}, f32[16,256]{1,0:T(8,128)S(1)}, u32[]{:S(2)}, u32[]{:S(2)}) collective-permute-start(f32[16,256]{1,0:T(8,128)S(1)} %get-tuple-element.69), channel_id=1, source_target_pairs={{0,5},{1,4},{2,7},{3,6},{4,1},{5,0},{6,3},{7,2},{8,13},{9,12},{10,... | collective-permute-start | bytes 49160 | tf_op jit(solution)/shard_map/ppermute | solution.py:681
  37.9 9.6 %collective-permute-start.13 = (f32[16,256]{1,0:T(8,128)S(1)}, f32[16,256]{1,0:T(8,128)S(1)}, u32[]{:S(2)}, u32[]{:S(2)}) collective-permute-start(f32[16,256]{1,0:T(8,128)S(1)} %get-tuple-element.70), channel_id=1, source_target_pairs={{0,6},{1,7},{2,4},{3,5},{4,2},{5,3},{6,0},{7,1},{8,14},{9,15},{10,... | collective-permute-start | bytes 49160 | tf_op jit(solution)/shard_map/ppermute | solution.py:681
  41.1 6.4 %collective-permute-start.14 = (f32[16,256]{1,0:T(8,128)S(1)}, f32[16,256]{1,0:T(8,128)S(1)}, u32[]{:S(2)}, u32[]{:S(2)}) collective-permute-start(f32[16,256]{1,0:T(8,128)S(1)} %get-tuple-element.71), channel_id=1, source_target_pairs={{0,7},{1,6},{2,5},{3,4},{4,3},{5,2},{6,1},{7,0},{8,15},{9,14},{10,... | collective-permute-start | bytes 49160 | tf_op jit(solution)/shard_map/ppermute | solution.py:681

commit v8 on v7

--- a/solution.py
+++ b/solution.py
@@ -587,21 +587,25 @@
 
     other = to_core(velocity[0])
     active_other = to_core(active[:, 0])
-    mine = [velocity[0], delays, station_cells, active[:, 0]]
-    layer, delays, station_cells, active = call(
-        fetch_kernel,
-        "fetch",
-        [jax.ShapeDtypeStruct(a.shape, a.dtype) for a in mine],
-        mine,
-        [pltpu.SemaphoreType.DMA((len(mine),))],
-        hbm_in=range(len(mine)),
-    )
+    def fetch(name, *arrays):
+        return call(
+            fetch_kernel,
+            name,
+            [jax.ShapeDtypeStruct(a.shape, a.dtype) for a in arrays],
+            arrays,
+            [pltpu.SemaphoreType.DMA((len(arrays),))],
+            hbm_in=range(len(arrays)),
+        )
+
+    delays, station_cells, active = fetch("fetch", delays, station_cells, active[:, 0])
     (payload,) = call(
         head_kernel,
         "head",
         [out(1, events + LANES * (1 + 2 * ROUNDS))],
         [delays, station_cells, active, active_other],
     )
+    layer, payload = lax.optimization_barrier((velocity[0], payload))
+    (layer,) = fetch("fetch_layer", layer)
     pays = [payload] + [to_line(payload, j) for j in range(1, slots)]
 
     height = 2 * rows + -(-slots * ROUNDS // 8) * 8

time: 49.1 us -> 49.2 us (level)
  waiting for transfers between devices: 10.5 us -> 9.78 us
  Pallas kernels: 14 us -> 14.7 us
    ppermute x3, waiting for transfers between devices: 2.41 us -> 1.34 us  [to_line(): return lax.ppermute(array, 'src', [(i, i ^ j) for i in range(slots)])]
    pallas_call x7 -> x8, Pallas kernels: 14 us -> 14.7 us  [call(): pl.pallas_call(body, out_shape=list(outs), in_specs=[spec(pltpu.HBM if i...]
  transfers between devices with their start and end apart: 16 -> 16, of which waited for: 8 -> 7; matrix products, arithmetic and copies ran while one was open for 0% -> 0% of each run, Pallas kernels for 13% -> 15%
where the time goes in v8:
time: 49.2 us; the launch traced here: 48.6 us
  starting transfers between devices  23.2 us (47%)
  Pallas kernels  14.7 us (30%)
  waiting for transfers between devices  9.78 us (20%)
  between operations  0.89 us (2%)
    pallas_call x8, Pallas kernels, call(): pl.pallas_call(body, out_shape=list(outs), in_specs=[spec(pltpu.HBM if i...  14.7 us
    ppermute x7, starting transfers between devices, per_device(): lax.ppermute(kernel[m], 'space', [(i, i ^ m) for i in range(layers)])  10.5 us
    all_to_all x1, starting transfers between devices, per_device(): lax.all_to_all(times.reshape(slots * layers, own_rows, depth), ('src', 's...  4.67 us
    ppermute x7, waiting for transfers between devices, per_device(): lax.ppermute(kernel[m], 'space', [(i, i ^ m) for i in range(layers)])  3.91 us
    ppermute x3, starting transfers between devices, to_chip(): return lax.ppermute(array, 'space', [(i, i ^ 2 * j) for i in range(layers)])  3.75 us
    ppermute x3, starting transfers between devices, to_line(): return lax.ppermute(array, 'src', [(i, i ^ j) for i in range(slots)])  3.65 us
    ppermute x3, waiting for transfers between devices, to_chip(): return lax.ppermute(array, 'space', [(i, i ^ 2 * j) for i in range(layers)])  3.59 us
    ppermute x3, waiting for transfers between devices, to_line(): return lax.ppermute(array, 'src', [(i, i ^ j) for i in range(slots)])  1.34 us
  transfers between devices with their start and end apart: 16, of which 7 were waited for; matrix products, arithmetic and copies ran while one was open for 0% of the time, Pallas kernels for 15%

profile of v8, /device:TPU:1, one launch (start us, length us, event | category | flops | bytes accessed | tf_op | source)
XLA Modules:
  0.0 48.6 jit_solution(7531947523972461117)
XLA Ops:
  0.6 0.0 copy-start
  0.6 0.1 collective-permute-start.4
  0.8 0.5 collective-permute-start
  1.2 0.7 %fetch.1 = (f32[1,2048]{1,0:T(1,128)S(1)}, s32[1,3]{1,0:T(1,128)S(1)}, s32[2,1,16]{2,1,0:T(1,128)S(1)}) custom-call(f32[1,2048]{1,0:T(1,128)} %refs_0_.1, s32[1,3]{1,0:T(1,128)} %refs_1_.1, s32[2,1,16]{2,1,0:T(1,128)} %bitcast.12), custom_call_target="tpu_custom_call" | custom-call | bytes 3500000 | tf_op jit(solution)/shard_map/fetch/pallas_call | solution.py:32
  2.0 0.9 %collective-permute-done.active_other = s32[2,1,16]{2,1,0:T(1,128)S(1)} collective-permute-done((s32[2,1,16]{2,1,0:T(1,128)}, s32[2,1,16]{2,1,0:T(1,128)S(1)}, u32[]{:S(2)}, u32[]{:S(2)}) %collective-permute-start) | collective-permute-done | bytes 160 | tf_op jit(solution)/shard_map/ppermute | solution.py:576
  2.8 3.3 %collective-permute-start.3 = (f32[1,2688]{1,0:T(1,128)S(1)}, f32[1,2688]{1,0:T(1,128)S(1)}, u32[]{:S(2)}, u32[]{:S(2)}) collective-permute-start(f32[1,2688]{1,0:T(1,128)S(1)} %head.1.refs_0_), channel_id=1, source_target_pairs={{0,24},{8,16},{16,8},{24,0},{1,25},{9,17},{17,9},{25,1},{2,26},{10... | collective-permute-start | bytes 32264 | tf_op jit(solution)/shard_map/ppermute | solution.py:570
  6.1 0.2 collective-permute-start.2
  6.4 0.1 collective-permute-start.1
  6.5 1.0 %fetch_layer.1.own = f32[512,256]{1,0:T(8,128)S(1)} custom-call(f32[512,256]{1,0:T(8,128)} %bitcast.10), custom_call_target="tpu_custom_call" | custom-call | bytes 3500000 | tf_op jit(solution)/shard_map/fetch_layer/pallas_call | solution.py:32
  7.5 0.0 collective-permute-done.3.refs_3_
  7.5 1.1 %collective-permute-done.2.refs_2_ = f32[1,2688]{1,0:T(1,128)S(1)} collective-permute-done((f32[1,2688]{1,0:T(1,128)S(1)}, f32[1,2688]{1,0:T(1,128)S(1)}, u32[]{:S(2)}, u32[]{:S(2)}) %collective-permute-start.2) | collective-permute-done | bytes 10784 | tf_op jit(solution)/shard_map/ppermute | solution.py:570
  8.7 0.2 collective-permute-done.1.refs_1_
  8.9 0.0 collective-permute-done.4.other
  8.9 0.1 pack.1
  9.0 3.4 %collective-permute-start.5 = (f32[72,256]{1,0:T(8,128)S(1)}, f32[72,256]{1,0:T(8,128)S(1)}, u32[]{:S(2)}, u32[]{:S(2)}) collective-permute-start(f32[72,256]{1,0:T(8,128)S(1)} %get-tuple-element.58), channel_id=1, source_target_pairs={{0,6},{1,7},{2,4},{3,5},{4,2},{5,3},{6,0},{7,1},{8,14},{9,15},{10,... | collective-permute-start | bytes 221192 | tf_op jit(solution)/shard_map/ppermute | solution.py:573
  12.3 0.0 collective-permute-start.6
  12.3 0.4 collective-permute-start.7
  12.7 0.0 copy-done
  12.7 2.6 %events.1 = (f32[208,256]{1,0:T(8,128)S(1)}, f32[4,208,256]{2,1,0:T(8,128)S(1)}, f32[4,34,8,256]{3,2,1,0:T(8,128)S(1)}) custom-call(s32[3,2048]{1,0:T(4,128)S(1)} %copy-done, f32[1,2688]{1,0:T(1,128)S(1)} %head.1.refs_0_, f32[1,2688]{1,0:T(1,128)S(1)} %collective-permute-done.1.refs_1_, f32[1,2688]{1,0:T(1,128)S(1)} %collective-permute-done.2.refs_2_, ...), custom_call_target="tpu_custom_call" | custom-call | bytes 10500000 | tf_op jit(solution)/shard_map/events/pallas_call | solution.py:32
  15.3 0.0 collective-permute-done.5.refs_5_
  15.4 3.6 %collective-permute-done.6.refs_6_ = f32[72,256]{1,0:T(8,128)S(1)} collective-permute-done((f32[72,256]{1,0:T(8,128)S(1)}, f32[72,256]{1,0:T(8,128)S(1)}, u32[]{:S(2)}, u32[]{:S(2)}) %collective-permute-start.6) | collective-permute-done | bytes 73760 | tf_op jit(solution)/shard_map/ppermute | solution.py:573
  18.9 0.0 collective-permute-done.7.refs_7_
  18.9 6.6 %sweeps.1 = (f32[4,8,16,256]{3,2,1,0:T(8,128)}, f32[4,26,8,256]{3,2,1,0:T(8,128)S(1)}, f32[32,8,256]{2,1,0:T(8,128)S(1)}) custom-call(f32[1,2688]{1,0:T(1,128)S(1)} %head.1.refs_0_, f32[1,2688]{1,0:T(1,128)S(1)} %collective-permute-done.1.refs_1_, f32[1,2688]{1,0:T(1,128)S(1)} %collective-permute-done.2.refs_2_, ...), custom_call_target="tpu_custom_call" | custom-call | bytes 35000000 | tf_op jit(solution)/shard_map/sweeps/pallas_call | solution.py:32
  25.5 4.7 %all-to-all-start = ((f32[32,16,256]{2,1,0:T(8,128)}), f32[32,16,256]{2,1,0:T(8,128)S(1)}, u32[]{:S(2)}, u32[]{:S(2)}) async-start(f32[32,16,256]{2,1,0:T(8,128)} %bitcast.4), calls=%async_computation | async-start | bytes 1048576 | tf_op jit(solution)/shard_map/all_to_all | solution.py:681
  30.2 2.8 %adjoint.1 = (f32[16,256]{1,0:T(8,128)S(1)}, f32[16,256]{1,0:T(8,128)S(1)}, f32[16,256]{1,0:T(8,128)S(1)}, f32[16,256]{1,0:T(8,128)S(1)}, f32[16,256]{1,0:T(8,12...) custom-call(f32[1,2688]{1,0:T(1,128)S(1)} %head.1.refs_0_, ...), custom_call_target="tpu_custom_call" | custom-call | bytes 24500000 | tf_op jit(solution)/shard_map/adjoint/pallas_call | solution.py:32
  33.0 0.5 %collective-permute-start.8 = (f32[16,256]{1,0:T(8,128)S(1)}, f32[16,256]{1,0:T(8,128)S(1)}, u32[]{:S(2)}, u32[]{:S(2)}) collective-permute-start(f32[16,256]{1,0:T(8,128)S(1)} %get-tuple-element.67), channel_id=1, source_target_pairs={{0,1},{1,0},{2,3},{3,2},{4,5},{5,4},{6,7},{7,6},{8,9},{9,8},{10,11... | collective-permute-start | bytes 49160 | tf_op jit(solution)/shard_map/ppermute | solution.py:685
  33.5 1.3 %collective-permute-start.9 = (f32[16,256]{1,0:T(8,128)S(1)}, f32[16,256]{1,0:T(8,128)S(1)}, u32[]{:S(2)}, u32[]{:S(2)}) collective-permute-start(f32[16,256]{1,0:T(8,128)S(1)} %get-tuple-element.68), channel_id=1, source_target_pairs={{0,2},{1,3},{2,0},{3,1},{4,6},{5,7},{6,4},{7,5},{8,10},{9,11},{10,... | collective-permute-start | bytes 49160 | tf_op jit(solution)/shard_map/ppermute | solution.py:685
  34.8 0.4 collective-permute-start.10
  35.2 2.3 %collective-permute-start.11 = (f32[16,256]{1,0:T(8,128)S(1)}, f32[16,256]{1,0:T(8,128)S(1)}, u32[]{:S(2)}, u32[]{:S(2)}) collective-permute-start(f32[16,256]{1,0:T(8,128)S(1)} %get-tuple-element.70), channel_id=1, source_target_pairs={{0,4},{1,5},{2,6},{3,7},{4,0},{5,1},{6,2},{7,3},{8,12},{9,13},{10,... | collective-permute-start | bytes 49160 | tf_op jit(solution)/shard_map/ppermute | solution.py:685
  37.5 0.4 collective-permute-start.12
  37.9 0.0 collective-permute-done.8.refs_1_
  37.9 3.2 %collective-permute-start.13 = (f32[16,256]{1,0:T(8,128)S(1)}, f32[16,256]{1,0:T(8,128)S(1)}, u32[]{:S(2)}, u32[]{:S(2)}) collective-permute-start(f32[16,256]{1,0:T(8,128)S(1)} %get-tuple-element.72), channel_id=1, source_target_pairs={{0,6},{1,7},{2,4},{3,5},{4,2},{5,3},{6,0},{7,1},{8,14},{9,15},{10,... | collective-permute-start | bytes 49160 | tf_op jit(solution)/shard_map/ppermute | solution.py:685
  41.1 0.0 collective-permute-done.9.refs_2_
  41.1 2.5 %collective-permute-start.14 = (f32[16,256]{1,0:T(8,128)S(1)}, f32[16,256]{1,0:T(8,128)S(1)}, u32[]{:S(2)}, u32[]{:S(2)}) collective-permute-start(f32[16,256]{1,0:T(8,128)S(1)} %get-tuple-element.73), channel_id=1, source_target_pairs={{0,7},{1,6},{2,5},{3,4},{4,3},{5,2},{6,1},{7,0},{8,15},{9,14},{10,... | collective-permute-start | bytes 49160 | tf_op jit(solution)/shard_map/ppermute | solution.py:685
  43.6 0.0 collective-permute-done.10.refs_3_
  43.6 2.4 %collective-permute-done.11.refs_4_ = f32[16,256]{1,0:T(8,128)S(1)} collective-permute-done((f32[16,256]{1,0:T(8,128)S(1)}, f32[16,256]{1,0:T(8,128)S(1)}, u32[]{:S(2)}, u32[]{:S(2)}) %collective-permute-start.11) | collective-permute-done | bytes 16416 | tf_op jit(solution)/shard_map/ppermute | solution.py:685
  46.0 1.5 %collective-permute-done.12.refs_5_ = f32[16,256]{1,0:T(8,128)S(1)} collective-permute-done((f32[16,256]{1,0:T(8,128)S(1)}, f32[16,256]{1,0:T(8,128)S(1)}, u32[]{:S(2)}, u32[]{:S(2)}) %collective-permute-start.12) | collective-permute-done | bytes 16416 | tf_op jit(solution)/shard_map/ppermute | solution.py:685
  47.5 0.0 collective-permute-done.13.refs_6_
  47.5 0.0 collective-permute-done.14.refs_7_
  47.5 0.1 all-to-all-done
  47.5 0.9 %join.1 = (f32[512,256]{1,0:T(8,128)}, f32[128,256]{1,0:T(8,128)}) custom-call(f32[512,256]{1,0:T(8,128)S(1)} %bitcast.8, f32[16,256]{1,0:T(8,128)S(1)} %get-tuple-element.66.refs_0_, f32[16,256]{1,0:T(8,128)S(1)} %collective-permute-done.8.refs_1_, f32[16,256]{1,0:T(8,128)S(1)} %collective-permute-done.9.refs_2_, ...), custom_call_target="tpu_custom_call" | custom-call | bytes 3500000 | tf_op jit(solution)/shard_map/join/pallas_call | solution.py:32
  (1 shorter events, 0.0 us)
Async XLA Ops:
  0.6 12.1 %copy-start = (s32[3,2048]{1,0:T(4,128)S(1)}, s32[3,2048]{1,0:T(4,128)}, u32[]{:S(2)}) copy-start(s32[3,2048]{1,0:T(4,128)} %cells) | copy-start | bytes 73732
  0.6 8.3 %collective-permute-start.4 = (f32[512,256]{1,0:T(8,128)}, f32[512,256]{1,0:T(8,128)S(1)}, u32[]{:S(2)}, u32[]{:S(2)}) collective-permute-start(f32[512,256]{1,0:T(8,128)} %bitcast.9), channel_id=1, source_target_pairs={{0,1},{1,0},{2,3},{3,2},{4,5},{5,4},{6,7},{7,6},{8,9},{9,8},{10,11... | collective-permute-start | bytes 1572872 | tf_op jit(solution)/shard_map/ppermute | solution.py:576
  0.8 2.1 %collective-permute-start = (s32[2,1,16]{2,1,0:T(1,128)}, s32[2,1,16]{2,1,0:T(1,128)S(1)}, u32[]{:S(2)}, u32[]{:S(2)}) collective-permute-start(s32[2,1,16]{2,1,0:T(1,128)} %bitcast.11), channel_id=1, source_target_pairs={{0,1},{1,0},{2,3},{3,2},{4,5},{5,4},{6,7},{7,6},{8,9},{9,8},{10,11... | collective-permute-start | bytes 392 | tf_op jit(solution)/shard_map/ppermute | solution.py:576
  2.8 4.7 %collective-permute-start.3 = (f32[1,2688]{1,0:T(1,128)S(1)}, f32[1,2688]{1,0:T(1,128)S(1)}, u32[]{:S(2)}, u32[]{:S(2)}) collective-permute-start(f32[1,2688]{1,0:T(1,128)S(1)} %head.1.refs_0_), channel_id=1, source_target_pairs={{0,24},{8,16},{16,8},{24,0},{1,25},{9,17},{17,9},{25,1},{2,26},{10... | collective-permute-start | bytes 32264 | tf_op jit(solution)/shard_map/ppermute | solution.py:570
  6.1 2.5 %collective-permute-start.2 = (f32[1,2688]{1,0:T(1,128)S(1)}, f32[1,2688]{1,0:T(1,128)S(1)}, u32[]{:S(2)}, u32[]{:S(2)}) collective-permute-start(f32[1,2688]{1,0:T(1,128)S(1)} %head.1.refs_0_), channel_id=1, source_target_pairs={{0,16},{8,24},{16,0},{24,8},{1,17},{9,25},{17,1},{25,9},{2,18},{10... | collective-permute-start | bytes 32264 | tf_op jit(solution)/shard_map/ppermute | solution.py:570
  6.4 2.5 %collective-permute-start.1 = (f32[1,2688]{1,0:T(1,128)S(1)}, f32[1,2688]{1,0:T(1,128)S(1)}, u32[]{:S(2)}, u32[]{:S(2)}) collective-permute-start(f32[1,2688]{1,0:T(1,128)S(1)} %head.1.refs_0_), channel_id=1, source_target_pairs={{0,8},{8,0},{16,24},{24,16},{1,9},{9,1},{17,25},{25,17},{2,10},{10... | collective-permute-start | bytes 32264 | tf_op jit(solution)/shard_map/ppermute | solution.py:570
  9.0 6.4 %collective-permute-start.5 = (f32[72,256]{1,0:T(8,128)S(1)}, f32[72,256]{1,0:T(8,128)S(1)}, u32[]{:S(2)}, u32[]{:S(2)}) collective-permute-start(f32[72,256]{1,0:T(8,128)S(1)} %get-tuple-element.58), channel_id=1, source_target_pairs={{0,6},{1,7},{2,4},{3,5},{4,2},{5,3},{6,0},{7,1},{8,14},{9,15},{10,... | collective-permute-start | bytes 221192 | tf_op jit(solution)/shard_map/ppermute | solution.py:573
  12.3 6.6 %collective-permute-start.6 = (f32[72,256]{1,0:T(8,128)S(1)}, f32[72,256]{1,0:T(8,128)S(1)}, u32[]{:S(2)}, u32[]{:S(2)}) collective-permute-start(f32[72,256]{1,0:T(8,128)S(1)} %get-tuple-element.59), channel_id=1, source_target_pairs={{0,4},{1,5},{2,6},{3,7},{4,0},{5,1},{6,2},{7,3},{8,12},{9,13},{10,... | collective-permute-start | bytes 221192 | tf_op jit(solution)/shard_map/ppermute | solution.py:573
  12.3 6.6 %collective-permute-start.7 = (f32[72,256]{1,0:T(8,128)S(1)}, f32[72,256]{1,0:T(8,128)S(1)}, u32[]{:S(2)}, u32[]{:S(2)}) collective-permute-start(f32[72,256]{1,0:T(8,128)S(1)} %get-tuple-element.60), channel_id=1, source_target_pairs={{0,2},{1,3},{2,0},{3,1},{4,6},{5,7},{6,4},{7,5},{8,10},{9,11},{10,... | collective-permute-start | bytes 221192 | tf_op jit(solution)/shard_map/ppermute | solution.py:573
  25.5 22.0 %all-to-all-start = ((f32[32,16,256]{2,1,0:T(8,128)}), f32[32,16,256]{2,1,0:T(8,128)S(1)}, u32[]{:S(2)}, u32[]{:S(2)}) async-start(f32[32,16,256]{2,1,0:T(8,128)} %bitcast.4), calls=%async_computation | async-start | bytes 1048576 | tf_op jit(solution)/shard_map/all_to_all | solution.py:681
  33.0 4.9 %collective-permute-start.8 = (f32[16,256]{1,0:T(8,128)S(1)}, f32[16,256]{1,0:T(8,128)S(1)}, u32[]{:S(2)}, u32[]{:S(2)}) collective-permute-start(f32[16,256]{1,0:T(8,128)S(1)} %get-tuple-element.67), channel_id=1, source_target_pairs={{0,1},{1,0},{2,3},{3,2},{4,5},{5,4},{6,7},{7,6},{8,9},{9,8},{10,11... | collective-permute-start | bytes 49160 | tf_op jit(solution)/shard_map/ppermute | solution.py:685
  33.5 7.6 %collective-permute-start.9 = (f32[16,256]{1,0:T(8,128)S(1)}, f32[16,256]{1,0:T(8,128)S(1)}, u32[]{:S(2)}, u32[]{:S(2)}) collective-permute-start(f32[16,256]{1,0:T(8,128)S(1)} %get-tuple-element.68), channel_id=1, source_target_pairs={{0,2},{1,3},{2,0},{3,1},{4,6},{5,7},{6,4},{7,5},{8,10},{9,11},{10,... | collective-permute-start | bytes 49160 | tf_op jit(solution)/shard_map/ppermute | solution.py:685
  34.8 8.7 %collective-permute-start.10 = (f32[16,256]{1,0:T(8,128)S(1)}, f32[16,256]{1,0:T(8,128)S(1)}, u32[]{:S(2)}, u32[]{:S(2)}) collective-permute-start(f32[16,256]{1,0:T(8,128)S(1)} %get-tuple-element.69), channel_id=1, source_target_pairs={{0,3},{1,2},{2,1},{3,0},{4,7},{5,6},{6,5},{7,4},{8,11},{9,10},{10,... | collective-permute-start | bytes 49160 | tf_op jit(solution)/shard_map/ppermute | solution.py:685
  35.2 10.8 %collective-permute-start.11 = (f32[16,256]{1,0:T(8,128)S(1)}, f32[16,256]{1,0:T(8,128)S(1)}, u32[]{:S(2)}, u32[]{:S(2)}) collective-permute-start(f32[16,256]{1,0:T(8,128)S(1)} %get-tuple-element.70), channel_id=1, source_target_pairs={{0,4},{1,5},{2,6},{3,7},{4,0},{5,1},{6,2},{7,3},{8,12},{9,13},{10,... | collective-permute-start | bytes 49160 | tf_op jit(solution)/shard_map/ppermute | solution.py:685
  37.5 9.9 %collective-permute-start.12 = (f32[16,256]{1,0:T(8,128)S(1)}, f32[16,256]{1,0:T(8,128)S(1)}, u32[]{:S(2)}, u32[]{:S(2)}) collective-permute-start(f32[16,256]{1,0:T(8,128)S(1)} %get-tuple-element.71), channel_id=1, source_target_pairs={{0,5},{1,4},{2,7},{3,6},{4,1},{5,0},{6,3},{7,2},{8,13},{9,12},{10,... | collective-permute-start | bytes 49160 | tf_op jit(solution)/shard_map/ppermute | solution.py:685
  37.9 9.6 %collective-permute-start.13 = (f32[16,256]{1,0:T(8,128)S(1)}, f32[16,256]{1,0:T(8,128)S(1)}, u32[]{:S(2)}, u32[]{:S(2)}) collective-permute-start(f32[16,256]{1,0:T(8,128)S(1)} %get-tuple-element.72), channel_id=1, source_target_pairs={{0,6},{1,7},{2,4},{3,5},{4,2},{5,3},{6,0},{7,1},{8,14},{9,15},{10,... | collective-permute-start | bytes 49160 | tf_op jit(solution)/shard_map/ppermute | solution.py:685
  41.1 6.4 %collective-permute-start.14 = (f32[16,256]{1,0:T(8,128)S(1)}, f32[16,256]{1,0:T(8,128)S(1)}, u32[]{:S(2)}, u32[]{:S(2)}) collective-permute-start(f32[16,256]{1,0:T(8,128)S(1)} %get-tuple-element.73), channel_id=1, source_target_pairs={{0,7},{1,6},{2,5},{3,4},{4,3},{5,2},{6,1},{7,0},{8,15},{9,14},{10,... | collective-permute-start | bytes 49160 | tf_op jit(solution)/shard_map/ppermute | solution.py:685
